TPU v7x, 512 devices: a whole 4x4x16 slice. The times are simulated.
512 devices in a mesh: gx: 32 (over x, y, core), gz: 16 (over z).
Axes of the slice: x: 4, y: 4, z: 16, core: 2. Of those that a mesh axis runs over, the one named last changes fastest.
Arguments:
- element_rhs_load: float32 [32, 8, 32, 8, 128], P('gx', None, 'gz'), may hold values from -6 to 6
- metric: float32 [3, 32, 32, 16], P(None, 'gx', 'gz'), may hold values from 0.5 to 2
- coarse_factor: float32 [32, 16, 10, 32, 16], P('gx', 'gz'), may hold values from -1 to 1
Outputs:
- solution_field: float32 [32, 8, 32, 8, 128], P('gx', None, 'gz')
- residual: float32 [32, 8, 32, 8, 128], P('gx', None, 'gz')
All inputs are finite; a program needn't handle non-finite values.
Results may differ from a plain program's by a relative error of at most 0.00019.
Values sent between devices are 32-bit elements; how exact they have to be, the bound alone decides.
No kernel may reach another device: no remote copies, remote signals or barrier semaphores. Data moves between devices by JAX's collectives and lax.ppermute only.
A program may use at most 64 MiB of HBM per device.

v0:
```python
import jax
import jax.numpy as jnp
import numpy as np
from jax import lax
from jax.sharding import PartitionSpec as P

CHEB = 4


cheb_high = 2.0
cheb_low = 0.1
gll_inner = (
    -0.8717401485096066,
    -0.5917001814331423,
    -0.2092992179024789,
    0.2092992179024789,
    0.5917001814331423,
    0.8717401485096066,
)


def extended(block, sides, width):
    for axis, dim in sides:
        count = lax.axis_size(axis)
        forward = [(i, i + 1) for i in range(count - 1)]
        forward.append((count - 1, 0))
        backward = [(target, source) for source, target in forward]
        low = lax.ppermute(
            lax.slice_in_dim(block, block.shape[dim] - width, None, axis=dim), axis, forward
        )
        high = lax.ppermute(lax.slice_in_dim(block, 0, width, axis=dim), axis, backward)
        block = jnp.concatenate([low, block, high], axis=dim)
    return block


def partner_2(value, axis, stride):
    mask = 2**stride
    pairs = [(source, source ^ mask) for source in range(lax.axis_size(axis))]
    return lax.ppermute(value, axis, pairs)


def legendre_seven(points):
    before = np.ones(points.shape[0])
    current = points.copy()
    for degree in range(1, 7):
        following = ((2.0 * degree + 1.0) * points * current - degree * before) / (degree + 1.0)
        before = current
        current = following
    return current


def gll_tables():
    order = 7
    points = np.concatenate([[-1.0], np.array(gll_inner), [1.0]])
    values = legendre_seven(points)
    weights = 2.0 / (order * (order + 1) * values**2)
    count = order + 1
    deriv = np.zeros((count, count))
    for row_index in range(count):
        for col_index in range(count):
            if row_index != col_index:
                deriv[row_index, col_index] = values[row_index] / (
                    values[col_index] * (points[row_index] - points[col_index])
                )
    deriv[0, 0] = -order * (order + 1) / 4.0
    deriv[-1, -1] = order * (order + 1) / 4.0
    stiff = deriv.T @ (weights[:, None] * deriv)
    return (points, weights, stiff)


def bump_tables(count_x, count_z, count_across):
    points, weights, stiff = gll_tables()

    def positions(count):
        return ((np.arange(count)[:, None] + (1.0 + points[None, :]) / 2.0) / count).reshape(-1)

    along_x = np.stack([np.sin(np.pi * mode * positions(count_x)) for mode in (1, 2)])
    along_z = np.stack([np.sin(np.pi * mode * positions(count_z)) for mode in (1, 2)])
    along_y = np.stack([np.sin(np.pi * mode * positions(count_across)) for mode in range(1, 9)])
    return (
        jnp.asarray(along_x, jnp.float32),
        jnp.asarray(along_z, jnp.float32),
        jnp.asarray(along_y, jnp.float32),
    )


def wall_mask(count_across):
    table = np.ones(count_across * 8)
    table[0] = 0.0
    table[-1] = 0.0
    return jnp.asarray(table, jnp.float32)


def node_weights(count_across):
    edge = np.ones(8)
    edge[0] = 0.5
    edge[7] = 0.5
    across = np.ones(count_across * 8)
    for element in range(count_across):
        if element > 0:
            across[8 * element] = 0.5
        if element < count_across - 1:
            across[8 * element + 7] = 0.5
    table = edge[:, None, None] * edge[None, :, None] * across[None, None, :]
    return jnp.asarray(table, jnp.float32).reshape(1, 8, 1, 8, count_across * 8)


def element_apply(field, metric):
    points, weights, stiff = gll_tables()
    stiffness = jnp.asarray(stiff, jnp.float32)
    weight = jnp.asarray(weights, jnp.float32)
    count_x, count_z, count_across = (metric.shape[1], metric.shape[2], metric.shape[3])
    cube = field.reshape(count_x, 8, count_z, 8, count_across, 8)
    highest = lax.Precision.HIGHEST
    weight_i = weight[None, :, None, None, None, None]
    weight_j = weight[None, None, None, :, None, None]
    weight_l = weight[None, None, None, None, None, :]
    term_x = jnp.einsum("aibjcl,ip->apbjcl", cube, stiffness, precision=highest) * (
        weight_j * weight_l
    )
    term_z = jnp.einsum("aibjcl,jp->aibpcl", cube, stiffness, precision=highest) * (
        weight_i * weight_l
    )
    term_y = jnp.einsum("aibjcl,lp->aibjcp", cube, stiffness, precision=highest) * (
        weight_i * weight_j
    )
    factor_x = metric[0][:, None, :, None, :, None]
    factor_z = metric[1][:, None, :, None, :, None]
    factor_y = metric[2][:, None, :, None, :, None]
    result = factor_x * term_x + factor_z * term_z + factor_y * term_y
    return result.reshape(count_x, 8, count_z, 8, count_across * 8)


def element_diagonal(metric):
    points, weights, stiff = gll_tables()
    weight = jnp.asarray(weights, jnp.float32)
    kdiag = jnp.asarray(stiff[np.arange(8), np.arange(8)], jnp.float32)
    count_x, count_z, count_across = (metric.shape[1], metric.shape[2], metric.shape[3])
    weight_i = weight[None, :, None, None, None, None]
    weight_j = weight[None, None, None, :, None, None]
    weight_l = weight[None, None, None, None, None, :]
    stiff_i = kdiag[None, :, None, None, None, None]
    stiff_j = kdiag[None, None, None, :, None, None]
    stiff_l = kdiag[None, None, None, None, None, :]
    factor_x = metric[0][:, None, :, None, :, None]
    factor_z = metric[1][:, None, :, None, :, None]
    factor_y = metric[2][:, None, :, None, :, None]
    result = (
        factor_x * (stiff_i * weight_j * weight_l)
        + factor_z * (weight_i * stiff_j * weight_l)
        + factor_y * (weight_i * weight_j * stiff_l)
    )
    return result.reshape(count_x, 8, count_z, 8, count_across * 8)


def sum_y(field):
    shape = field.shape
    cube = field.reshape(shape[:-1] + (shape[-1] // 8, 8))
    lower = cube[..., 0]
    upper = cube[..., 7]
    joined = upper[..., :-1] + lower[..., 1:]
    cube = cube.at[..., 1:, 0].set(joined).at[..., :-1, 7].set(joined)
    return cube.reshape(shape)


def chebyshev(rhs, inv_diag, operator):
    theta = 0.5 * (cheb_high + cheb_low)
    delta = 0.5 * (cheb_high - cheb_low)
    sigma = theta / delta
    rho = 1.0 / sigma
    update = inv_diag * rhs / theta
    smooth = update
    for sweep in range(CHEB - 1):
        remainder = rhs - operator(smooth)
        rho_next = 1.0 / (2.0 * sigma - rho)
        update = rho_next * rho * update + 2.0 * rho_next / delta * inv_diag * remainder
        smooth = smooth + update
        rho = rho_next
    return smooth


def faces_x(field):
    lower = field[:, 0]
    upper = field[:, 7]
    rim = jnp.stack([lower[0], upper[-1]], axis=0)
    padded = extended(rim, (("gx", 0),), 1)
    before = jnp.concatenate([padded[0:1], upper[:-1]], axis=0)
    after = jnp.concatenate([lower[1:], padded[3:4]], axis=0)
    return field.at[:, 0].set(lower + before).at[:, 7].set(upper + after)


def faces_z(field):
    lower = field[:, :, :, 0]
    upper = field[:, :, :, 7]
    rim = jnp.stack([lower[:, :, 0], upper[:, :, -1]], axis=2)
    padded = extended(rim, (("gz", 2),), 1)
    before = jnp.concatenate([padded[:, :, 0:1], upper[:, :, :-1]], axis=2)
    after = jnp.concatenate([lower[:, :, 1:], padded[:, :, 3:4]], axis=2)
    return field.at[:, :, :, 0].set(lower + before).at[:, :, :, 7].set(upper + after)


def per_device(element_rhs_load, metric, coarse_factor):
    highest = lax.Precision.HIGHEST
    count_x, count_z, count_across = (metric.shape[1], metric.shape[2], metric.shape[3])
    boundary_mask = wall_mask(count_across)
    mult = node_weights(count_across)

    def assemble(field):
        return sum_y(faces_z(faces_x(field)))

    def operator(field):
        return assemble(element_apply(field, metric)) * boundary_mask

    rhs = assemble(element_rhs_load) * boundary_mask
    inv_diag = boundary_mask / assemble(element_diagonal(metric))
    smooth = chebyshev(rhs, inv_diag, operator)
    along_x, along_z, along_y = bump_tables(count_x, count_z, count_across)
    weighted = (rhs * mult).reshape(count_x * 8, count_z * 8, count_across * 8)
    partial_y = jnp.einsum("xzy,ky->xzk", weighted, along_y, precision=highest)
    partial_x = jnp.einsum("xzk,ax->azk", partial_y, along_x, precision=highest)
    coarse_rhs = jnp.einsum("azk,bz->abk", partial_x, along_z, precision=highest).reshape(-1)
    factor = coarse_factor.reshape(
        coarse_factor.shape[2], coarse_factor.shape[3], coarse_factor.shape[4]
    )
    devices = lax.axis_size(("gx", "gz"))
    levels = devices.bit_length() - 1
    own = jnp.einsum("lck,c->lk", factor, coarse_rhs, precision=highest)
    column_sum = own
    for bit in range(levels):
        partner = partner_2(column_sum[bit + 1 :], ("gx", "gz"), bit)
        column_sum = jnp.concatenate(
            [column_sum[: bit + 1], column_sum[bit + 1 :] + partner], axis=0
        )
    coarse_sol = jnp.einsum("lck,lk->c", factor, column_sum, precision=highest).reshape(2, 2, 8)
    spread_y = jnp.einsum("abk,ky->aby", coarse_sol, along_y, precision=highest)
    spread_z = jnp.einsum("aby,bz->azy", spread_y, along_z, precision=highest)
    streamwise_spread = jnp.einsum("azy,ax->xzy", spread_z, along_x, precision=highest)
    coarse_solution = (
        streamwise_spread.reshape(count_x, 8, count_z, 8, count_across * 8) * boundary_mask
    )
    precond = smooth + coarse_solution
    local_rz = jnp.sum(mult * rhs * precond)
    rz = lax.psum(local_rz, ("gx", "gz"))
    image = operator(precond)
    curvature = lax.psum(jnp.sum(mult * precond * image), ("gx", "gz"))
    alpha = rz / curvature
    solution_field = alpha * precond
    residual = rhs - alpha * image
    return (solution_field, residual)


def solution(mesh):
    placed = (
        P("gx", None, "gz", None, None),
        P(None, "gx", "gz", None),
        P("gx", "gz", None, None, None),
    )
    return jax.shard_map(
        per_device,
        mesh=mesh,
        in_specs=placed,
        out_specs=(P("gx", None, "gz", None, None), P("gx", None, "gz", None, None)),
        check_vma=False,
    )
```

profile of v0, /device:TPU:1, one launch (start us, length us, event | category | flops | bytes accessed | tf_op | source)
XLA Modules:
  0.0 606.6 jit_solution(7205843960231055302)
XLA Ops:
  3.7 8.8 %collective-permute-start.5 = (f32[1,2,8,128]{3,1,2,0:T(2,128)S(1)}, f32[1,2,8,128]{3,1,2,0:T(2,128)S(1)}, u32[]{:S(2)}, u32[]{:S(2)}) collective-permute-start(f32[1,2,8,128]{3,1,2,0:T(2,128)S(1)} %get-tuple-element.472), channel_id=1, source_target_pairs={{16,0},{32,16},{48,32},{64,48},{80,64},{96,80},{112,96},{128,112},... | collective-permute-start | bytes 24584 | tf_op jit(solution)/shard_map/ppermute | solution.py:31
  22.0 8.6 %collective-permute-start.7 = (f32[1,8,1,128]{3,1,2,0:T(8,128)S(1)}, f32[1,8,1,128]{3,1,2,0:T(8,128)S(1)}, u32[]{:S(2)}, u32[]{:S(2)}) collective-permute-start(f32[1,8,1,128]{3,1,2,0:T(8,128)S(1)} %get-tuple-element.496), channel_id=1, source_target_pairs={{1,0},{2,1},{3,2},{4,3},{5,4},{6,5},{7,6},{8,7},{9,8},{10,9},{11,1... | collective-permute-start | bytes 12296 | tf_op jit(solution)/shard_map/ppermute | solution.py:31
  38.2 3.6 collective-permute-start.3
  42.8 4.4 scatter.136
  50.7 6.1 scatter.126
  56.8 5.1 dynamic-slice_select_fusion.4
  61.9 24.4 %scatter.139 = f32[1,8,2,8,16,8]{5,4,3,2,1,0:T(8,128)S(1)} dynamic-update-slice(f32[1,8,2,8,16,8]{5,4,3,2,1,0:T(8,128)S(1)} %scatter.136, f32[1,8,2,8,15,1]{5,4,3,2,1,0:T(8,128)} %get-tuple-element.515, s32[]{:T(128)} %constant.794.clone.1, s32[]{:T(128)} %constant.794.clone.1, s32[]{:T(128)} %constant.794.clone.1, s32[]{:T(128)} %constant.794.clone.1, s32[]{:T(128)} %bitcast.12, s32[]{:T(128)} %bitcast.13) | dynamic-update-slice | bytes 15364 | tf_op jit(solution)/shard_map/scatter | solution.py:162
  86.3 23.5 %scatter.129 = f32[1,8,2,8,16,8]{5,4,3,2,1,0:T(8,128)S(1)} dynamic-update-slice(f32[1,8,2,8,16,8]{5,4,3,2,1,0:T(8,128)S(1)} %scatter.126, f32[1,8,2,8,15,1]{5,4,3,2,1,0:T(8,128)S(1)} %copy-done.3, s32[]{:T(128)} %constant.794.clone.1, s32[]{:T(128)} %constant.794.clone.1, s32[]{:T(128)} %constant.794.clone.1, s32[]{:T(128)} %constant.794.clone.1, s32[]{:T(128)} %bitcast.12, s32[]{:T(128)} %bitcast.13) | dynamic-update-slice | bytes 15364 | tf_op jit(solution)/shard_map/scatter | solution.py:162
  115.4 8.2 %fusion.73 = f32[8,2,8,16,8]{3,4,2,1,0:T(8,128)} fusion(f32[8,2,8,16,8]{4,3,2,1,0:T(8,128)S(1)} %multiply_bitcast_fusion, f32[8,8,1,1,1]{0,1,4,3,2:T(8,128)S(1)} %copy-done.10), kind=kOutput, calls=%fused_computation.213 | convolution fusion | flops 1572864 | bytes 131328 | tf_op jit(solution)/shard_map/aibjcl,lp->aibjcp/dot_general | solution.py:124
  126.7 2.4 fusion.72
  130.3 4.8 collective-permute-start.22
  135.1 3.3 fusion.9
  140.3 7.8 %collective-permute-start.23 = (f32[6,16]{1,0:T(8,128)S(1)}, f32[6,16]{1,0:T(8,128)S(1)}, u32[]{:S(2)}, u32[]{:S(2)}) collective-permute-start(f32[6,16]{1,0:T(8,128)S(1)} %slice.1562), channel_id=1, source_target_pairs={{0,8},{1,9},{2,10},{3,11},{4,12},{5,13},{6,14},{7,15},{8,0},{9,1},... | collective-permute-start | bytes 1160 | tf_op jit(solution)/shard_map/ppermute | solution.py:39
  148.1 5.3 collective-permute-done.23
  153.4 10.1 %collective-permute-start.24 = (f32[5,16]{1,0:T(8,128)S(1)}, f32[5,16]{1,0:T(8,128)S(1)}, u32[]{:S(2)}, u32[]{:S(2)}) collective-permute-start(f32[5,16]{1,0:T(8,128)S(1)} %slice.1564), channel_id=1, source_target_pairs={{0,16},{1,17},{2,18},{3,19},{4,20},{5,21},{6,22},{7,23},{8,24},{9,... | collective-permute-start | bytes 968 | tf_op jit(solution)/shard_map/ppermute | solution.py:39
  166.3 3.9 collective-permute-start.8
  174.1 3.9 collective-permute-done.26
  180.0 5.4 collective-permute-start.11
  188.1 2.4 collective-permute-start.28
  196.0 6.1 scatter.146
  202.0 4.5 dynamic-slice_select_fusion.3
  206.5 24.3 %scatter.149 = f32[1,8,2,8,16,8]{5,4,3,2,1,0:T(8,128)S(1)} dynamic-update-slice(f32[1,8,2,8,16,8]{5,4,3,2,1,0:T(8,128)S(1)} %scatter.146, f32[1,8,2,8,15,1]{5,4,3,2,1,0:T(8,128)} %dynamic-slice_select_fusion.3, s32[]{:T(128)} %constant.794.clone.1, s32[]{:T(128)} %constant.794.clone.1, s32[]{:T(128)} %constant.794.clone.1, s32[]{:T(128)} %constant.794.clone.1, s32[]{:T(128)} %bitcast.12, s32[]{:T(128)} %bitcast.13) | dynamic-update-slice | bytes 15364 | tf_op jit(solution)/shard_map/scatter | solution.py:162
  237.0 8.7 %fusion.53 = f32[8,2,8,16,8]{3,4,2,1,0:T(8,128)S(1)} fusion(f32[8,8,1,1,1]{0,1,4,3,2:T(8,128)S(1)} %copy-done.10, f32[1,8,2,8,16,8]{5,4,3,2,1,0:T(8,128)} %multiply_add_fusion.3), kind=kOutput, calls=%fused_computation.183 | convolution fusion | flops 1572864 | bytes 131328 | tf_op jit(solution)/shard_map/aibjcl,lp->aibjcp/dot_general | solution.py:124
  252.7 6.8 %collective-permute-start.12 = (f32[1,2,8,128]{3,2,1,0:T(8,128)S(1)}, f32[1,2,8,128]{3,2,1,0:T(8,128)S(1)}, u32[]{:S(2)}, u32[]{:S(2)}) collective-permute-start(f32[1,2,8,128]{3,2,1,0:T(8,128)S(1)} %get-tuple-element.462), channel_id=1, source_target_pairs={{0,16},{16,32},{32,48},{48,64},{64,80},{80,96},{96,112},{112,128},... | collective-permute-start | bytes 24584 | tf_op jit(solution)/shard_map/ppermute | solution.py:28
  259.6 3.6 collective-permute-start.13
  264.6 3.6 collective-permute-start.15
  269.0 2.5 collective-permute-start.14
  276.7 2.5 slice_reduce_fusion.5
  281.1 6.5 %scatter.156 = f32[1,8,2,8,16,8]{5,4,3,2,1,0:T(8,128)} dynamic-update-slice(f32[1,8,2,8,16,8]{5,4,3,2,1,0:T(8,128)} %reshape.2685, f32[1,8,2,8,15,1]{5,4,3,2,1,0:T(8,128)} %copy.461, s32[]{:T(128)} %constant.794.clone.1, s32[]{:T(128)} %constant.794.clone.1, s32[]{:T(128)} %constant.794.clone.1, s32[]{:T(128)} %constant.794.clone.1, s32[]{:T(128)} %constant.796.clone.1, s32[]{:T(128)} %constant.794.clone.1) | dynamic-update-slice | bytes 15364 | tf_op jit(solution)/shard_map/scatter | solution.py:162
  287.6 4.8 dynamic-slice_select_fusion.2
  292.4 24.1 %scatter.159 = f32[1,8,2,8,16,8]{5,4,3,2,1,0:T(8,128)} dynamic-update-slice(f32[1,8,2,8,16,8]{5,4,3,2,1,0:T(8,128)} %scatter.156, f32[1,8,2,8,15,1]{5,4,3,2,1,0:T(8,128)} %dynamic-slice_select_fusion.2, s32[]{:T(128)} %constant.794.clone.1, s32[]{:T(128)} %constant.794.clone.1, s32[]{:T(128)} %constant.794.clone.1, s32[]{:T(128)} %constant.794.clone.1, s32[]{:T(128)} %bitcast.12, s32[]{:T(128)} %bitcast.13) | dynamic-update-slice | bytes 15364 | tf_op jit(solution)/shard_map/scatter | solution.py:162
  316.5 3.2 fusion.58
  324.4 8.7 %fusion.51 = f32[8,2,8,16,8]{3,4,2,1,0:T(8,128)S(1)} fusion(f32[8,8,1,1,1]{0,1,4,3,2:T(8,128)S(1)} %copy-done.10, f32[1,8,2,8,16,8]{5,4,3,2,1,0:T(8,128)} %fusion.58), kind=kOutput, calls=%fused_computation.181 | convolution fusion | flops 1572864 | bytes 131328 | tf_op jit(solution)/shard_map/aibjcl,lp->aibjcp/dot_general | solution.py:124
  340.1 4.0 collective-permute-start.16
  344.2 6.9 %collective-permute-start.17 = (f32[1,2,8,128]{3,2,1,0:T(8,128)S(1)}, f32[1,2,8,128]{3,2,1,0:T(8,128)S(1)}, u32[]{:S(2)}, u32[]{:S(2)}) collective-permute-start(f32[1,2,8,128]{3,2,1,0:T(8,128)S(1)} %get-tuple-element.459), channel_id=1, source_target_pairs={{16,0},{32,16},{48,32},{64,48},{80,64},{96,80},{112,96},{128,112},... | collective-permute-start | bytes 24584 | tf_op jit(solution)/shard_map/ppermute | solution.py:31
  352.0 3.6 collective-permute-start.19
  364.1 2.5 slice_reduce_fusion.3
  368.6 6.5 %scatter.166 = f32[1,8,2,8,16,8]{5,4,3,2,1,0:T(8,128)} dynamic-update-slice(f32[1,8,2,8,16,8]{5,4,3,2,1,0:T(8,128)} %reshape.2691, f32[1,8,2,8,15,1]{5,4,3,2,1,0:T(8,128)} %copy.475, s32[]{:T(128)} %constant.794.clone.1, s32[]{:T(128)} %constant.794.clone.1, s32[]{:T(128)} %constant.794.clone.1, s32[]{:T(128)} %constant.794.clone.1, s32[]{:T(128)} %constant.796.clone.1, s32[]{:T(128)} %constant.794.clone.1) | dynamic-update-slice | bytes 15364 | tf_op jit(solution)/shard_map/scatter | solution.py:162
  375.1 4.8 dynamic-slice_select_fusion.1
  379.9 24.1 %scatter.169 = f32[1,8,2,8,16,8]{5,4,3,2,1,0:T(8,128)} dynamic-update-slice(f32[1,8,2,8,16,8]{5,4,3,2,1,0:T(8,128)} %scatter.166, f32[1,8,2,8,15,1]{5,4,3,2,1,0:T(8,128)} %dynamic-slice_select_fusion.1, s32[]{:T(128)} %constant.794.clone.1, s32[]{:T(128)} %constant.794.clone.1, s32[]{:T(128)} %constant.794.clone.1, s32[]{:T(128)} %constant.794.clone.1, s32[]{:T(128)} %bitcast.12, s32[]{:T(128)} %bitcast.13) | dynamic-update-slice | bytes 15364 | tf_op jit(solution)/shard_map/scatter | solution.py:162
  404.0 4.1 multiply_add_fusion
  412.8 8.7 %fusion.49 = f32[8,2,8,16,8]{3,4,2,1,0:T(8,128)S(1)} fusion(f32[8,8,1,1,1]{0,1,4,3,2:T(8,128)S(1)} %copy-done.10, f32[1,8,2,8,16,8]{5,4,3,2,1,0:T(8,128)} %multiply_add_fusion), kind=kOutput, calls=%fused_computation.179 | convolution fusion | flops 1572864 | bytes 131328 | tf_op jit(solution)/shard_map/aibjcl,lp->aibjcp/dot_general | solution.py:124
  430.5 9.5 %collective-permute-start.30 = (f32[1,2,8,128]{3,2,1,0:T(8,128)S(1)}, f32[1,2,8,128]{3,2,1,0:T(8,128)S(1)}, u32[]{:S(2)}, u32[]{:S(2)}) collective-permute-start(f32[1,2,8,128]{3,2,1,0:T(8,128)S(1)} %get-tuple-element.455), channel_id=1, source_target_pairs={{16,0},{32,16},{48,32},{64,48},{80,64},{96,80},{112,96},{128,112},... | collective-permute-start | bytes 24584 | tf_op jit(solution)/shard_map/ppermute | solution.py:31
  440.9 3.6 collective-permute-start.32
  458.1 4.4 scatter.176
  462.5 3.2 dynamic-slice_select_fusion
  465.7 24.3 %scatter.179 = f32[1,8,2,8,16,8]{5,4,3,2,1,0:T(8,128)S(1)} dynamic-update-slice(f32[1,8,2,8,16,8]{5,4,3,2,1,0:T(8,128)S(1)} %scatter.176, f32[1,8,2,8,15,1]{5,4,3,2,1,0:T(8,128)} %dynamic-slice_select_fusion, s32[]{:T(128)} %constant.794.clone.1, s32[]{:T(128)} %constant.794.clone.1, s32[]{:T(128)} %constant.794.clone.1, s32[]{:T(128)} %constant.794.clone.1, s32[]{:T(128)} %bitcast.12, s32[]{:T(128)} %bitcast.13) | dynamic-update-slice | bytes 15364 | tf_op jit(solution)/shard_map/scatter | solution.py:162
  493.3 109.3 %all-reduce = (f32[]{:T(128)}, f32[]{:T(128)}) all-reduce(f32[]{:T(128)} %get-tuple-element.435, f32[]{:T(128)} %get-tuple-element.434), channel_id=1, replica_groups=mesh['gx'=32,'gz'=16] {'gx','gz'}, use_global_device_ids=true, to_apply=%region_2.0 | all-reduce | flops 2 | bytes 16 | tf_op jit(solution)/shard_map/psum | solution.py:243
  (295 shorter events, 131.8 us)
Async XLA Ops:
  3.6 11.0 %copy-start.14 = (f32[1,8,2,8,128]{4,3,2,1,0:T(8,128)S(1)}, f32[1,8,2,8,128]{4,3,2,1,0:T(8,128)}, u32[]{:S(2)}) copy-start(f32[1,8,2,8,128]{4,3,2,1,0:T(8,128)} %param.90) | copy-start | bytes 196612
  3.7 18.2 %collective-permute-start.5 = (f32[1,2,8,128]{3,1,2,0:T(2,128)S(1)}, f32[1,2,8,128]{3,1,2,0:T(2,128)S(1)}, u32[]{:S(2)}, u32[]{:S(2)}) collective-permute-start(f32[1,2,8,128]{3,1,2,0:T(2,128)S(1)} %get-tuple-element.472), channel_id=1, source_target_pairs={{16,0},{32,16},{48,32},{64,48},{80,64},{96,80},{112,96},{128,112},... | collective-permute-start | bytes 24584 | tf_op jit(solution)/shard_map/ppermute | solution.py:31
  12.4 6.5 %copy-start.26 = (s32[6]{0:T(128)S(1)}, s32[6]{0:T(128)}, u32[]{:S(2)}) copy-start(s32[6]{0:T(128)} %constant.798.clone.1) | copy-start | bytes 76
  12.5 7.8 %copy-start.11 = (f32[1,1,10,32,16]{3,4,2,1,0:T(8,128)S(1)}, f32[1,1,10,32,16]{3,4,2,1,0:T(8,128)}, u32[]{:S(2)}) copy-start(f32[1,1,10,32,16]{3,4,2,1,0:T(8,128)} %param.92) | copy-start | bytes 61444
  12.5 9.4 %collective-permute-start.4 = (f32[1,2,8,128]{3,1,2,0:T(2,128)S(1)}, f32[1,2,8,128]{3,1,2,0:T(2,128)S(1)}, u32[]{:S(2)}, u32[]{:S(2)}) collective-permute-start(f32[1,2,8,128]{3,1,2,0:T(2,128)S(1)} %get-tuple-element.471), channel_id=1, source_target_pairs={{0,16},{16,32},{32,48},{48,64},{64,80},{80,96},{96,112},{112,128},... | collective-permute-start | bytes 24584 | tf_op jit(solution)/shard_map/ppermute | solution.py:28
  14.6 5.8 collective-permute-start
  16.5 5.3 collective-permute-start.1
  22.0 14.2 %collective-permute-start.7 = (f32[1,8,1,128]{3,1,2,0:T(8,128)S(1)}, f32[1,8,1,128]{3,1,2,0:T(8,128)S(1)}, u32[]{:S(2)}, u32[]{:S(2)}) collective-permute-start(f32[1,8,1,128]{3,1,2,0:T(8,128)S(1)} %get-tuple-element.496), channel_id=1, source_target_pairs={{1,0},{2,1},{3,2},{4,3},{5,4},{6,5},{7,6},{8,7},{9,8},{10,9},{11,1... | collective-permute-start | bytes 12296 | tf_op jit(solution)/shard_map/ppermute | solution.py:31
  30.7 5.6 collective-permute-start.6
  32.6 5.6 collective-permute-start.2
  38.2 9.1 %collective-permute-start.3 = (f32[1,8,1,128]{3,1,2,0:T(8,128)S(1)}, f32[1,8,1,128]{3,1,2,0:T(8,128)S(1)}, u32[]{:S(2)}, u32[]{:S(2)}) collective-permute-start(f32[1,8,1,128]{3,1,2,0:T(8,128)S(1)} %get-tuple-element.500), channel_id=1, source_target_pairs={{1,0},{2,1},{3,2},{4,3},{5,4},{6,5},{7,6},{8,7},{9,8},{10,9},{11,1... | collective-permute-start | bytes 12296 | tf_op jit(solution)/shard_map/ppermute | solution.py:31
  61.9 24.4 %copy-start.3 = (f32[1,8,2,8,15,1]{5,4,3,2,1,0:T(8,128)S(1)}, f32[1,8,2,8,15,1]{5,4,3,2,1,0:T(8,128)}, u32[]{:S(2)}) copy-start(f32[1,8,2,8,15,1]{5,4,3,2,1,0:T(8,128)} %get-tuple-element.516) | copy-start | bytes 23044
  112.9 2.3 copy-start.13
  112.9 2.5 copy-start.10
  112.9 11.9 %collective-permute-start.20 = (f32[9,16]{1,0:T(8,128)S(1)}, f32[9,16]{1,0:T(8,128)S(1)}, u32[]{:S(2)}, u32[]{:S(2)}) collective-permute-start(f32[9,16]{1,0:T(8,128)S(1)} %slice.1644), channel_id=1, source_target_pairs={{0,1},{1,0},{2,3},{3,2},{4,5},{5,4},{6,7},{7,6},{8,9},{9,8},{10,11... | collective-permute-start | bytes 1736 | tf_op jit(solution)/shard_map/ppermute | solution.py:39
  124.8 5.5 collective-permute-start.21
  130.3 10.0 %collective-permute-start.22 = (f32[7,16]{1,0:T(8,128)S(1)}, f32[7,16]{1,0:T(8,128)S(1)}, u32[]{:S(2)}, u32[]{:S(2)}) collective-permute-start(f32[7,16]{1,0:T(8,128)S(1)} %slice.1560), channel_id=1, source_target_pairs={{0,4},{1,5},{2,6},{3,7},{4,0},{5,1},{6,2},{7,3},{8,12},{9,13},{10,... | collective-permute-start | bytes 1352 | tf_op jit(solution)/shard_map/ppermute | solution.py:39
  140.3 13.1 %collective-permute-start.23 = (f32[6,16]{1,0:T(8,128)S(1)}, f32[6,16]{1,0:T(8,128)S(1)}, u32[]{:S(2)}, u32[]{:S(2)}) collective-permute-start(f32[6,16]{1,0:T(8,128)S(1)} %slice.1562), channel_id=1, source_target_pairs={{0,8},{1,9},{2,10},{3,11},{4,12},{5,13},{6,14},{7,15},{8,0},{9,1},... | collective-permute-start | bytes 1160 | tf_op jit(solution)/shard_map/ppermute | solution.py:39
  153.4 10.9 %collective-permute-start.24 = (f32[5,16]{1,0:T(8,128)S(1)}, f32[5,16]{1,0:T(8,128)S(1)}, u32[]{:S(2)}, u32[]{:S(2)}) collective-permute-start(f32[5,16]{1,0:T(8,128)S(1)} %slice.1564), channel_id=1, source_target_pairs={{0,16},{1,17},{2,18},{3,19},{4,20},{5,21},{6,22},{7,23},{8,24},{9,... | collective-permute-start | bytes 968 | tf_op jit(solution)/shard_map/ppermute | solution.py:39
  164.3 7.8 %collective-permute-start.25 = (f32[4,16]{1,0:T(4,128)S(1)}, f32[4,16]{1,0:T(4,128)S(1)}, u32[]{:S(2)}, u32[]{:S(2)}) collective-permute-start(f32[4,16]{1,0:T(4,128)S(1)} %slice.1566), channel_id=1, source_target_pairs={{0,32},{1,33},{2,34},{3,35},{4,36},{5,37},{6,38},{7,39},{8,40},{9,... | collective-permute-start | bytes 776 | tf_op jit(solution)/shard_map/ppermute | solution.py:39
  166.3 13.6 %collective-permute-start.8 = (f32[1,2,8,128]{3,2,1,0:T(8,128)S(1)}, f32[1,2,8,128]{3,2,1,0:T(8,128)S(1)}, u32[]{:S(2)}, u32[]{:S(2)}) collective-permute-start(f32[1,2,8,128]{3,2,1,0:T(8,128)S(1)} %get-tuple-element.466), channel_id=1, source_target_pairs={{0,16},{16,32},{32,48},{48,64},{64,80},{80,96},{96,112},{112,128},... | collective-permute-start | bytes 24584 | tf_op jit(solution)/shard_map/ppermute | solution.py:28
  170.2 9.8 %collective-permute-start.9 = (f32[1,2,8,128]{3,2,1,0:T(8,128)S(1)}, f32[1,2,8,128]{3,2,1,0:T(8,128)S(1)}, u32[]{:S(2)}, u32[]{:S(2)}) collective-permute-start(f32[1,2,8,128]{3,2,1,0:T(8,128)S(1)} %get-tuple-element.467), channel_id=1, source_target_pairs={{16,0},{32,16},{48,32},{64,48},{80,64},{96,80},{112,96},{128,112},... | collective-permute-start | bytes 24584 | tf_op jit(solution)/shard_map/ppermute | solution.py:31
  172.1 5.8 collective-permute-start.26
  178.0 7.4 %collective-permute-start.27 = (f32[2,16]{1,0:T(2,128)S(1)}, f32[2,16]{1,0:T(2,128)S(1)}, u32[]{:S(2)}, u32[]{:S(2)}) collective-permute-start(f32[2,16]{1,0:T(2,128)S(1)} %slice.1570), channel_id=1, source_target_pairs={{0,128},{1,129},{2,130},{3,131},{4,132},{5,133},{6,134},{7,135},{8... | collective-permute-start | bytes 392 | tf_op jit(solution)/shard_map/ppermute | solution.py:39
  180.0 6.1 %collective-permute-start.11 = (f32[1,8,1,128]{3,1,2,0:T(8,128)S(1)}, f32[1,8,1,128]{3,1,2,0:T(8,128)S(1)}, u32[]{:S(2)}, u32[]{:S(2)}) collective-permute-start(f32[1,8,1,128]{3,1,2,0:T(8,128)S(1)} %get-tuple-element.492), channel_id=1, source_target_pairs={{1,0},{2,1},{3,2},{4,3},{5,4},{6,5},{7,6},{8,7},{9,8},{10,9},{11,1... | collective-permute-start | bytes 12296 | tf_op jit(solution)/shard_map/ppermute | solution.py:31
  186.1 5.8 collective-permute-start.10
  188.1 71.4 %collective-permute-start.28 = (f32[1,16]{1,0:T(1,128)S(1)}, f32[1,16]{1,0:T(1,128)S(1)}, u32[]{:S(2)}, u32[]{:S(2)}) collective-permute-start(f32[1,16]{1,0:T(1,128)S(1)} %slice.1572), channel_id=1, source_target_pairs={{0,256},{1,257},{2,258},{3,259},{4,260},{5,261},{6,262},{7,263},{8... | collective-permute-start | bytes 200 | tf_op jit(solution)/shard_map/ppermute | solution.py:39
  237.0 8.7 %copy-start.7 = (f32[8,2,8,16,8]{3,2,4,1,0:T(8,128)S(1)}, f32[8,2,8,16,8]{3,2,4,1,0:T(8,128)}, u32[]{:S(2)}) copy-start(f32[8,2,8,16,8]{3,2,4,1,0:T(8,128)} %copy.450) | copy-start | bytes 196612
  245.7 1.1 copy-start.5
  252.7 10.5 %collective-permute-start.12 = (f32[1,2,8,128]{3,2,1,0:T(8,128)S(1)}, f32[1,2,8,128]{3,2,1,0:T(8,128)S(1)}, u32[]{:S(2)}, u32[]{:S(2)}) collective-permute-start(f32[1,2,8,128]{3,2,1,0:T(8,128)S(1)} %get-tuple-element.462), channel_id=1, source_target_pairs={{0,16},{16,32},{32,48},{48,64},{64,80},{80,96},{96,112},{112,128},... | collective-permute-start | bytes 24584 | tf_op jit(solution)/shard_map/ppermute | solution.py:28
  259.6 5.0 collective-permute-start.13
  264.6 4.4 collective-permute-start.15
  269.0 5.8 collective-permute-start.14
  324.4 8.7 %copy-start.8 = (f32[8,2,8,16,8]{3,2,4,1,0:T(8,128)S(1)}, f32[8,2,8,16,8]{3,2,4,1,0:T(8,128)}, u32[]{:S(2)}) copy-start(f32[8,2,8,16,8]{3,2,4,1,0:T(8,128)} %copy.464) | copy-start | bytes 196612
  340.1 11.1 %collective-permute-start.16 = (f32[1,2,8,128]{3,2,1,0:T(8,128)S(1)}, f32[1,2,8,128]{3,2,1,0:T(8,128)S(1)}, u32[]{:S(2)}, u32[]{:S(2)}) collective-permute-start(f32[1,2,8,128]{3,2,1,0:T(8,128)S(1)} %get-tuple-element.458), channel_id=1, source_target_pairs={{0,16},{16,32},{32,48},{48,64},{64,80},{80,96},{96,112},{112,128},... | collective-permute-start | bytes 24584 | tf_op jit(solution)/shard_map/ppermute | solution.py:28
  344.2 7.8 %collective-permute-start.17 = (f32[1,2,8,128]{3,2,1,0:T(8,128)S(1)}, f32[1,2,8,128]{3,2,1,0:T(8,128)S(1)}, u32[]{:S(2)}, u32[]{:S(2)}) collective-permute-start(f32[1,2,8,128]{3,2,1,0:T(8,128)S(1)} %get-tuple-element.459), channel_id=1, source_target_pairs={{16,0},{32,16},{48,32},{64,48},{80,64},{96,80},{112,96},{128,112},... | collective-permute-start | bytes 24584 | tf_op jit(solution)/shard_map/ppermute | solution.py:31
  352.0 4.4 collective-permute-start.19
  356.4 5.8 collective-permute-start.18
  412.8 8.7 %copy-start.9 = (f32[8,2,8,16,8]{3,2,4,1,0:T(8,128)S(1)}, f32[8,2,8,16,8]{3,2,4,1,0:T(8,128)}, u32[]{:S(2)}) copy-start(f32[8,2,8,16,8]{3,2,4,1,0:T(8,128)} %copy.483) | copy-start | bytes 196612
  428.5 11.5 %collective-permute-start.29 = (f32[1,2,8,128]{3,2,1,0:T(8,128)S(1)}, f32[1,2,8,128]{3,2,1,0:T(8,128)S(1)}, u32[]{:S(2)}, u32[]{:S(2)}) collective-permute-start(f32[1,2,8,128]{3,2,1,0:T(8,128)S(1)} %get-tuple-element.454), channel_id=1, source_target_pairs={{0,16},{16,32},{32,48},{48,64},{64,80},{80,96},{96,112},{112,128},... | collective-permute-start | bytes 24584 | tf_op jit(solution)/shard_map/ppermute | solution.py:28
  430.5 10.3 %collective-permute-start.30 = (f32[1,2,8,128]{3,2,1,0:T(8,128)S(1)}, f32[1,2,8,128]{3,2,1,0:T(8,128)S(1)}, u32[]{:S(2)}, u32[]{:S(2)}) collective-permute-start(f32[1,2,8,128]{3,2,1,0:T(8,128)S(1)} %get-tuple-element.455), channel_id=1, source_target_pairs={{16,0},{32,16},{48,32},{64,48},{80,64},{96,80},{112,96},{128,112},... | collective-permute-start | bytes 24584 | tf_op jit(solution)/shard_map/ppermute | solution.py:31
  440.9 4.4 collective-permute-start.32
  446.5 6.2 %collective-permute-start.31 = (f32[1,8,1,128]{3,1,2,0:T(8,128)}, f32[1,8,1,128]{3,1,2,0:T(8,128)}, u32[]{:S(2)}, u32[]{:S(2)}) collective-permute-start(f32[1,8,1,128]{3,1,2,0:T(8,128)} %get-tuple-element.481), channel_id=1, source_target_pairs={{0,1},{1,2},{2,3},{3,4},{4,5},{5,6},{6,7},{7,8},{8,9},{9,10},{10,1... | collective-permute-start | bytes 12296 | tf_op jit(solution)/shard_map/ppermute | solution.py:28
  449.1 1.2 copy-start
  450.4 1.2 copy-start.1
  451.6 1.1 copy-start.18
  490.0 1.2 copy-start.2
  491.3 112.7 %copy-start.12 = (f32[1,8,2,8,128]{4,3,2,1,0:T(8,128)S(1)}, f32[1,8,2,8,128]{4,3,2,1,0:T(8,128)}, u32[]{:S(2)}) copy-start(f32[1,8,2,8,128]{4,3,2,1,0:T(8,128)} %reshape.2707) | copy-start | bytes 196612
  (12 other events, 9.1 us)
where the time goes:
time: 618 us; the launch traced here: 607 us
  local copies, waits for them, and re-layouts  250 us (40%)
  starting transfers between devices  130 us (21%)
  blocking collectives  109 us (18%)
  matrix products  50.8 us (8%)
  other arithmetic  38.4 us (6%)
  waiting for transfers between devices  24.6 us (4%)
    scatter x12, local copies, waits for them, and re-layouts, sum_y(): cube = cube.at[..., 1:, 0].set(joined).at[..., :-1, 7].set(joined)  179 us
    psum x1, blocking collectives, per_device(): rz = lax.psum(local_rz, ('gx', 'gz'))  109 us
    ppermute x12, starting transfers between devices, extended(): lax.ppermute(lax.slice_in_dim(block, 0, width, axis=dim), axis, backward)  61.7 us
    ppermute x9, starting transfers between devices, partner_2(): return lax.ppermute(value, axis, pairs)  35 us
    dot_general x4, matrix products, element_apply(): jnp.einsum('aibjcl,lp->aibjcp', cube, stiffness, precision=highest)  34.2 us
    ppermute x12, starting transfers between devices, extended(): lax.ppermute(lax.slice_in_dim(block, block.shape[dim] - width, None, axis...  32.8 us
    another operation x16, local copies, waits for them, and re-layouts  27.3 us
    another operation x14, other arithmetic  24.3 us
  transfers between devices with their start and end apart: 33, of which 16 were waited for; matrix products, arithmetic and copies ran while one was open for 15% of the time, Pallas kernels for 0%

commit v1 on v0

v1 whole, which is shorter than its diff:
```python
import jax
import jax.numpy as jnp
import numpy as np
from jax import lax
from jax.experimental import pallas as pl
from jax.experimental.pallas import tpu as pltpu
from jax.sharding import PartitionSpec as P

CHEB = 4
N_GX = 32
N_GZ = 16
F32 = jnp.float32
HIGHEST = lax.Precision.HIGHEST

cheb_high = 2.0
cheb_low = 0.1
gll_inner = (
    -0.8717401485096066,
    -0.5917001814331423,
    -0.2092992179024789,
    0.2092992179024789,
    0.5917001814331423,
    0.8717401485096066,
)


def legendre_seven(points):
    before = np.ones(points.shape[0])
    current = points.copy()
    for degree in range(1, 7):
        following = ((2.0 * degree + 1.0) * points * current - degree * before) / (degree + 1.0)
        before = current
        current = following
    return current


def gll_tables():
    order = 7
    points = np.concatenate([[-1.0], np.array(gll_inner), [1.0]])
    values = legendre_seven(points)
    weights = 2.0 / (order * (order + 1) * values**2)
    count = order + 1
    deriv = np.zeros((count, count))
    for row_index in range(count):
        for col_index in range(count):
            if row_index != col_index:
                deriv[row_index, col_index] = values[row_index] / (
                    values[col_index] * (points[row_index] - points[col_index])
                )
    deriv[0, 0] = -order * (order + 1) / 4.0
    deriv[-1, -1] = order * (order + 1) / 4.0
    stiff = deriv.T @ (weights[:, None] * deriv)
    return (points, weights, stiff)


POINTS, WEIGHTS, STIFF = gll_tables()
KDIAG = np.diag(STIFF)
W = [float(v) for v in WEIGHTS]
KD = [float(v) for v in KDIAG]
K = [[float(v) for v in row] for row in STIFF]


def positions(count):
    return ((np.arange(count)[:, None] + (1.0 + POINTS[None, :]) / 2.0) / count).reshape(-1)


ALONG_X = np.stack([np.sin(np.pi * mode * positions(1)) for mode in (1, 2)])
ALONG_Z = np.stack([np.sin(np.pi * mode * positions(2)) for mode in (1, 2)])
ALONG_Y = np.stack([np.sin(np.pi * mode * positions(16)) for mode in range(1, 9)])
EDGE = np.array([0.5] + [1.0] * 6 + [0.5])


def build_tables():
    w_l = np.tile(WEIGHTS, 16)[None, :]
    k_l = np.tile(KDIAG, 16)[None, :]
    w_j = WEIGHTS[:, None]
    k_j = KDIAG[:, None]
    ones = np.ones((1, 128))
    across = np.ones(128)
    across[8::8] = 0.5
    across[7:127:8] = 0.5
    pieces = {
        "stiff": np.kron(np.eye(16), STIFF),
        "ww": w_j * w_l,
        "kw": k_j * w_l,
        "wk": w_j * k_l,
        "wl": np.ones((8, 1)) * w_l,
        "wj": w_j * ones,
        "mult": EDGE[:, None] * across[None, :],
        "expand": np.kron(np.eye(16), np.ones((1, 8))),
        "modes": np.tile(ALONG_Y, (4, 1)),
    }
    for b in range(2):
        for z in range(2):
            pieces[f"bz{b}{z}"] = ALONG_Z[b, 8 * z : 8 * z + 8, None] * ones
    offsets = {}
    rows = []
    start = 0
    for name, piece in pieces.items():
        offsets[name] = (start, start + piece.shape[0])
        rows.append(piece)
        start += piece.shape[0]
    return np.concatenate(rows).astype(np.float32), offsets


TABLE, OFFSETS = build_tables()


def chebyshev_steps():
    theta = 0.5 * (cheb_high + cheb_low)
    delta = 0.5 * (cheb_high - cheb_low)
    sigma = theta / delta
    rho = 1.0 / sigma
    steps = []
    for sweep in range(CHEB - 1):
        rho_next = 1.0 / (2.0 * sigma - rho)
        steps.append((rho_next * rho, 2.0 * rho_next / delta))
        rho = rho_next
    return theta, steps


THETA, STEPS = chebyshev_steps()


def table(table_ref, name):
    low, high = OFFSETS[name]
    return table_ref[low:high, :]


def lane_iota():
    return lax.broadcasted_iota(jnp.int32, (8, 128), 1)


def read(ref):
    return [[ref[i, z] for z in range(2)] for i in range(8)]


def write(ref, field):
    for i in range(8):
        for z in range(2):
            ref[i, z] = field[i][z]


def spread(row):
    return jnp.broadcast_to(row, (8, 128))


def sum_x(field, left, right):
    out = [list(pair) for pair in field]
    for z in range(2):
        out[0][z] = field[0][z] + left[z]
        out[7][z] = field[7][z] + right[z]
    return out


def sum_z(field, before, after):
    node = lax.broadcasted_iota(jnp.int32, (8, 128), 0)
    out = []
    for i in range(8):
        low, high = field[i]
        add_low = jnp.where(node == 0, spread(before(i)), jnp.where(node == 7, spread(high[0:1, :]), 0.0))
        add_high = jnp.where(node == 7, spread(after(i)), jnp.where(node == 0, spread(low[7:8, :]), 0.0))
        out.append([low + add_low, high + add_high])
    return out


def sum_y(field):
    lane = lane_iota()
    first = (lane % 8 == 0) & (lane > 0)
    last = (lane % 8 == 7) & (lane < 127)
    return [
        [
            value
            + jnp.where(
                last, pltpu.roll(value, 127, 1), jnp.where(first, pltpu.roll(value, 1, 1), 0.0)
            )
            for value in pair
        ]
        for pair in field
    ]


def wall(value):
    lane = lane_iota()
    return jnp.where((lane == 0) | (lane == 127), 0.0, value)


def each(function, *fields):
    return [[function(*(f[i][z] for f in fields)) for z in range(2)] for i in range(8)]


def metric_rows(metric_ref, m, z):
    return spread(metric_ref[2 * m + z : 2 * m + z + 1, :])


def element_apply(field, metric_ref, table_ref):
    stiff = table(table_ref, "stiff")
    stacked = jnp.concatenate([value for pair in field for value in pair], axis=0)
    along_l = jnp.dot(stacked, stiff, precision=HIGHEST, preferred_element_type=F32)
    along_j = jnp.dot(stiff, stacked, precision=HIGHEST, preferred_element_type=F32)
    out = [[None, None] for i in range(8)]
    for z in range(2):
        scale_x = metric_rows(metric_ref, 0, z) * table(table_ref, "ww")
        scale_z = metric_rows(metric_ref, 1, z) * table(table_ref, "wl")
        scale_y = metric_rows(metric_ref, 2, z) * table(table_ref, "wj")
        for p in range(8):
            along_i = K[0][p] * field[0][z]
            for i in range(1, 8):
                along_i = along_i + K[i][p] * field[i][z]
            row = 8 * (2 * p + z)
            out[p][z] = scale_x * along_i + W[p] * (
                scale_z * along_j[row : row + 8, :] + scale_y * along_l[row : row + 8, :]
            )
    return out


def diagonal_parts(metric_ref, base, table_ref, z):
    def row(m):
        return spread(metric_ref[base + 2 * m + z : base + 2 * m + z + 1, :])

    part_x = row(0) * table(table_ref, "ww")
    part_rest = row(1) * table(table_ref, "kw") + row(2) * table(table_ref, "wk")
    return part_x, part_rest


def write_x_faces(field, low_ref, high_ref):
    for z in range(2):
        low_ref[8 * z : 8 * z + 8, :] = field[0][z]
        high_ref[8 * z : 8 * z + 8, :] = field[7][z]


def write_z_faces(field, low_ref, high_ref):
    for i in range(8):
        low_ref[i : i + 1, :] = field[i][0][0:1, :]
        high_ref[i : i + 1, :] = field[i][1][7:8, :]


def halves(ref):
    return [ref[0:8, :], ref[8:16, :]]


def first_faces(load_ref, metric_ref, table_ref, rows_ref, low_ref, high_ref):
    expanded = jnp.dot(
        metric_ref[...], table(table_ref, "expand"), precision=HIGHEST, preferred_element_type=F32
    )
    rows_ref[0:6, :] = expanded
    rows_ref[6:8, :] = jnp.zeros((2, 128), F32)
    for face, ref in ((0, low_ref), (7, high_ref)):
        for z in range(2):
            ref[8 * z : 8 * z + 8, :] = load_ref[face, z]
        ref[16:22, :] = expanded
        ref[22:24, :] = jnp.zeros((2, 128), F32)


def first_z_faces(load_ref, rows_ref, left_ref, right_ref, table_ref, low_ref, high_ref):
    for z, node, ref in ((0, 0, low_ref), (1, 7, high_ref)):
        part_x, part_rest = diagonal_parts(rows_ref, 0, table_ref, z)
        for i in range(8):
            load = load_ref[i, z, node : node + 1, :]
            sum_of_x, sum_of_rest = part_x, part_rest
            if i in (0, 7):
                side = left_ref if i == 0 else right_ref
                load = load + side[8 * z + node : 8 * z + node + 1, :]
                side_x, side_rest = diagonal_parts(side, 16, table_ref, z)
                sum_of_x, sum_of_rest = part_x + side_x, part_rest + side_rest
            diagonal = KD[i] * sum_of_x + W[i] * sum_of_rest
            ref[i : i + 1, :] = load
            ref[8 + i : 9 + i, :] = diagonal[node : node + 1, :]


def send_along_z(field, extra, send_ref):
    here = lax.axis_index("gz")
    above = lax.rem(here + 1, N_GZ)
    for i in range(8):
        for chunk in range(N_GZ):
            send_ref[chunk, i : i + 1, :] = jnp.where(
                above == chunk, field[i][1][7:8, :], field[i][0][0:1, :]
            )
    for chunk in range(N_GZ):
        send_ref[chunk, 8:16, :] = extra


def send_along_x(field, extra, send_ref):
    here = lax.axis_index("gx")
    above = lax.rem(here + 1, N_GX)
    for chunk in range(N_GX):
        for z in range(2):
            send_ref[chunk, 8 * z : 8 * z + 8, :] = jnp.where(
                above == chunk, field[7][z], field[0][z]
            )
        send_ref[chunk, 16:24, :] = extra


def two_rows(first, second):
    node = lax.broadcasted_iota(jnp.int32, (8, 128), 0)
    return jnp.where(node == 0, spread(first), jnp.where(node == 1, spread(second), 0.0))


def begin(
    load_ref, rows_ref, left_ref, right_ref, before_ref, after_ref, factor_ref, table_ref,
    rhs_ref, inverse_ref, smooth_ref, applied_ref, send_ref,
):
    load = sum_x(read(load_ref), halves(left_ref), halves(right_ref))
    load = sum_z(load, lambda i: before_ref[i : i + 1, :], lambda i: after_ref[i : i + 1, :])
    rhs = each(wall, sum_y(load))
    diagonal = [[None, None] for i in range(8)]
    for z in range(2):
        part_x, part_rest = diagonal_parts(rows_ref, 0, table_ref, z)
        for i in range(8):
            sum_of_x, sum_of_rest = part_x, part_rest
            if i in (0, 7):
                side = left_ref if i == 0 else right_ref
                side_x, side_rest = diagonal_parts(side, 16, table_ref, z)
                sum_of_x, sum_of_rest = part_x + side_x, part_rest + side_rest
            diagonal[i][z] = KD[i] * sum_of_x + W[i] * sum_of_rest
    diagonal = sum_z(
        diagonal, lambda i: before_ref[8 + i : 9 + i, :], lambda i: after_ref[8 + i : 9 + i, :]
    )
    inverse = each(lambda d: wall(1.0 / d), sum_y(diagonal))
    smooth = each(lambda d, r: d * r / THETA, inverse, rhs)
    write(rhs_ref, rhs)
    write(inverse_ref, inverse)
    write(smooth_ref, smooth)
    applied = element_apply(smooth, rows_ref, table_ref)
    write(applied_ref, applied)

    mult = table(table_ref, "mult")
    weighted = [[rhs[i][z] * (mult * float(EDGE[i])) for z in range(2)] for i in range(8)]
    parts = []
    for a in range(2):
        along_x = []
        for z in range(2):
            total = float(ALONG_X[a, 0]) * weighted[0][z]
            for i in range(1, 8):
                total = total + float(ALONG_X[a, i]) * weighted[i][z]
            along_x.append(total)
        for b in range(2):
            both = (
                table(table_ref, f"bz{b}0") * along_x[0] + table(table_ref, f"bz{b}1") * along_x[1]
            )
            parts.append(jnp.sum(both, axis=0, keepdims=True))
    node = lax.broadcasted_iota(jnp.int32, (8, 128), 0)
    stacked = jnp.zeros((8, 128), F32)
    for index, part in enumerate(parts):
        stacked = jnp.where(node == index, spread(part), stacked)
    modes = lax.dot_general(
        stacked, table(table_ref, "modes"), (((1,), (1,)), ((), ())),
        precision=HIGHEST, preferred_element_type=F32,
    )
    owner = lax.broadcasted_iota(jnp.int32, (8, 32), 1) // 8
    row = lax.broadcasted_iota(jnp.int32, (8, 32), 0)
    coarse_rhs = jnp.sum(jnp.where(owner == row, modes, 0.0), axis=0, keepdims=True)
    own = jnp.dot(
        jnp.broadcast_to(coarse_rhs, (8, 32)), factor_ref[...],
        precision=HIGHEST, preferred_element_type=F32,
    )
    send_along_z(applied, two_rows(own[0:1, 0:128], own[0:1, 128:256]), send_ref)


def level_of_lane(first):
    return first + lax.broadcasted_iota(jnp.int32, (1, 128), 1) // 16


def tree_sum(rows_of, count, here, shift):
    total = jnp.zeros((1, 128), F32)
    mine = lax.shift_right_logical(jnp.full((1, 128), here, jnp.int32), shift)
    for e in range(count):
        other = lax.shift_right_logical(jnp.full((1, 128), e, jnp.int32), shift)
        total = total + jnp.where(other == mine, rows_of(e), 0.0)
    return total


def neighbours(axis, count):
    here = lax.axis_index(axis)
    return lax.rem(here + count - 1, count), lax.rem(here + 1, count)


def middle(applied_ref, received_ref, summed_ref, send_ref, *, tree):
    below, above = neighbours("gz", N_GZ)
    field = sum_z(
        read(applied_ref),
        lambda i: received_ref[below, i : i + 1, :],
        lambda i: received_ref[above, i : i + 1, :],
    )
    write(summed_ref, field)
    here = lax.axis_index("gz")
    if tree:
        first = tree_sum(lambda e: received_ref[e, 8:9, :], N_GZ, here, level_of_lane(0))
        second = tree_sum(lambda e: received_ref[e, 9:10, :], N_GZ, here, level_of_lane(8))
        extra = two_rows(first, second)
    else:
        extra = received_ref[0, 8:16, :]
        for e in range(1, N_GZ):
            extra = extra + received_ref[e, 8:16, :]
    send_along_x(field, extra, send_ref)


def x_faces_received(received_ref):
    below, above = neighbours("gx", N_GX)
    left = [received_ref[below, 8 * z : 8 * z + 8, :] for z in range(2)]
    right = [received_ref[above, 8 * z : 8 * z + 8, :] for z in range(2)]
    return left, right


def relax(step, image, rhs_ref, inverse_ref, smooth_ref, update_ref):
    first, second = STEPS[step]
    rhs, inverse, smooth, update = (
        read(rhs_ref), read(inverse_ref), read(smooth_ref), read(update_ref)
    )
    update = each(
        lambda u, d, r, a: first * u + (second * d) * (r - a), update, inverse, rhs, image
    )
    return each(lambda s, u: s + u, smooth, update), update


def after_tree(
    summed_ref, received_ref, rows_ref, rhs_ref, inverse_ref, smooth_ref, factor_ref, table_ref,
    next_ref, update_ref, coarse_ref, applied_ref, low_ref, high_ref, zlow_ref, zhigh_ref,
):
    left, right = x_faces_received(received_ref)
    image = each(wall, sum_y(sum_x(read(summed_ref), left, right)))
    smooth, update = relax(0, image, rhs_ref, inverse_ref, smooth_ref, smooth_ref)
    write(next_ref, smooth)
    write(update_ref, update)
    applied = element_apply(smooth, rows_ref, table_ref)
    write(applied_ref, applied)
    write_x_faces(applied, low_ref, high_ref)
    write_z_faces(applied, zlow_ref, zhigh_ref)

    here = lax.axis_index("gx")
    first = tree_sum(
        lambda e: received_ref[e, 16:17, :], N_GX, here, jnp.maximum(level_of_lane(0) - 4, 0)
    )
    second = tree_sum(lambda e: received_ref[e, 17:18, :], N_GX, here, level_of_lane(8) - 4)
    columns = jnp.broadcast_to(jnp.concatenate([first, second], axis=1), (8, 256))
    coarse = lax.dot_general(
        columns, factor_ref[...], (((1,), (1,)), ((), ())),
        precision=HIGHEST, preferred_element_type=F32,
    )
    owner = lax.broadcasted_iota(jnp.int32, (8, 32), 1) // 8
    row = lax.broadcasted_iota(jnp.int32, (8, 32), 0)
    across = jnp.dot(
        jnp.where(owner == row, coarse, 0.0), table(table_ref, "modes"),
        precision=HIGHEST, preferred_element_type=F32,
    )
    for z in range(2):
        along_z = []
        for a in range(2):
            along_z.append(
                table(table_ref, f"bz0{z}") * spread(across[2 * a : 2 * a + 1, :])
                + table(table_ref, f"bz1{z}") * spread(across[2 * a + 1 : 2 * a + 2, :])
            )
        for i in range(8):
            coarse_ref[i, z] = wall(
                float(ALONG_X[0, i]) * along_z[0] + float(ALONG_X[1, i]) * along_z[1]
            )


def join_edges(zlow_ref, zhigh_ref, left_ref, right_ref, low_ref, high_ref):
    for z, node, source, target in ((0, 0, zlow_ref, low_ref), (1, 7, zhigh_ref, high_ref)):
        row = 8 * z + node
        target[...] = source[...]
        target[0:1, :] = source[0:1, :] + left_ref[row : row + 1, :]
        target[7:8, :] = source[7:8, :] + right_ref[row : row + 1, :]


def assembled(applied_ref, left_ref, right_ref, before_ref, after_ref):
    field = sum_x(read(applied_ref), halves(left_ref), halves(right_ref))
    field = sum_z(field, lambda i: before_ref[i : i + 1, :], lambda i: after_ref[i : i + 1, :])
    return each(wall, sum_y(field))


def sweep_two(
    applied_ref, left_ref, right_ref, before_ref, after_ref,
    rows_ref, rhs_ref, inverse_ref, smooth_ref, update_ref, table_ref,
    next_ref, next_update_ref, out_ref, low_ref, high_ref, zlow_ref, zhigh_ref,
):
    image = assembled(applied_ref, left_ref, right_ref, before_ref, after_ref)
    smooth, update = relax(1, image, rhs_ref, inverse_ref, smooth_ref, update_ref)
    write(next_ref, smooth)
    write(next_update_ref, update)
    applied = element_apply(smooth, rows_ref, table_ref)
    write(out_ref, applied)
    write_x_faces(applied, low_ref, high_ref)
    write_z_faces(applied, zlow_ref, zhigh_ref)


def sweep_three(
    applied_ref, left_ref, right_ref, before_ref, after_ref,
    rows_ref, rhs_ref, inverse_ref, smooth_ref, update_ref, coarse_ref, load_ref, table_ref,
    precond_ref, out_ref, send_ref,
):
    image = assembled(applied_ref, left_ref, right_ref, before_ref, after_ref)
    smooth, update = relax(2, image, rhs_ref, inverse_ref, smooth_ref, update_ref)
    precond = each(lambda s, c: s + c, smooth, read(coarse_ref))
    write(precond_ref, precond)
    applied = element_apply(precond, rows_ref, table_ref)
    write(out_ref, applied)
    first = jnp.zeros((8, 128), F32)
    second = jnp.zeros((8, 128), F32)
    load = read(load_ref)
    for i in range(8):
        for z in range(2):
            first = first + load[i][z] * precond[i][z]
            second = second + applied[i][z] * precond[i][z]
    extra = two_rows(jnp.sum(first, axis=0, keepdims=True), jnp.sum(second, axis=0, keepdims=True))
    send_along_z(applied, extra, send_ref)


def finish(summed_ref, received_ref, precond_ref, rhs_ref, solution_ref, residual_ref):
    left, right = x_faces_received(received_ref)
    image = each(wall, sum_y(sum_x(read(summed_ref), left, right)))
    extra = received_ref[0, 16:24, :]
    for e in range(1, N_GX):
        extra = extra + received_ref[e, 16:24, :]
    totals = jnp.sum(extra, axis=1, keepdims=True)
    alpha = spread(totals[0:1, :] / totals[1:2, :])
    write(solution_ref, each(lambda p: alpha * p, read(precond_ref)))
    write(residual_ref, each(lambda r, a: r - alpha * a, read(rhs_ref), image))


FIELD = (8, 2, 8, 128)


def run(kernel, shapes, *operands, last=False):
    spec = pl.BlockSpec(memory_space=pltpu.VMEM)
    outs = [
        jax.ShapeDtypeStruct(shape, F32) if last else pltpu.VMEM(shape, F32) for shape in shapes
    ]
    operands = [pltpu.with_memory_space_constraint(value, pltpu.VMEM) for value in operands]
    return pl.pallas_call(
        kernel, out_shape=outs, in_specs=[spec] * len(operands), out_specs=[spec] * len(outs)
    )(*operands)


def exchange(low, high, axis):
    count = lax.axis_size(axis)
    up = [(i, (i + 1) % count) for i in range(count)]
    down = [(target, source) for source, target in up]
    return lax.ppermute(high, axis, up), lax.ppermute(low, axis, down)


def per_device(element_rhs_load, metric, coarse_factor):
    load = element_rhs_load.reshape(FIELD)
    constants = jnp.asarray(TABLE)
    factor = coarse_factor.reshape(10, 32, 16).transpose(1, 0, 2).reshape(32, 160)
    factor = jnp.pad(factor, ((0, 0), (0, 96)))
    rows, low, high = run(
        first_faces, [(8, 128), (24, 128), (24, 128)], load, metric.reshape(6, 16), constants
    )
    left, right = exchange(low, high, "gx")
    low, high = run(
        first_z_faces, [(16, 128), (16, 128)], load, rows, left, right, constants
    )
    before, after = exchange(low, high, "gz")
    rhs, inverse, smooth, applied, send = run(
        begin, [FIELD] * 4 + [(N_GZ, 16, 128)],
        load, rows, left, right, before, after, factor, constants,
    )
    received = lax.all_to_all(send, "gz", 0, 0, tiled=True)

    def middle_tree(*refs):
        middle(*refs, tree=True)

    def middle_plain(*refs):
        middle(*refs, tree=False)

    summed, send = run(middle_tree, [FIELD, (N_GX, 24, 128)], applied, received)
    received = lax.all_to_all(send, "gx", 0, 0, tiled=True)
    faces = [(16, 128)] * 2 + [(8, 128)] * 2
    smooth, update, coarse, applied, low, high, zlow, zhigh = run(
        after_tree, [FIELD] * 4 + faces,
        summed, received, rows, rhs, inverse, smooth, factor, constants,
    )
    left, right = exchange(low, high, "gx")
    zlow, zhigh = run(join_edges, [(8, 128)] * 2, zlow, zhigh, left, right)
    before, after = exchange(zlow, zhigh, "gz")
    smooth, update, applied, low, high, zlow, zhigh = run(
        sweep_two, [FIELD] * 3 + faces,
        applied, left, right, before, after, rows, rhs, inverse, smooth, update, constants,
    )
    left, right = exchange(low, high, "gx")
    zlow, zhigh = run(join_edges, [(8, 128)] * 2, zlow, zhigh, left, right)
    before, after = exchange(zlow, zhigh, "gz")
    precond, applied, send = run(
        sweep_three, [FIELD] * 2 + [(N_GZ, 16, 128)],
        applied, left, right, before, after,
        rows, rhs, inverse, smooth, update, coarse, load, constants,
    )
    received = lax.all_to_all(send, "gz", 0, 0, tiled=True)
    summed, send = run(middle_plain, [FIELD, (N_GX, 24, 128)], applied, received)
    received = lax.all_to_all(send, "gx", 0, 0, tiled=True)
    solution_field, residual = run(
        finish, [FIELD] * 2, summed, received, precond, rhs, last=True
    )
    shape = element_rhs_load.shape
    return solution_field.reshape(shape), residual.reshape(shape)


def solution(mesh):
    placed = (
        P("gx", None, "gz", None, None),
        P(None, "gx", "gz", None),
        P("gx", "gz", None, None, None),
    )
    return jax.shard_map(
        per_device,
        mesh=mesh,
        in_specs=placed,
        out_specs=(P("gx", None, "gz", None, None), P("gx", None, "gz", None, None)),
        check_vma=False,
    )
```

time: 618 us -> 143 us (0.23); the launches traced: 607 us -> 143 us
  local copies, waits for them, and re-layouts: 250 us -> 2.52 us
  starting transfers between devices: 130 us -> 47.5 us
  matrix products: 50.8 us -> 0 us
  other arithmetic: 38.4 us -> 0 us
  blocking collectives: 109 us -> 81.5 us
  waiting for transfers between devices: 24.6 us -> 7.36 us
    scatter x27 -> x0, local copies, waits for them, and re-layouts: 180 us -> none  [the longest x12 179 us: sum_y(): cube = cube.at[..., 1:, 0].set(joined).at[..., :-1, 7].set(joined)]
    psum x1 -> x0, blocking collectives: 109 us -> none  [per_device(): rz = lax.psum(local_rz, ('gx', 'gz'))]
    ppermute x33 -> x12, starting transfers between devices: 130 us -> 47.5 us  [exchange(): return (lax.ppermute(high, axis, up), lax.ppermute(low, axis, down))]
    all_to_all x0 -> x4, blocking collectives: none -> 81.5 us  [the longest x2 42.9 us: per_device(): received = lax.all_to_all(send, 'gx', 0, 0, tiled=True)]
    dot_general x20 -> x0, matrix products: 50.8 us -> none  [the longest x4 34.2 us: element_apply(): jnp.einsum('aibjcl,lp->aibjcp', cube, stiffness, precision=highest)]
    another operation x21 -> x0, local copies, waits for them, and re-layouts: 27.3 us -> none
    another operation x14 -> x0, other arithmetic: 24.3 us -> none
    ppermute x33 -> x12, waiting for transfers between devices: 24.6 us -> 7.36 us  [exchange(): return (lax.ppermute(high, axis, up), lax.ppermute(low, axis, down))]
  transfers between devices with their start and end apart: 33 -> 12, of which waited for: 16 -> 6; matrix products, arithmetic and copies ran while one was open for 15% -> 0% of each run, Pallas kernels for 0% -> 0%
where the time goes in v1:
time: 143 us
  blocking collectives  81.5 us (57%)
  starting transfers between devices  47.5 us (33%)
  waiting for transfers between devices  7.36 us (5%)
  Pallas kernels  2.89 us (2%)
  local copies, waits for them, and re-layouts  2.52 us (2%)
    ppermute x12, starting transfers between devices, exchange(): return (lax.ppermute(high, axis, up), lax.ppermute(low, axis, down))  47.5 us
    all_to_all x2, blocking collectives, per_device(): received = lax.all_to_all(send, 'gx', 0, 0, tiled=True)  42.9 us
    all_to_all x2, blocking collectives, per_device(): received = lax.all_to_all(send, 'gz', 0, 0, tiled=True)  38.6 us
    ppermute x12, waiting for transfers between devices, exchange(): return (lax.ppermute(high, axis, up), lax.ppermute(low, axis, down))  7.36 us
    pallas_call x11, Pallas kernels, run(): pl.pallas_call(kernel, out_shape=outs, in_specs=[spec] * len(operands), o...  2.89 us
  transfers between devices with their start and end apart: 12, of which 6 were waited for; matrix products, arithmetic and copies ran while one was open for 0% of the time, Pallas kernels for 0%

profile of v1, /device:TPU:1, one launch (start us, length us, event | category | flops | bytes accessed | tf_op | source)
XLA Modules:
  0.0 142.6 jit_solution(18318408396709774429)
XLA Ops:
  0.6 0.7 reshape.23.metric_ref
  1.3 0.0 copy-start
  1.3 0.9 copy-done
  2.2 0.0 copy-start.2
  2.2 0.8 copy-done.2
  3.1 0.0 copy-start.1
  3.1 0.1 shard_map.59
  3.2 4.6 %collective-permute-start = (f32[24,128]{1,0:T(8,128)S(1)}, f32[24,128]{1,0:T(8,128)S(1)}, u32[]{:S(2)}, u32[]{:S(2)}) collective-permute-start(f32[24,128]{1,0:T(8,128)S(1)} %get-tuple-element.41), channel_id=1, source_target_pairs={{0,16},{16,32},{32,48},{48,64},{64,80},{80,96},{96,112},{112,128},... | collective-permute-start | bytes 36872 | tf_op jit(solution)/shard_map/ppermute | solution.py:540
  7.8 6.1 %collective-permute-start.1 = (f32[24,128]{1,0:T(8,128)S(1)}, f32[24,128]{1,0:T(8,128)S(1)}, u32[]{:S(2)}, u32[]{:S(2)}) collective-permute-start(f32[24,128]{1,0:T(8,128)S(1)} %get-tuple-element.42), channel_id=1, source_target_pairs={{16,0},{32,16},{48,32},{64,48},{80,64},{96,80},{112,96},{128,112},... | collective-permute-start | bytes 36872 | tf_op jit(solution)/shard_map/ppermute | solution.py:540
  13.9 0.0 collective-permute-done.left_ref
  13.9 0.8 collective-permute-done.1.right_ref
  14.7 0.0 copy-done.1
  14.7 0.0 copy-start.4
  14.8 2.1 %collective-permute-start.2 = (f32[16,128]{1,0:T(8,128)S(1)}, f32[16,128]{1,0:T(8,128)S(1)}, u32[]{:S(2)}, u32[]{:S(2)}) collective-permute-start(f32[16,128]{1,0:T(8,128)S(1)} %get-tuple-element.43), channel_id=1, source_target_pairs={{0,1},{1,2},{2,3},{3,4},{4,5},{5,6},{6,7},{7,8},{8,9},{9,10},{10,1... | collective-permute-start | bytes 24584 | tf_op jit(solution)/shard_map/ppermute | solution.py:540
  16.8 9.2 %collective-permute-start.3 = (f32[16,128]{1,0:T(8,128)S(1)}, f32[16,128]{1,0:T(8,128)S(1)}, u32[]{:S(2)}, u32[]{:S(2)}) collective-permute-start(f32[16,128]{1,0:T(8,128)S(1)} %get-tuple-element.44), channel_id=1, source_target_pairs={{1,0},{2,1},{3,2},{4,3},{5,4},{6,5},{7,6},{8,7},{9,8},{10,9},{11,1... | collective-permute-start | bytes 24584 | tf_op jit(solution)/shard_map/ppermute | solution.py:540
  26.0 0.0 copy-done.4
  26.0 0.1 copy.7
  26.1 0.0 collective-permute-done.2.before_ref
  26.1 0.7 collective-permute-done.3.after_ref
  26.8 0.6 shard_map.61
  27.4 20.7 %all_to_all.20.refs_1_ = f32[16,16,128]{2,1,0:T(8,128)S(1)} all-to-all(f32[16,16,128]{2,1,0:T(8,128)S(1)} %get-tuple-element.46), channel_id=1, replica_groups=mesh['gx'=32,'gz'=16] {'gz'}, dimensions={0} | all-to-all | bytes 262144 | tf_op jit(solution)/shard_map/all_to_all | solution.py:560
  48.0 0.1 shard_map.62
  48.1 20.5 %all_to_all.21.received_ref = f32[32,24,128]{2,1,0:T(8,128)S(1)} all-to-all(f32[32,24,128]{2,1,0:T(8,128)S(1)} %get-tuple-element.48), channel_id=1, replica_groups=mesh['gx'=32,'gz'=16] {'gx'}, dimensions={0} | all-to-all | bytes 786432 | tf_op jit(solution)/shard_map/all_to_all | solution.py:569
  68.6 0.5 shard_map.63
  69.1 1.9 %collective-permute-start.4 = (f32[16,128]{1,0:T(8,128)S(1)}, f32[16,128]{1,0:T(8,128)S(1)}, u32[]{:S(2)}, u32[]{:S(2)}) collective-permute-start(f32[16,128]{1,0:T(8,128)S(1)} %get-tuple-element.53), channel_id=1, source_target_pairs={{0,16},{16,32},{32,48},{48,64},{64,80},{80,96},{96,112},{112,128},... | collective-permute-start | bytes 24584 | tf_op jit(solution)/shard_map/ppermute | solution.py:540
  71.0 2.4 %collective-permute-start.5 = (f32[16,128]{1,0:T(8,128)S(1)}, f32[16,128]{1,0:T(8,128)S(1)}, u32[]{:S(2)}, u32[]{:S(2)}) collective-permute-start(f32[16,128]{1,0:T(8,128)S(1)} %get-tuple-element.54), channel_id=1, source_target_pairs={{16,0},{32,16},{48,32},{64,48},{80,64},{96,80},{112,96},{128,112},... | collective-permute-start | bytes 24584 | tf_op jit(solution)/shard_map/ppermute | solution.py:540
  73.4 0.0 collective-permute-done.4.left_ref
  73.4 2.8 %collective-permute-done.5.right_ref = f32[16,128]{1,0:T(8,128)S(1)} collective-permute-done((f32[16,128]{1,0:T(8,128)S(1)}, f32[16,128]{1,0:T(8,128)S(1)}, u32[]{:S(2)}, u32[]{:S(2)}) %collective-permute-start.5) | collective-permute-done | bytes 8224 | tf_op jit(solution)/shard_map/ppermute | solution.py:540
  76.3 3.7 %collective-permute-start.6 = (f32[8,128]{1,0:T(8,128)S(1)}, f32[8,128]{1,0:T(8,128)S(1)}, u32[]{:S(2)}, u32[]{:S(2)}) collective-permute-start(f32[8,128]{1,0:T(8,128)S(1)} %get-tuple-element.57), channel_id=1, source_target_pairs={{0,1},{1,2},{2,3},{3,4},{4,5},{5,6},{6,7},{7,8},{8,9},{9,10},{10,1... | collective-permute-start | bytes 12296 | tf_op jit(solution)/shard_map/ppermute | solution.py:540
  80.0 2.8 %collective-permute-start.7 = (f32[8,128]{1,0:T(8,128)S(1)}, f32[8,128]{1,0:T(8,128)S(1)}, u32[]{:S(2)}, u32[]{:S(2)}) collective-permute-start(f32[8,128]{1,0:T(8,128)S(1)} %get-tuple-element.58), channel_id=1, source_target_pairs={{1,0},{2,1},{3,2},{4,3},{5,4},{6,5},{7,6},{8,7},{9,8},{10,9},{11,1... | collective-permute-start | bytes 12296 | tf_op jit(solution)/shard_map/ppermute | solution.py:540
  82.8 0.0 collective-permute-done.6.before_ref
  82.8 1.5 %collective-permute-done.7.after_ref = f32[8,128]{1,0:T(8,128)S(1)} collective-permute-done((f32[8,128]{1,0:T(8,128)S(1)}, f32[8,128]{1,0:T(8,128)S(1)}, u32[]{:S(2)}, u32[]{:S(2)}) %collective-permute-start.7) | collective-permute-done | bytes 4128 | tf_op jit(solution)/shard_map/ppermute | solution.py:540
  84.4 0.0 copy-start.3
  84.4 0.4 shard_map.65
  84.7 3.1 %collective-permute-start.8 = (f32[16,128]{1,0:T(8,128)S(1)}, f32[16,128]{1,0:T(8,128)S(1)}, u32[]{:S(2)}, u32[]{:S(2)}) collective-permute-start(f32[16,128]{1,0:T(8,128)S(1)} %get-tuple-element.62), channel_id=1, source_target_pairs={{0,16},{16,32},{32,48},{48,64},{64,80},{80,96},{96,112},{112,128},... | collective-permute-start | bytes 24584 | tf_op jit(solution)/shard_map/ppermute | solution.py:540
  87.8 5.1 %collective-permute-start.9 = (f32[16,128]{1,0:T(8,128)S(1)}, f32[16,128]{1,0:T(8,128)S(1)}, u32[]{:S(2)}, u32[]{:S(2)}) collective-permute-start(f32[16,128]{1,0:T(8,128)S(1)} %get-tuple-element.63), channel_id=1, source_target_pairs={{16,0},{32,16},{48,32},{64,48},{80,64},{96,80},{112,96},{128,112},... | collective-permute-start | bytes 24584 | tf_op jit(solution)/shard_map/ppermute | solution.py:540
  92.9 0.0 collective-permute-done.8.left_ref
  92.9 0.8 collective-permute-done.9.right_ref
  93.7 2.3 %collective-permute-start.10 = (f32[8,128]{1,0:T(8,128)S(1)}, f32[8,128]{1,0:T(8,128)S(1)}, u32[]{:S(2)}, u32[]{:S(2)}) collective-permute-start(f32[8,128]{1,0:T(8,128)S(1)} %get-tuple-element.66), channel_id=1, source_target_pairs={{0,1},{1,2},{2,3},{3,4},{4,5},{5,6},{6,7},{7,8},{8,9},{9,10},{10,1... | collective-permute-start | bytes 12296 | tf_op jit(solution)/shard_map/ppermute | solution.py:540
  96.1 4.2 %collective-permute-start.11 = (f32[8,128]{1,0:T(8,128)S(1)}, f32[8,128]{1,0:T(8,128)S(1)}, u32[]{:S(2)}, u32[]{:S(2)}) collective-permute-start(f32[8,128]{1,0:T(8,128)S(1)} %get-tuple-element.67), channel_id=1, source_target_pairs={{1,0},{2,1},{3,2},{4,3},{5,4},{6,5},{7,6},{8,7},{9,8},{10,9},{11,1... | collective-permute-start | bytes 12296 | tf_op jit(solution)/shard_map/ppermute | solution.py:540
  100.2 0.0 collective-permute-done.10.before_ref
  100.2 0.7 collective-permute-done.11.after_ref
  101.0 0.0 copy-done.3
  101.0 0.4 shard_map.67
  101.4 17.9 %all_to_all.22.refs_1_ = f32[16,16,128]{2,1,0:T(8,128)S(1)} all-to-all(f32[16,16,128]{2,1,0:T(8,128)S(1)} %get-tuple-element.72), channel_id=1, replica_groups=mesh['gx'=32,'gz'=16] {'gz'}, dimensions={0} | all-to-all | bytes 262144 | tf_op jit(solution)/shard_map/all_to_all | solution.py:590
  119.3 0.1 shard_map.68
  119.4 22.4 %all_to_all.23.received_ref = f32[32,24,128]{2,1,0:T(8,128)S(1)} all-to-all(f32[32,24,128]{2,1,0:T(8,128)S(1)} %get-tuple-element.74), channel_id=1, replica_groups=mesh['gx'=32,'gz'=16] {'gx'}, dimensions={0} | all-to-all | bytes 786432 | tf_op jit(solution)/shard_map/all_to_all | solution.py:592
  141.8 0.8 shard_map.69
  (4 shorter events, 0.0 us)
Async XLA Ops:
  1.3 0.9 copy-start
  2.2 0.8 copy-start.2
  3.1 11.7 %copy-start.1 = (f32[256,128]{1,0:T(8,128)S(1)}, f32[256,128]{1,0:T(8,128)}, u32[]{:S(2)}) copy-start(f32[256,128]{1,0:T(8,128)} %constant.5.clone.table_ref) | copy-start | bytes 393220
  3.2 10.7 %collective-permute-start = (f32[24,128]{1,0:T(8,128)S(1)}, f32[24,128]{1,0:T(8,128)S(1)}, u32[]{:S(2)}, u32[]{:S(2)}) collective-permute-start(f32[24,128]{1,0:T(8,128)S(1)} %get-tuple-element.41), channel_id=1, source_target_pairs={{0,16},{16,32},{32,48},{48,64},{64,80},{80,96},{96,112},{112,128},... | collective-permute-start | bytes 36872 | tf_op jit(solution)/shard_map/ppermute | solution.py:540
  7.8 6.9 %collective-permute-start.1 = (f32[24,128]{1,0:T(8,128)S(1)}, f32[24,128]{1,0:T(8,128)S(1)}, u32[]{:S(2)}, u32[]{:S(2)}) collective-permute-start(f32[24,128]{1,0:T(8,128)S(1)} %get-tuple-element.42), channel_id=1, source_target_pairs={{16,0},{32,16},{48,32},{64,48},{80,64},{96,80},{112,96},{128,112},... | collective-permute-start | bytes 36872 | tf_op jit(solution)/shard_map/ppermute | solution.py:540
  14.7 11.3 %copy-start.4 = (f32[1,1,10,32,16]{3,4,2,1,0:T(8,128)S(1)}, f32[1,1,10,32,16]{3,4,2,1,0:T(8,128)}, u32[]{:S(2)}) copy-start(f32[1,1,10,32,16]{3,4,2,1,0:T(8,128)} %param.6) | copy-start | bytes 61444
  14.8 11.4 %collective-permute-start.2 = (f32[16,128]{1,0:T(8,128)S(1)}, f32[16,128]{1,0:T(8,128)S(1)}, u32[]{:S(2)}, u32[]{:S(2)}) collective-permute-start(f32[16,128]{1,0:T(8,128)S(1)} %get-tuple-element.43), channel_id=1, source_target_pairs={{0,1},{1,2},{2,3},{3,4},{4,5},{5,6},{6,7},{7,8},{8,9},{9,10},{10,1... | collective-permute-start | bytes 24584 | tf_op jit(solution)/shard_map/ppermute | solution.py:540
  16.8 10.0 %collective-permute-start.3 = (f32[16,128]{1,0:T(8,128)S(1)}, f32[16,128]{1,0:T(8,128)S(1)}, u32[]{:S(2)}, u32[]{:S(2)}) collective-permute-start(f32[16,128]{1,0:T(8,128)S(1)} %get-tuple-element.44), channel_id=1, source_target_pairs={{1,0},{2,1},{3,2},{4,3},{5,4},{6,5},{7,6},{8,7},{9,8},{10,9},{11,1... | collective-permute-start | bytes 24584 | tf_op jit(solution)/shard_map/ppermute | solution.py:540
  69.1 4.3 %collective-permute-start.4 = (f32[16,128]{1,0:T(8,128)S(1)}, f32[16,128]{1,0:T(8,128)S(1)}, u32[]{:S(2)}, u32[]{:S(2)}) collective-permute-start(f32[16,128]{1,0:T(8,128)S(1)} %get-tuple-element.53), channel_id=1, source_target_pairs={{0,16},{16,32},{32,48},{48,64},{64,80},{80,96},{96,112},{112,128},... | collective-permute-start | bytes 24584 | tf_op jit(solution)/shard_map/ppermute | solution.py:540
  71.0 5.3 %collective-permute-start.5 = (f32[16,128]{1,0:T(8,128)S(1)}, f32[16,128]{1,0:T(8,128)S(1)}, u32[]{:S(2)}, u32[]{:S(2)}) collective-permute-start(f32[16,128]{1,0:T(8,128)S(1)} %get-tuple-element.54), channel_id=1, source_target_pairs={{16,0},{32,16},{48,32},{64,48},{80,64},{96,80},{112,96},{128,112},... | collective-permute-start | bytes 24584 | tf_op jit(solution)/shard_map/ppermute | solution.py:540
  76.3 6.5 %collective-permute-start.6 = (f32[8,128]{1,0:T(8,128)S(1)}, f32[8,128]{1,0:T(8,128)S(1)}, u32[]{:S(2)}, u32[]{:S(2)}) collective-permute-start(f32[8,128]{1,0:T(8,128)S(1)} %get-tuple-element.57), channel_id=1, source_target_pairs={{0,1},{1,2},{2,3},{3,4},{4,5},{5,6},{6,7},{7,8},{8,9},{9,10},{10,1... | collective-permute-start | bytes 12296 | tf_op jit(solution)/shard_map/ppermute | solution.py:540
  80.0 4.4 %collective-permute-start.7 = (f32[8,128]{1,0:T(8,128)S(1)}, f32[8,128]{1,0:T(8,128)S(1)}, u32[]{:S(2)}, u32[]{:S(2)}) collective-permute-start(f32[8,128]{1,0:T(8,128)S(1)} %get-tuple-element.58), channel_id=1, source_target_pairs={{1,0},{2,1},{3,2},{4,3},{5,4},{6,5},{7,6},{8,7},{9,8},{10,9},{11,1... | collective-permute-start | bytes 12296 | tf_op jit(solution)/shard_map/ppermute | solution.py:540
  84.4 16.6 %copy-start.3 = (f32[1,8,2,8,128]{4,3,2,1,0:T(8,128)S(1)}, f32[1,8,2,8,128]{4,3,2,1,0:T(8,128)}, u32[]{:S(2)}) copy-start(f32[1,8,2,8,128]{4,3,2,1,0:T(8,128)} %param.4) | copy-start | bytes 196612
  84.7 8.2 %collective-permute-start.8 = (f32[16,128]{1,0:T(8,128)S(1)}, f32[16,128]{1,0:T(8,128)S(1)}, u32[]{:S(2)}, u32[]{:S(2)}) collective-permute-start(f32[16,128]{1,0:T(8,128)S(1)} %get-tuple-element.62), channel_id=1, source_target_pairs={{0,16},{16,32},{32,48},{48,64},{64,80},{80,96},{96,112},{112,128},... | collective-permute-start | bytes 24584 | tf_op jit(solution)/shard_map/ppermute | solution.py:540
  87.8 5.9 %collective-permute-start.9 = (f32[16,128]{1,0:T(8,128)S(1)}, f32[16,128]{1,0:T(8,128)S(1)}, u32[]{:S(2)}, u32[]{:S(2)}) collective-permute-start(f32[16,128]{1,0:T(8,128)S(1)} %get-tuple-element.63), channel_id=1, source_target_pairs={{16,0},{32,16},{48,32},{64,48},{80,64},{96,80},{112,96},{128,112},... | collective-permute-start | bytes 24584 | tf_op jit(solution)/shard_map/ppermute | solution.py:540
  93.7 6.5 %collective-permute-start.10 = (f32[8,128]{1,0:T(8,128)S(1)}, f32[8,128]{1,0:T(8,128)S(1)}, u32[]{:S(2)}, u32[]{:S(2)}) collective-permute-start(f32[8,128]{1,0:T(8,128)S(1)} %get-tuple-element.66), channel_id=1, source_target_pairs={{0,1},{1,2},{2,3},{3,4},{4,5},{5,6},{6,7},{7,8},{8,9},{9,10},{10,1... | collective-permute-start | bytes 12296 | tf_op jit(solution)/shard_map/ppermute | solution.py:540
  96.1 4.9 %collective-permute-start.11 = (f32[8,128]{1,0:T(8,128)S(1)}, f32[8,128]{1,0:T(8,128)S(1)}, u32[]{:S(2)}, u32[]{:S(2)}) collective-permute-start(f32[8,128]{1,0:T(8,128)S(1)} %get-tuple-element.67), channel_id=1, source_target_pairs={{1,0},{2,1},{3,2},{4,3},{5,4},{6,5},{7,6},{8,7},{9,8},{10,9},{11,1... | collective-permute-start | bytes 12296 | tf_op jit(solution)/shard_map/ppermute | solution.py:540

commit v2 on v1

v2 whole, which is shorter than its diff:
```python
import jax
import jax.numpy as jnp
import numpy as np
from jax import lax
from jax.experimental import pallas as pl
from jax.experimental.pallas import tpu as pltpu
from jax.sharding import PartitionSpec as P

CHEB = 4
N_GX = 32
N_GZ = 16
F32 = jnp.float32
HIGHEST = lax.Precision.HIGHEST

cheb_high = 2.0
cheb_low = 0.1
gll_inner = (
    -0.8717401485096066,
    -0.5917001814331423,
    -0.2092992179024789,
    0.2092992179024789,
    0.5917001814331423,
    0.8717401485096066,
)


def legendre_seven(points):
    before = np.ones(points.shape[0])
    current = points.copy()
    for degree in range(1, 7):
        following = ((2.0 * degree + 1.0) * points * current - degree * before) / (degree + 1.0)
        before = current
        current = following
    return current


def gll_tables():
    order = 7
    points = np.concatenate([[-1.0], np.array(gll_inner), [1.0]])
    values = legendre_seven(points)
    weights = 2.0 / (order * (order + 1) * values**2)
    count = order + 1
    deriv = np.zeros((count, count))
    for row_index in range(count):
        for col_index in range(count):
            if row_index != col_index:
                deriv[row_index, col_index] = values[row_index] / (
                    values[col_index] * (points[row_index] - points[col_index])
                )
    deriv[0, 0] = -order * (order + 1) / 4.0
    deriv[-1, -1] = order * (order + 1) / 4.0
    stiff = deriv.T @ (weights[:, None] * deriv)
    return (points, weights, stiff)


POINTS, WEIGHTS, STIFF = gll_tables()
KDIAG = np.diag(STIFF)
W = [float(v) for v in WEIGHTS]
KD = [float(v) for v in KDIAG]
K = [[float(v) for v in row] for row in STIFF]


def positions(count):
    return ((np.arange(count)[:, None] + (1.0 + POINTS[None, :]) / 2.0) / count).reshape(-1)


ALONG_X = np.stack([np.sin(np.pi * mode * positions(1)) for mode in (1, 2)])
ALONG_Z = np.stack([np.sin(np.pi * mode * positions(2)) for mode in (1, 2)])
ALONG_Y = np.stack([np.sin(np.pi * mode * positions(16)) for mode in range(1, 9)])
EDGE = np.array([0.5] + [1.0] * 6 + [0.5])


def build_tables():
    w_l = np.tile(WEIGHTS, 16)[None, :]
    k_l = np.tile(KDIAG, 16)[None, :]
    w_j = WEIGHTS[:, None]
    k_j = KDIAG[:, None]
    ones = np.ones((1, 128))
    across = np.ones(128)
    across[8::8] = 0.5
    across[7:127:8] = 0.5
    pieces = {
        "stiff": np.kron(np.eye(16), STIFF),
        "ww": w_j * w_l,
        "kw": k_j * w_l,
        "wk": w_j * k_l,
        "wl": np.ones((8, 1)) * w_l,
        "wj": w_j * ones,
        "mult": EDGE[:, None] * across[None, :],
        "expand": np.kron(np.eye(16), np.ones((1, 8))),
        "modes": np.tile(ALONG_Y, (4, 1)),
    }
    for b in range(2):
        for z in range(2):
            pieces[f"bz{b}{z}"] = ALONG_Z[b, 8 * z : 8 * z + 8, None] * ones
    offsets = {}
    rows = []
    start = 0
    for name, piece in pieces.items():
        offsets[name] = (start, start + piece.shape[0])
        rows.append(piece)
        start += piece.shape[0]
    return np.concatenate(rows).astype(np.float32), offsets


TABLE, OFFSETS = build_tables()


def chebyshev_steps():
    theta = 0.5 * (cheb_high + cheb_low)
    delta = 0.5 * (cheb_high - cheb_low)
    sigma = theta / delta
    rho = 1.0 / sigma
    steps = []
    for sweep in range(CHEB - 1):
        rho_next = 1.0 / (2.0 * sigma - rho)
        steps.append((rho_next * rho, 2.0 * rho_next / delta))
        rho = rho_next
    return theta, steps


THETA, STEPS = chebyshev_steps()


def table(table_ref, name):
    low, high = OFFSETS[name]
    return table_ref[low:high, :]


def lane_iota():
    return lax.broadcasted_iota(jnp.int32, (8, 128), 1)


def read(ref, first=0, count=2):
    return [[ref[i, c] for c in range(first, first + count)] for i in range(8)]


def write(ref, field):
    for i in range(8):
        for c, value in enumerate(field[i]):
            ref[i, c] = value


def spread(row):
    return jnp.broadcast_to(row, (8, 128))


def sum_x(field, left, right):
    out = [list(row) for row in field]
    for c in range(len(field[0])):
        out[0][c] = field[0][c] + left[c]
        out[7][c] = field[7][c] + right[c]
    return out


def sum_z(field, before=None, after=None):
    node = lax.broadcasted_iota(jnp.int32, (8, 128), 0)
    count = len(field[0])
    out = []
    for i in range(8):
        lows = [None] + [field[i][c][7:8, :] for c in range(count - 1)]
        highs = [field[i][c][0:1, :] for c in range(1, count)] + [None]
        if before is not None:
            lows[0], highs[-1] = before(i), after(i)
        out.append(
            [
                field[i][c]
                + jnp.where(node == 0, spread(lows[c]), jnp.where(node == 7, spread(highs[c]), 0.0))
                for c in range(count)
                if lows[c] is not None and highs[c] is not None
            ]
        )
    return out


def sum_y(field):
    lane = lane_iota()
    first = (lane % 8 == 0) & (lane > 0)
    last = (lane % 8 == 7) & (lane < 127)
    return each(
        lambda value: value
        + jnp.where(last, pltpu.roll(value, 127, 1), jnp.where(first, pltpu.roll(value, 1, 1), 0.0)),
        field,
    )


def wall(value):
    lane = lane_iota()
    return jnp.where((lane == 0) | (lane == 127), 0.0, value)


def each(function, *fields):
    return [[function(*values) for values in zip(*rows)] for rows in zip(*fields)]


ROWS = 10


def metric_row(ref, base, m, column):
    row = base + ROWS * m + 4 + column
    return ref[row : row + 1, :]


def element_apply(field, first, metric_ref, table_ref):
    count = len(field[0])
    stiff = table(table_ref, "stiff")
    out = [[None] * count for i in range(8)]
    for c in range(count):
        stacked = jnp.concatenate([field[i][c] for i in range(8)], axis=0)
        along_l = jnp.dot(stacked, stiff, precision=HIGHEST, preferred_element_type=F32)
        along_j = jnp.dot(
            stiff[0:64, 0:64], stacked, precision=HIGHEST, preferred_element_type=F32
        )
        rows = [spread(metric_row(metric_ref, 0, m, first + c)) for m in range(3)]
        scale_x = rows[0] * table(table_ref, "ww")
        scale_z = rows[1] * table(table_ref, "wl")
        scale_y = rows[2] * table(table_ref, "wj")
        for p in range(8):
            along_i = K[0][p] * field[0][c]
            for i in range(1, 8):
                along_i = along_i + K[i][p] * field[i][c]
            out[p][c] = scale_x * along_i + W[p] * (
                scale_z * along_j[8 * p : 8 * p + 8, :] + scale_y * along_l[8 * p : 8 * p + 8, :]
            )
    return out


def diagonal_parts(ref, base, column, table_ref):
    part_x = spread(metric_row(ref, base, 0, column)) * table(table_ref, "ww")
    part_rest = spread(metric_row(ref, base, 1, column)) * table(table_ref, "kw") + spread(
        metric_row(ref, base, 2, column)
    ) * table(table_ref, "wk")
    return part_x, part_rest


def diagonal_sum_x(rows_ref, left_ref, right_ref, column, table_ref):
    part_x, part_rest = diagonal_parts(rows_ref, 0, column, table_ref)
    out = []
    for i in range(8):
        sum_of_x, sum_of_rest = part_x, part_rest
        if i in (0, 7):
            side = left_ref if i == 0 else right_ref
            side_x, side_rest = diagonal_parts(side, FACE_METRIC, column, table_ref)
            sum_of_x, sum_of_rest = part_x + side_x, part_rest + side_rest
        out.append(KD[i] * sum_of_x + W[i] * sum_of_rest)
    return out


def write_x_faces(field, low_ref, high_ref):
    for c in range(len(field[0])):
        low_ref[8 * c : 8 * c + 8, :] = field[0][c]
        high_ref[8 * c : 8 * c + 8, :] = field[7][c]


def faces(ref, count):
    return [ref[8 * c : 8 * c + 8, :] for c in range(count)]


def pack(load_ref, metric_ref, table_ref, near_ref, up_ref, down_ref):
    expanded = jnp.dot(
        metric_ref[...], table(table_ref, "expand"), precision=HIGHEST, preferred_element_type=F32
    )
    for ref, start in ((near_ref, 128), (up_ref, 72), (down_ref, 72)):
        ref[start : start + 6, :] = expanded
        ref[start + 6 : start + 8, :] = jnp.zeros((2, 128), F32)
    for i in range(8):
        for z in range(2):
            near_ref[8 * (2 * i + z) : 8 * (2 * i + z) + 8, :] = load_ref[i, z]
        up_ref[8 * i : 8 * i + 8, :] = load_ref[i, 1]
        up_ref[64 + i : 65 + i, :] = load_ref[i, 0, 7:8, :]
        down_ref[8 * i : 8 * i + 8, :] = load_ref[i, 0]
        down_ref[64 + i : 65 + i, :] = load_ref[i, 1, 0:1, :]


FACE_METRIC = 72
FACE_ROWS = 104


def gather(
    near_ref, below_ref, far_below_ref, above_ref, far_above_ref,
    load_ref, edge_ref, rows_ref, low_ref, high_ref,
):
    for i in range(8):
        load_ref[i, 0] = far_below_ref[8 * i : 8 * i + 8, :]
        load_ref[i, 7] = far_above_ref[8 * i : 8 * i + 8, :]
        for z in range(2):
            start = 8 * (2 * i + z)
            load_ref[i, 1 + z] = below_ref[start : start + 8, :]
            load_ref[i, 3 + z] = near_ref[start : start + 8, :]
            load_ref[i, 5 + z] = above_ref[start : start + 8, :]
    edge_ref[0:8, :] = far_below_ref[64:72, :]
    edge_ref[8:16, :] = far_above_ref[64:72, :]
    sources = (
        (far_below_ref, 72), (below_ref, 128), (near_ref, 128), (above_ref, 128), (far_above_ref, 72),
    )
    for index, (source, start) in enumerate(sources):
        for m in range(3):
            row = ROWS * m + 2 * index
            rows_ref[row : row + 2, :] = source[start + 2 * m : start + 2 * m + 2, :]
    rows_ref[30:32, :] = jnp.zeros((2, 128), F32)
    rows = rows_ref[...]
    for face, ref in ((0, low_ref), (7, high_ref)):
        for c in range(8):
            ref[8 * c : 8 * c + 8, :] = load_ref[face, c]
        ref[64:65, :] = far_below_ref[64 + face : 65 + face, :]
        ref[65:66, :] = far_above_ref[64 + face : 65 + face, :]
        ref[66:72, :] = jnp.zeros((6, 128), F32)
        ref[FACE_METRIC:FACE_ROWS, :] = rows


def send_along_z(field, extra, send_ref):
    here = lax.axis_index("gz")
    above = lax.rem(here + 1, N_GZ)
    for i in range(8):
        for chunk in range(N_GZ):
            send_ref[chunk, i : i + 1, :] = jnp.where(
                above == chunk, field[i][1][7:8, :], field[i][0][0:1, :]
            )
    for chunk in range(N_GZ):
        send_ref[chunk, 8:16, :] = extra


def send_along_x(field, extra, send_ref):
    here = lax.axis_index("gx")
    above = lax.rem(here + 1, N_GX)
    for chunk in range(N_GX):
        for z in range(2):
            send_ref[chunk, 8 * z : 8 * z + 8, :] = jnp.where(
                above == chunk, field[7][z], field[0][z]
            )
        send_ref[chunk, 16:24, :] = extra


def two_rows(first, second):
    node = lax.broadcasted_iota(jnp.int32, (8, 128), 0)
    return jnp.where(node == 0, spread(first), jnp.where(node == 1, spread(second), 0.0))


def begin(
    load_ref, edge_ref, rows_ref, left_ref, right_ref, factor_ref, table_ref,
    rhs_ref, inverse_ref, smooth_ref, applied_ref, low_ref, high_ref, send_ref,
):
    def edge(which):
        start = 8 * which

        def row(i):
            value = edge_ref[start + i : start + i + 1, :]
            if i == 0:
                value = value + left_ref[64 + which : 65 + which, :]
            if i == 7:
                value = value + right_ref[64 + which : 65 + which, :]
            return value

        return row

    load = sum_x(read(load_ref, 0, 8), faces(left_ref, 8), faces(right_ref, 8))
    rhs = each(wall, sum_y(sum_z(load, edge(0), edge(1))))
    columns = [
        diagonal_sum_x(rows_ref, left_ref, right_ref, column, table_ref) for column in range(-4, 6)
    ]
    diagonal = sum_z([[columns[c][i] for c in range(10)] for i in range(8)])
    inverse = each(lambda d: wall(1.0 / d), sum_y(diagonal))
    smooth = each(lambda d, r: d * r / THETA, inverse, rhs)
    write(rhs_ref, [row[1:7] for row in rhs])
    write(inverse_ref, [row[1:7] for row in inverse])
    write(smooth_ref, [row[1:7] for row in smooth])
    applied = element_apply(smooth, -3, rows_ref, table_ref)
    write(applied_ref, applied)
    write_x_faces(applied, low_ref, high_ref)

    mult = table(table_ref, "mult")
    weighted = [[rhs[i][3 + z] * (mult * float(EDGE[i])) for z in range(2)] for i in range(8)]
    parts = []
    for a in range(2):
        along_x = []
        for z in range(2):
            total = float(ALONG_X[a, 0]) * weighted[0][z]
            for i in range(1, 8):
                total = total + float(ALONG_X[a, i]) * weighted[i][z]
            along_x.append(total)
        for b in range(2):
            both = (
                table(table_ref, f"bz{b}0") * along_x[0] + table(table_ref, f"bz{b}1") * along_x[1]
            )
            parts.append(jnp.sum(both, axis=0, keepdims=True))
    node = lax.broadcasted_iota(jnp.int32, (8, 128), 0)
    stacked = jnp.zeros((8, 128), F32)
    for index, part in enumerate(parts):
        stacked = jnp.where(node == index, spread(part), stacked)
    modes = lax.dot_general(
        stacked, table(table_ref, "modes"), (((1,), (1,)), ((), ())),
        precision=HIGHEST, preferred_element_type=F32,
    )
    owner = lax.broadcasted_iota(jnp.int32, (8, 32), 1) // 8
    row = lax.broadcasted_iota(jnp.int32, (8, 32), 0)
    coarse_rhs = jnp.sum(jnp.where(owner == row, modes, 0.0), axis=0, keepdims=True)
    own = jnp.dot(
        jnp.broadcast_to(coarse_rhs, (8, 32)), factor_ref[...],
        precision=HIGHEST, preferred_element_type=F32,
    )
    for chunk in range(N_GZ):
        send_ref[chunk, 0:1, :] = own[0:1, 0:128]
        send_ref[chunk, 1:2, :] = own[0:1, 128:256]


def level_of_lane(first):
    return first + lax.broadcasted_iota(jnp.int32, (1, 128), 1) // 16


def tree_sum(rows_of, count, here, shift):
    total = jnp.zeros((1, 128), F32)
    mine = lax.shift_right_logical(jnp.full((1, 128), here, jnp.int32), shift)
    for e in range(count):
        other = lax.shift_right_logical(jnp.full((1, 128), e, jnp.int32), shift)
        total = total + jnp.where(other == mine, rows_of(e), 0.0)
    return total


def neighbours(axis, count):
    here = lax.axis_index(axis)
    return lax.rem(here + count - 1, count), lax.rem(here + 1, count)


def lower_tree(received_ref, send_ref):
    here = lax.axis_index("gz")
    for row in range(2):
        total = tree_sum(
            lambda e: received_ref[e, row : row + 1, :], N_GZ, here, level_of_lane(8 * row)
        )
        for chunk in range(N_GX):
            send_ref[chunk, row : row + 1, :] = total


def middle(applied_ref, received_ref, summed_ref, send_ref):
    below, above = neighbours("gz", N_GZ)
    field = sum_z(
        read(applied_ref),
        lambda i: received_ref[below, i : i + 1, :],
        lambda i: received_ref[above, i : i + 1, :],
    )
    write(summed_ref, field)
    extra = received_ref[0, 8:16, :]
    for e in range(1, N_GZ):
        extra = extra + received_ref[e, 8:16, :]
    send_along_x(field, extra, send_ref)


def x_faces_received(received_ref):
    below, above = neighbours("gx", N_GX)
    left = [received_ref[below, 8 * z : 8 * z + 8, :] for z in range(2)]
    right = [received_ref[above, 8 * z : 8 * z + 8, :] for z in range(2)]
    return left, right


def relax(step, count, applied_ref, left_ref, right_ref, rhs_ref, inverse_ref, smooth_ref, update_ref):
    field = sum_x(
        read(applied_ref, 0, count + 2), faces(left_ref, count + 2), faces(right_ref, count + 2)
    )
    image = each(wall, sum_y(sum_z(field)))
    first, second = STEPS[step]
    inset = (6 - count) // 2
    shift = 1 if step else 0
    update = each(
        lambda u, d, r, a: first * u + (second * d) * (r - a),
        read(update_ref, shift, count), read(inverse_ref, inset, count), read(rhs_ref, inset, count),
        image,
    )
    return each(lambda s, u: s + u, read(smooth_ref, shift, count), update), update


def sweep(
    applied_ref, left_ref, right_ref, rhs_ref, inverse_ref, smooth_ref, update_ref, rows_ref, table_ref,
    next_ref, next_update_ref, out_ref, low_ref, high_ref, *, step, count,
):
    smooth, update = relax(
        step, count, applied_ref, left_ref, right_ref, rhs_ref, inverse_ref, smooth_ref, update_ref
    )
    write(next_ref, smooth)
    write(next_update_ref, update)
    applied = element_apply(smooth, 1 - count // 2, rows_ref, table_ref)
    write(out_ref, applied)
    write_x_faces(applied, low_ref, high_ref)


def coarse_field(received_ref, factor_ref, table_ref):
    here = lax.axis_index("gx")
    first = tree_sum(
        lambda e: received_ref[e, 0:1, :], N_GX, here, jnp.maximum(level_of_lane(0) - 4, 0)
    )
    second = tree_sum(lambda e: received_ref[e, 1:2, :], N_GX, here, level_of_lane(8) - 4)
    columns = jnp.broadcast_to(jnp.concatenate([first, second], axis=1), (8, 256))
    coarse = lax.dot_general(
        columns, factor_ref[...], (((1,), (1,)), ((), ())),
        precision=HIGHEST, preferred_element_type=F32,
    )
    owner = lax.broadcasted_iota(jnp.int32, (8, 32), 1) // 8
    row = lax.broadcasted_iota(jnp.int32, (8, 32), 0)
    across = jnp.dot(
        jnp.where(owner == row, coarse, 0.0), table(table_ref, "modes"),
        precision=HIGHEST, preferred_element_type=F32,
    )
    out = [[None, None] for i in range(8)]
    for z in range(2):
        along_z = []
        for a in range(2):
            along_z.append(
                table(table_ref, f"bz0{z}") * spread(across[2 * a : 2 * a + 1, :])
                + table(table_ref, f"bz1{z}") * spread(across[2 * a + 1 : 2 * a + 2, :])
            )
        for i in range(8):
            out[i][z] = wall(float(ALONG_X[0, i]) * along_z[0] + float(ALONG_X[1, i]) * along_z[1])
    return out


def last_sweep(
    applied_ref, left_ref, right_ref, rhs_ref, inverse_ref, smooth_ref, update_ref, rows_ref,
    tree_ref, factor_ref, near_ref, table_ref,
    precond_ref, out_ref, send_ref,
):
    smooth, update = relax(
        2, 2, applied_ref, left_ref, right_ref, rhs_ref, inverse_ref, smooth_ref, update_ref
    )
    coarse = coarse_field(tree_ref, factor_ref, table_ref)
    precond = each(lambda s, c: s + c, smooth, coarse)
    write(precond_ref, precond)
    applied = element_apply(precond, 0, rows_ref, table_ref)
    write(out_ref, applied)
    first = jnp.zeros((8, 128), F32)
    second = jnp.zeros((8, 128), F32)
    for i in range(8):
        for z in range(2):
            start = 8 * (2 * i + z)
            first = first + near_ref[start : start + 8, :] * precond[i][z]
            second = second + applied[i][z] * precond[i][z]
    extra = two_rows(jnp.sum(first, axis=0, keepdims=True), jnp.sum(second, axis=0, keepdims=True))
    send_along_z(applied, extra, send_ref)


def finish(summed_ref, received_ref, precond_ref, rhs_ref, solution_ref, residual_ref):
    left, right = x_faces_received(received_ref)
    image = each(wall, sum_y(sum_x(read(summed_ref), left, right)))
    extra = received_ref[0, 16:24, :]
    for e in range(1, N_GX):
        extra = extra + received_ref[e, 16:24, :]
    totals = jnp.sum(extra, axis=1, keepdims=True)
    alpha = spread(totals[0:1, :] / totals[1:2, :])
    write(solution_ref, each(lambda p: alpha * p, read(precond_ref)))
    write(residual_ref, each(lambda r, a: r - alpha * a, read(rhs_ref, 2, 2), image))


def field_shape(count):
    return (8, count, 8, 128)


def run(kernel, shapes, *operands, last=False):
    spec = pl.BlockSpec(memory_space=pltpu.VMEM)
    outs = [
        jax.ShapeDtypeStruct(shape, F32) if last else pltpu.VMEM(shape, F32) for shape in shapes
    ]
    operands = [pltpu.with_memory_space_constraint(value, pltpu.VMEM) for value in operands]
    return pl.pallas_call(
        kernel, out_shape=outs, in_specs=[spec] * len(operands), out_specs=[spec] * len(outs)
    )(*operands)


def shifted(value, axis, distance):
    count = lax.axis_size(axis)
    return lax.ppermute(value, axis, [(i, (i + distance) % count) for i in range(count)])


def exchange(low, high, axis):
    return shifted(high, axis, 1), shifted(low, axis, -1)


def per_device(element_rhs_load, metric, coarse_factor):
    load = element_rhs_load.reshape(field_shape(2))
    constants = jnp.asarray(TABLE)
    factor = coarse_factor.reshape(10, 32, 16).transpose(1, 0, 2).reshape(32, 160)
    factor = jnp.pad(factor, ((0, 0), (0, 96)))
    near, up, down = run(
        pack, [(136, 128), (80, 128), (80, 128)], load, metric.reshape(6, 16), constants
    )
    below, far_below = shifted(near, "gz", 1), shifted(up, "gz", 2)
    above, far_above = shifted(near, "gz", -1), shifted(down, "gz", -2)
    wide, edge, rows, low, high = run(
        gather, [field_shape(8), (16, 128), (32, 128)] + [(FACE_ROWS, 128)] * 2,
        near, below, far_below, above, far_above,
    )
    left, right = exchange(low, high, "gx")
    rhs, inverse, smooth, applied, low, high, send = run(
        begin, [field_shape(6)] * 3 + [field_shape(8)] + [(64, 128)] * 2 + [(N_GZ, 2, 128)],
        wide, edge, rows, left, right, factor, constants,
    )
    tree = lax.all_to_all(send, "gz", 0, 0, tiled=True)
    left, right = exchange(low, high, "gx")
    update = smooth
    for step, count in ((0, 6), (1, 4)):

        def stage(*refs, step=step, count=count):
            sweep(*refs, step=step, count=count)

        smooth, update, applied, low, high = run(
            stage, [field_shape(count)] * 3 + [(8 * count, 128)] * 2,
            applied, left, right, rhs, inverse, smooth, update, rows, constants,
        )
        left, right = exchange(low, high, "gx")
        if step == 0:
            (send,) = run(lower_tree, [(N_GX, 2, 128)], tree)
            tree = lax.all_to_all(send, "gx", 0, 0, tiled=True)
    precond, applied, send = run(
        last_sweep, [field_shape(2)] * 2 + [(N_GZ, 16, 128)],
        applied, left, right, rhs, inverse, smooth, update, rows, tree, factor, near, constants,
    )
    received = lax.all_to_all(send, "gz", 0, 0, tiled=True)
    summed, send = run(middle, [field_shape(2), (N_GX, 24, 128)], applied, received)
    received = lax.all_to_all(send, "gx", 0, 0, tiled=True)
    solution_field, residual = run(
        finish, [field_shape(2)] * 2, summed, received, precond, rhs, last=True
    )
    shape = element_rhs_load.shape
    return solution_field.reshape(shape), residual.reshape(shape)


def solution(mesh):
    placed = (
        P("gx", None, "gz", None, None),
        P(None, "gx", "gz", None),
        P("gx", "gz", None, None, None),
    )
    return jax.shard_map(
        per_device,
        mesh=mesh,
        in_specs=placed,
        out_specs=(P("gx", None, "gz", None, None), P("gx", None, "gz", None, None)),
        check_vma=False,
    )
```

time: 143 us -> 129 us (0.902)
  blocking collectives: 81.5 us -> 43.3 us
  starting transfers between devices: 47.5 us -> 67.4 us
  Pallas kernels: 2.89 us -> 5.22 us
  waiting for transfers between devices: 7.36 us -> 9.08 us
    all_to_all x2 -> x1, blocking collectives: 42.9 us -> 19.8 us  [per_device(): received = lax.all_to_all(send, 'gx', 0, 0, tiled=True)]
    all_to_all x0 -> x2, starting transfers between devices: none -> 18.1 us  [the longest x1 9.53 us: per_device(): tree = lax.all_to_all(send, 'gz', 0, 0, tiled=True)]
    all_to_all x2 -> x1, blocking collectives: 38.6 us -> 23.5 us  [per_device(): received = lax.all_to_all(send, 'gz', 0, 0, tiled=True)]
    pallas_call x11 -> x9, Pallas kernels: 2.89 us -> 5.22 us  [run(): pl.pallas_call(kernel, out_shape=outs, in_specs=[spec] * len(operands), o...]
    ppermute x12, starting transfers between devices: 47.5 us -> 49.3 us  [shifted(): lax.ppermute(value, axis, [(i, (i + distance) % count) for i in range(cou...]
    ppermute x12, waiting for transfers between devices: 7.36 us -> 9.08 us  [shifted(): lax.ppermute(value, axis, [(i, (i + distance) % count) for i in range(cou...]
  transfers between devices with their start and end apart: 12 -> 14, of which waited for: 6 -> 4; matrix products, arithmetic and copies ran while one was open for 0% -> 0% of each run, Pallas kernels for 0% -> 1%
where the time goes in v2:
time: 129 us; the launch traced here: 128 us
  starting transfers between devices  67.4 us (52%)
  blocking collectives  43.3 us (34%)
  waiting for transfers between devices  9.08 us (7%)
  Pallas kernels  5.22 us (4%)
  local copies, waits for them, and re-layouts  2.53 us (2%)
    ppermute x12, starting transfers between devices, shifted(): lax.ppermute(value, axis, [(i, (i + distance) % count) for i in range(cou...  49.3 us
    all_to_all x1, blocking collectives, per_device(): received = lax.all_to_all(send, 'gz', 0, 0, tiled=True)  23.5 us
    all_to_all x1, blocking collectives, per_device(): received = lax.all_to_all(send, 'gx', 0, 0, tiled=True)  19.8 us
    all_to_all x1, starting transfers between devices, per_device(): tree = lax.all_to_all(send, 'gz', 0, 0, tiled=True)  9.53 us
    ppermute x12, waiting for transfers between devices, shifted(): lax.ppermute(value, axis, [(i, (i + distance) % count) for i in range(cou...  9.08 us
    all_to_all x1, starting transfers between devices, per_device(): tree = lax.all_to_all(send, 'gx', 0, 0, tiled=True)  8.57 us
    pallas_call x9, Pallas kernels, run(): pl.pallas_call(kernel, out_shape=outs, in_specs=[spec] * len(operands), o...  5.22 us
  transfers between devices with their start and end apart: 14, of which 4 were waited for; matrix products, arithmetic and copies ran while one was open for 0% of the time, Pallas kernels for 1%

profile of v2, /device:TPU:1, one launch (start us, length us, event | category | flops | bytes accessed | tf_op | source)
XLA Modules:
  0.0 128.4 jit_solution(17672456481694042974)
XLA Ops:
  0.6 0.7 reshape.23.metric_ref
  1.3 0.0 copy-start
  1.3 0.9 copy-done
  2.2 0.0 copy-start.2
  2.2 0.8 copy-done.2
  3.1 0.1 shard_map.59
  3.2 4.4 %collective-permute-start = (f32[136,128]{1,0:T(8,128)S(1)}, f32[136,128]{1,0:T(8,128)S(1)}, u32[]{:S(2)}, u32[]{:S(2)}) collective-permute-start(f32[136,128]{1,0:T(8,128)S(1)} %get-tuple-element.34.near_ref), channel_id=1, source_target_pairs={{0,1},{1,2},{2,3},{3,4},{4,5},{5,6},{6,7},{7,8},{8,9},{9,10},{10,1... | collective-permute-start | bytes 208904 | tf_op jit(solution)/shard_map/ppermute | solution.py:568
  7.6 9.5 %collective-permute-start.2 = (f32[136,128]{1,0:T(8,128)S(1)}, f32[136,128]{1,0:T(8,128)S(1)}, u32[]{:S(2)}, u32[]{:S(2)}) collective-permute-start(f32[136,128]{1,0:T(8,128)S(1)} %get-tuple-element.34.near_ref), channel_id=1, source_target_pairs={{0,15},{1,0},{2,1},{3,2},{4,3},{5,4},{6,5},{7,6},{8,7},{9,8},{10,9... | collective-permute-start | bytes 208904 | tf_op jit(solution)/shard_map/ppermute | solution.py:568
  17.1 1.9 %collective-permute-start.1 = (f32[80,128]{1,0:T(8,128)S(1)}, f32[80,128]{1,0:T(8,128)S(1)}, u32[]{:S(2)}, u32[]{:S(2)}) collective-permute-start(f32[80,128]{1,0:T(8,128)S(1)} %get-tuple-element.35), channel_id=1, source_target_pairs={{0,2},{1,3},{2,4},{3,5},{4,6},{5,7},{6,8},{7,9},{8,10},{9,11},{10,... | collective-permute-start | bytes 122888 | tf_op jit(solution)/shard_map/ppermute | solution.py:568
  19.0 0.0 copy-start.3
  19.0 5.6 %collective-permute-start.3 = (f32[80,128]{1,0:T(8,128)S(1)}, f32[80,128]{1,0:T(8,128)S(1)}, u32[]{:S(2)}, u32[]{:S(2)}) collective-permute-start(f32[80,128]{1,0:T(8,128)S(1)} %get-tuple-element.36), channel_id=1, source_target_pairs={{0,14},{1,15},{2,0},{3,1},{4,2},{5,3},{6,4},{7,5},{8,6},{9,7},{10,... | collective-permute-start | bytes 122888 | tf_op jit(solution)/shard_map/ppermute | solution.py:568
  24.6 0.0 collective-permute-done.1.far_below_ref
  24.6 1.1 collective-permute-done.3.far_above_ref
  25.7 0.0 collective-permute-done.below_ref
  25.7 0.0 collective-permute-done.2.above_ref
  25.8 0.0 copy-start.1
  25.8 5.3 %collective-permute-start.4 = (f32[104,128]{1,0:T(8,128)S(1)}, f32[104,128]{1,0:T(8,128)S(1)}, u32[]{:S(2)}, u32[]{:S(2)}) collective-permute-start(f32[104,128]{1,0:T(8,128)S(1)} %get-tuple-element.40), channel_id=1, source_target_pairs={{0,16},{16,32},{32,48},{48,64},{64,80},{80,96},{96,112},{112,128},... | collective-permute-start | bytes 159752 | tf_op jit(solution)/shard_map/ppermute | solution.py:568
  31.1 1.9 %collective-permute-start.5 = (f32[104,128]{1,0:T(8,128)S(1)}, f32[104,128]{1,0:T(8,128)S(1)}, u32[]{:S(2)}, u32[]{:S(2)}) collective-permute-start(f32[104,128]{1,0:T(8,128)S(1)} %get-tuple-element.41), channel_id=1, source_target_pairs={{0,496},{16,0},{32,16},{48,32},{64,48},{80,64},{96,80},{112,96},{1... | collective-permute-start | bytes 159752 | tf_op jit(solution)/shard_map/ppermute | solution.py:568
  33.0 0.0 copy-done.3
  33.0 0.1 copy.7
  33.1 0.0 collective-permute-done.4.left_ref
  33.1 3.4 %collective-permute-done.5.right_ref = f32[104,128]{1,0:T(8,128)S(1)} collective-permute-done((f32[104,128]{1,0:T(8,128)S(1)}, f32[104,128]{1,0:T(8,128)S(1)}, u32[]{:S(2)}, u32[]{:S(2)}) %collective-permute-start.5) | collective-permute-done | bytes 53280 | tf_op jit(solution)/shard_map/ppermute | solution.py:568
  36.5 0.0 copy-done.1
  36.5 1.6 %shard_map.61 = (f32[8,6,8,128]{3,2,1,0:T(8,128)S(1)}, f32[8,6,8,128]{3,2,1,0:T(8,128)S(1)}, f32[8,6,8,128]{3,2,1,0:T(8,128)S(1)}, f32[8,8,8,128]{3,2,1,0:T(8,12...) custom-call(f32[8,8,8,128]{3,2,1,0:T(8,128)S(1)} %get-tuple-element.37.load_ref, ...), custom_call_target="tpu_custom_call" | custom-call | tf_op jit(solution)/shard_map/pallas_call | solution.py:561
  38.2 9.5 %all-to-all-start = ((f32[16,2,128]{2,1,0:T(2,128)}), f32[16,2,128]{2,1,0:T(2,128)S(1)}, u32[]{:S(2)}, u32[]{:S(2)}) async-start(f32[16,2,128]{2,1,0:T(2,128)} %get-tuple-element.58), calls=%async_computation | async-start | bytes 32768 | tf_op jit(solution)/shard_map/all_to_all | solution.py:594
  47.7 2.2 %collective-permute-start.6 = (f32[64,128]{1,0:T(8,128)S(1)}, f32[64,128]{1,0:T(8,128)S(1)}, u32[]{:S(2)}, u32[]{:S(2)}) collective-permute-start(f32[64,128]{1,0:T(8,128)S(1)} %get-tuple-element.43), channel_id=1, source_target_pairs={{0,16},{16,32},{32,48},{48,64},{64,80},{80,96},{96,112},{112,128},... | collective-permute-start | bytes 98312 | tf_op jit(solution)/shard_map/ppermute | solution.py:568
  49.9 4.1 %collective-permute-start.7 = (f32[64,128]{1,0:T(8,128)S(1)}, f32[64,128]{1,0:T(8,128)S(1)}, u32[]{:S(2)}, u32[]{:S(2)}) collective-permute-start(f32[64,128]{1,0:T(8,128)S(1)} %get-tuple-element.44), channel_id=1, source_target_pairs={{0,496},{16,0},{32,16},{48,32},{64,48},{80,64},{96,80},{112,96},{1... | collective-permute-start | bytes 98312 | tf_op jit(solution)/shard_map/ppermute | solution.py:568
  54.0 0.0 collective-permute-done.6.refs_1_
  54.0 1.4 %collective-permute-done.7.refs_2_ = f32[64,128]{1,0:T(8,128)S(1)} collective-permute-done((f32[64,128]{1,0:T(8,128)S(1)}, f32[64,128]{1,0:T(8,128)S(1)}, u32[]{:S(2)}, u32[]{:S(2)}) %collective-permute-start.7) | collective-permute-done | bytes 32800 | tf_op jit(solution)/shard_map/ppermute | solution.py:568
  55.4 0.7 shard_map.62
  56.1 1.9 %collective-permute-start.8 = (f32[48,128]{1,0:T(8,128)S(1)}, f32[48,128]{1,0:T(8,128)S(1)}, u32[]{:S(2)}, u32[]{:S(2)}) collective-permute-start(f32[48,128]{1,0:T(8,128)S(1)} %get-tuple-element.49), channel_id=1, source_target_pairs={{0,16},{16,32},{32,48},{48,64},{64,80},{80,96},{96,112},{112,128},... | collective-permute-start | bytes 73736 | tf_op jit(solution)/shard_map/ppermute | solution.py:568
  58.1 7.1 %collective-permute-start.9 = (f32[48,128]{1,0:T(8,128)S(1)}, f32[48,128]{1,0:T(8,128)S(1)}, u32[]{:S(2)}, u32[]{:S(2)}) collective-permute-start(f32[48,128]{1,0:T(8,128)S(1)} %get-tuple-element.50), channel_id=1, source_target_pairs={{0,496},{16,0},{32,16},{48,32},{64,48},{80,64},{96,80},{112,96},{1... | collective-permute-start | bytes 73736 | tf_op jit(solution)/shard_map/ppermute | solution.py:568
  65.1 0.0 all-to-all-done.received_ref
  65.1 0.7 shard_map.64
  65.8 8.6 %all-to-all-start.1 = ((f32[32,2,128]{2,1,0:T(2,128)}), f32[32,2,128]{2,1,0:T(2,128)S(1)}, u32[]{:S(2)}, u32[]{:S(2)}) async-start(f32[32,2,128]{2,1,0:T(2,128)} %shard_map.64), calls=%async_computation.1 | async-start | bytes 65536 | tf_op jit(solution)/shard_map/all_to_all | solution.py:609
  74.4 0.0 collective-permute-done.8.refs_1_
  74.4 0.0 collective-permute-done.9.refs_2_
  74.4 0.5 shard_map.63
  74.9 3.5 %collective-permute-start.10 = (f32[32,128]{1,0:T(8,128)S(1)}, f32[32,128]{1,0:T(8,128)S(1)}, u32[]{:S(2)}, u32[]{:S(2)}) collective-permute-start(f32[32,128]{1,0:T(8,128)S(1)} %get-tuple-element.54), channel_id=1, source_target_pairs={{0,16},{16,32},{32,48},{48,64},{64,80},{80,96},{96,112},{112,128},... | collective-permute-start | bytes 49160 | tf_op jit(solution)/shard_map/ppermute | solution.py:568
  78.5 1.9 %collective-permute-start.11 = (f32[32,128]{1,0:T(8,128)S(1)}, f32[32,128]{1,0:T(8,128)S(1)}, u32[]{:S(2)}, u32[]{:S(2)}) collective-permute-start(f32[32,128]{1,0:T(8,128)S(1)} %get-tuple-element.55), channel_id=1, source_target_pairs={{0,496},{16,0},{32,16},{48,32},{64,48},{80,64},{96,80},{112,96},{1... | collective-permute-start | bytes 49160 | tf_op jit(solution)/shard_map/ppermute | solution.py:568
  80.4 0.0 collective-permute-done.10.left_ref
  80.4 3.1 %collective-permute-done.11.right_ref = f32[32,128]{1,0:T(8,128)S(1)} collective-permute-done((f32[32,128]{1,0:T(8,128)S(1)}, f32[32,128]{1,0:T(8,128)S(1)}, u32[]{:S(2)}, u32[]{:S(2)}) %collective-permute-start.11) | collective-permute-done | bytes 16416 | tf_op jit(solution)/shard_map/ppermute | solution.py:568
  83.5 0.0 all-to-all-done.1.tree_ref
  83.6 0.7 shard_map.65
  84.2 23.5 %all_to_all.20.received_ref = f32[16,16,128]{2,1,0:T(8,128)S(1)} all-to-all(f32[16,16,128]{2,1,0:T(8,128)S(1)} %get-tuple-element.60), channel_id=1, replica_groups=mesh['gx'=32,'gz'=16] {'gz'}, dimensions={0} | all-to-all | bytes 262144 | tf_op jit(solution)/shard_map/all_to_all | solution.py:614
  107.8 19.8 %all_to_all.21.received_ref = f32[32,24,128]{2,1,0:T(8,128)S(1)} all-to-all(f32[32,24,128]{2,1,0:T(8,128)S(1)} %get-tuple-element.62), channel_id=1, replica_groups=mesh['gx'=32,'gz'=16] {'gx'}, dimensions={0} | all-to-all | bytes 786432 | tf_op jit(solution)/shard_map/all_to_all | solution.py:616
  127.6 0.8 shard_map.67
  (3 shorter events, 0.1 us)
Async XLA Ops:
  1.3 0.9 copy-start
  2.2 0.8 copy-start.2
  3.2 22.5 %collective-permute-start = (f32[136,128]{1,0:T(8,128)S(1)}, f32[136,128]{1,0:T(8,128)S(1)}, u32[]{:S(2)}, u32[]{:S(2)}) collective-permute-start(f32[136,128]{1,0:T(8,128)S(1)} %get-tuple-element.34.near_ref), channel_id=1, source_target_pairs={{0,1},{1,2},{2,3},{3,4},{4,5},{5,6},{6,7},{7,8},{8,9},{9,10},{10,1... | collective-permute-start | bytes 208904 | tf_op jit(solution)/shard_map/ppermute | solution.py:568
  7.6 18.1 %collective-permute-start.2 = (f32[136,128]{1,0:T(8,128)S(1)}, f32[136,128]{1,0:T(8,128)S(1)}, u32[]{:S(2)}, u32[]{:S(2)}) collective-permute-start(f32[136,128]{1,0:T(8,128)S(1)} %get-tuple-element.34.near_ref), channel_id=1, source_target_pairs={{0,15},{1,0},{2,1},{3,2},{4,3},{5,4},{6,5},{7,6},{8,7},{9,8},{10,9... | collective-permute-start | bytes 208904 | tf_op jit(solution)/shard_map/ppermute | solution.py:568
  17.1 7.6 %collective-permute-start.1 = (f32[80,128]{1,0:T(8,128)S(1)}, f32[80,128]{1,0:T(8,128)S(1)}, u32[]{:S(2)}, u32[]{:S(2)}) collective-permute-start(f32[80,128]{1,0:T(8,128)S(1)} %get-tuple-element.35), channel_id=1, source_target_pairs={{0,2},{1,3},{2,4},{3,5},{4,6},{5,7},{6,8},{7,9},{8,10},{9,11},{10,... | collective-permute-start | bytes 122888 | tf_op jit(solution)/shard_map/ppermute | solution.py:568
  19.0 14.0 %copy-start.3 = (f32[1,1,10,32,16]{3,4,2,1,0:T(8,128)S(1)}, f32[1,1,10,32,16]{3,4,2,1,0:T(8,128)}, u32[]{:S(2)}) copy-start(f32[1,1,10,32,16]{3,4,2,1,0:T(8,128)} %param.6) | copy-start | bytes 61444
  19.0 6.7 %collective-permute-start.3 = (f32[80,128]{1,0:T(8,128)S(1)}, f32[80,128]{1,0:T(8,128)S(1)}, u32[]{:S(2)}, u32[]{:S(2)}) collective-permute-start(f32[80,128]{1,0:T(8,128)S(1)} %get-tuple-element.36), channel_id=1, source_target_pairs={{0,14},{1,15},{2,0},{3,1},{4,2},{5,3},{6,4},{7,5},{8,6},{9,7},{10,... | collective-permute-start | bytes 122888 | tf_op jit(solution)/shard_map/ppermute | solution.py:568
  25.8 10.8 %copy-start.1 = (f32[256,128]{1,0:T(8,128)S(1)}, f32[256,128]{1,0:T(8,128)}, u32[]{:S(2)}) copy-start(f32[256,128]{1,0:T(8,128)} %constant.5.clone.table_ref.refs_8_) | copy-start | bytes 393220
  25.8 7.3 %collective-permute-start.4 = (f32[104,128]{1,0:T(8,128)S(1)}, f32[104,128]{1,0:T(8,128)S(1)}, u32[]{:S(2)}, u32[]{:S(2)}) collective-permute-start(f32[104,128]{1,0:T(8,128)S(1)} %get-tuple-element.40), channel_id=1, source_target_pairs={{0,16},{16,32},{32,48},{48,64},{64,80},{80,96},{96,112},{112,128},... | collective-permute-start | bytes 159752 | tf_op jit(solution)/shard_map/ppermute | solution.py:568
  31.1 5.5 %collective-permute-start.5 = (f32[104,128]{1,0:T(8,128)S(1)}, f32[104,128]{1,0:T(8,128)S(1)}, u32[]{:S(2)}, u32[]{:S(2)}) collective-permute-start(f32[104,128]{1,0:T(8,128)S(1)} %get-tuple-element.41), channel_id=1, source_target_pairs={{0,496},{16,0},{32,16},{48,32},{64,48},{80,64},{96,80},{112,96},{1... | collective-permute-start | bytes 159752 | tf_op jit(solution)/shard_map/ppermute | solution.py:568
  38.2 26.9 %all-to-all-start = ((f32[16,2,128]{2,1,0:T(2,128)}), f32[16,2,128]{2,1,0:T(2,128)S(1)}, u32[]{:S(2)}, u32[]{:S(2)}) async-start(f32[16,2,128]{2,1,0:T(2,128)} %get-tuple-element.58), calls=%async_computation | async-start | bytes 32768 | tf_op jit(solution)/shard_map/all_to_all | solution.py:594
  47.7 6.2 %collective-permute-start.6 = (f32[64,128]{1,0:T(8,128)S(1)}, f32[64,128]{1,0:T(8,128)S(1)}, u32[]{:S(2)}, u32[]{:S(2)}) collective-permute-start(f32[64,128]{1,0:T(8,128)S(1)} %get-tuple-element.43), channel_id=1, source_target_pairs={{0,16},{16,32},{32,48},{48,64},{64,80},{80,96},{96,112},{112,128},... | collective-permute-start | bytes 98312 | tf_op jit(solution)/shard_map/ppermute | solution.py:568
  49.9 5.5 %collective-permute-start.7 = (f32[64,128]{1,0:T(8,128)S(1)}, f32[64,128]{1,0:T(8,128)S(1)}, u32[]{:S(2)}, u32[]{:S(2)}) collective-permute-start(f32[64,128]{1,0:T(8,128)S(1)} %get-tuple-element.44), channel_id=1, source_target_pairs={{0,496},{16,0},{32,16},{48,32},{64,48},{80,64},{96,80},{112,96},{1... | collective-permute-start | bytes 98312 | tf_op jit(solution)/shard_map/ppermute | solution.py:568
  56.1 18.3 %collective-permute-start.8 = (f32[48,128]{1,0:T(8,128)S(1)}, f32[48,128]{1,0:T(8,128)S(1)}, u32[]{:S(2)}, u32[]{:S(2)}) collective-permute-start(f32[48,128]{1,0:T(8,128)S(1)} %get-tuple-element.49), channel_id=1, source_target_pairs={{0,16},{16,32},{32,48},{48,64},{64,80},{80,96},{96,112},{112,128},... | collective-permute-start | bytes 73736 | tf_op jit(solution)/shard_map/ppermute | solution.py:568
  58.1 16.3 %collective-permute-start.9 = (f32[48,128]{1,0:T(8,128)S(1)}, f32[48,128]{1,0:T(8,128)S(1)}, u32[]{:S(2)}, u32[]{:S(2)}) collective-permute-start(f32[48,128]{1,0:T(8,128)S(1)} %get-tuple-element.50), channel_id=1, source_target_pairs={{0,496},{16,0},{32,16},{48,32},{64,48},{80,64},{96,80},{112,96},{1... | collective-permute-start | bytes 73736 | tf_op jit(solution)/shard_map/ppermute | solution.py:568
  65.8 17.7 %all-to-all-start.1 = ((f32[32,2,128]{2,1,0:T(2,128)}), f32[32,2,128]{2,1,0:T(2,128)S(1)}, u32[]{:S(2)}, u32[]{:S(2)}) async-start(f32[32,2,128]{2,1,0:T(2,128)} %shard_map.64), calls=%async_computation.1 | async-start | bytes 65536 | tf_op jit(solution)/shard_map/all_to_all | solution.py:609
  74.9 5.5 %collective-permute-start.10 = (f32[32,128]{1,0:T(8,128)S(1)}, f32[32,128]{1,0:T(8,128)S(1)}, u32[]{:S(2)}, u32[]{:S(2)}) collective-permute-start(f32[32,128]{1,0:T(8,128)S(1)} %get-tuple-element.54), channel_id=1, source_target_pairs={{0,16},{16,32},{32,48},{48,64},{64,80},{80,96},{96,112},{112,128},... | collective-permute-start | bytes 49160 | tf_op jit(solution)/shard_map/ppermute | solution.py:568
  78.5 5.1 %collective-permute-start.11 = (f32[32,128]{1,0:T(8,128)S(1)}, f32[32,128]{1,0:T(8,128)S(1)}, u32[]{:S(2)}, u32[]{:S(2)}) collective-permute-start(f32[32,128]{1,0:T(8,128)S(1)} %get-tuple-element.55), channel_id=1, source_target_pairs={{0,496},{16,0},{32,16},{48,32},{64,48},{80,64},{96,80},{112,96},{1... | collective-permute-start | bytes 49160 | tf_op jit(solution)/shard_map/ppermute | solution.py:568

commit v3 on v2

--- a/solution.py
+++ b/solution.py
@@ -9,6 +9,7 @@
 CHEB = 4
 N_GX = 32
 N_GZ = 16
+DEVICES = N_GX * N_GZ
 F32 = jnp.float32
 HIGHEST = lax.Precision.HIGHEST
 
@@ -87,7 +88,6 @@
         "wl": np.ones((8, 1)) * w_l,
         "wj": w_j * ones,
         "mult": EDGE[:, None] * across[None, :],
-        "expand": np.kron(np.eye(16), np.ones((1, 8))),
         "modes": np.tile(ALONG_Y, (4, 1)),
     }
     for b in range(2):
@@ -256,20 +256,25 @@
     return [ref[8 * c : 8 * c + 8, :] for c in range(count)]
 
 
-def pack(load_ref, metric_ref, table_ref, near_ref, up_ref, down_ref):
-    expanded = jnp.dot(
-        metric_ref[...], table(table_ref, "expand"), precision=HIGHEST, preferred_element_type=F32
-    )
+def pack(load_ref, metric_ref, near_ref, up_ref, down_ref):
+    element = lax.broadcasted_iota(jnp.int32, (16, 128), 0)
+    lane = lax.broadcasted_iota(jnp.int32, (16, 128), 1)
+    expand = jnp.where(element == lane // 8, 1.0, 0.0)
     for ref, start in ((near_ref, 128), (up_ref, 72), (down_ref, 72)):
-        ref[start : start + 6, :] = expanded
         ref[start + 6 : start + 8, :] = jnp.zeros((2, 128), F32)
+    for m in range(3):
+        expanded = jnp.dot(
+            metric_ref[m, 0], expand, precision=HIGHEST, preferred_element_type=F32
+        )
+        for ref, start in ((near_ref, 128), (up_ref, 72), (down_ref, 72)):
+            ref[start + 2 * m : start + 2 * m + 2, :] = expanded
     for i in range(8):
         for z in range(2):
-            near_ref[8 * (2 * i + z) : 8 * (2 * i + z) + 8, :] = load_ref[i, z]
-        up_ref[8 * i : 8 * i + 8, :] = load_ref[i, 1]
-        up_ref[64 + i : 65 + i, :] = load_ref[i, 0, 7:8, :]
-        down_ref[8 * i : 8 * i + 8, :] = load_ref[i, 0]
-        down_ref[64 + i : 65 + i, :] = load_ref[i, 1, 0:1, :]
+            near_ref[8 * (2 * i + z) : 8 * (2 * i + z) + 8, :] = load_ref[0, i, z]
+        up_ref[8 * i : 8 * i + 8, :] = load_ref[0, i, 1]
+        up_ref[64 + i : 65 + i, :] = load_ref[0, i, 0, 7:8, :]
+        down_ref[8 * i : 8 * i + 8, :] = load_ref[0, i, 0]
+        down_ref[64 + i : 65 + i, :] = load_ref[0, i, 1, 0:1, :]
 
 
 FACE_METRIC = 72
@@ -308,32 +313,10 @@
         ref[FACE_METRIC:FACE_ROWS, :] = rows
 
 
-def send_along_z(field, extra, send_ref):
-    here = lax.axis_index("gz")
-    above = lax.rem(here + 1, N_GZ)
+def write_z_faces(field, low_ref, high_ref):
     for i in range(8):
-        for chunk in range(N_GZ):
-            send_ref[chunk, i : i + 1, :] = jnp.where(
-                above == chunk, field[i][1][7:8, :], field[i][0][0:1, :]
-            )
-    for chunk in range(N_GZ):
-        send_ref[chunk, 8:16, :] = extra
-
-
-def send_along_x(field, extra, send_ref):
-    here = lax.axis_index("gx")
-    above = lax.rem(here + 1, N_GX)
-    for chunk in range(N_GX):
-        for z in range(2):
-            send_ref[chunk, 8 * z : 8 * z + 8, :] = jnp.where(
-                above == chunk, field[7][z], field[0][z]
-            )
-        send_ref[chunk, 16:24, :] = extra
-
-
-def two_rows(first, second):
-    node = lax.broadcasted_iota(jnp.int32, (8, 128), 0)
-    return jnp.where(node == 0, spread(first), jnp.where(node == 1, spread(second), 0.0))
+        low_ref[i : i + 1, :] = field[i][0][0:1, :]
+        high_ref[i : i + 1, :] = field[i][-1][7:8, :]
 
 
 def begin(
@@ -398,58 +381,27 @@
         jnp.broadcast_to(coarse_rhs, (8, 32)), factor_ref[...],
         precision=HIGHEST, preferred_element_type=F32,
     )
-    for chunk in range(N_GZ):
-        send_ref[chunk, 0:1, :] = own[0:1, 0:128]
-        send_ref[chunk, 1:2, :] = own[0:1, 128:256]
-
-
-def level_of_lane(first):
-    return first + lax.broadcasted_iota(jnp.int32, (1, 128), 1) // 16
-
-
-def tree_sum(rows_of, count, here, shift):
-    total = jnp.zeros((1, 128), F32)
-    mine = lax.shift_right_logical(jnp.full((1, 128), here, jnp.int32), shift)
-    for e in range(count):
-        other = lax.shift_right_logical(jnp.full((1, 128), e, jnp.int32), shift)
-        total = total + jnp.where(other == mine, rows_of(e), 0.0)
-    return total
-
-
-def neighbours(axis, count):
-    here = lax.axis_index(axis)
-    return lax.rem(here + count - 1, count), lax.rem(here + 1, count)
-
-
-def lower_tree(received_ref, send_ref):
-    here = lax.axis_index("gz")
-    for row in range(2):
-        total = tree_sum(
-            lambda e: received_ref[e, row : row + 1, :], N_GZ, here, level_of_lane(8 * row)
-        )
-        for chunk in range(N_GX):
-            send_ref[chunk, row : row + 1, :] = total
-
-
-def middle(applied_ref, received_ref, summed_ref, send_ref):
-    below, above = neighbours("gz", N_GZ)
-    field = sum_z(
-        read(applied_ref),
-        lambda i: received_ref[below, i : i + 1, :],
-        lambda i: received_ref[above, i : i + 1, :],
-    )
-    write(summed_ref, field)
-    extra = received_ref[0, 8:16, :]
-    for e in range(1, N_GZ):
-        extra = extra + received_ref[e, 8:16, :]
-    send_along_x(field, extra, send_ref)
-
-
-def x_faces_received(received_ref):
-    below, above = neighbours("gx", N_GX)
-    left = [received_ref[below, 8 * z : 8 * z + 8, :] for z in range(2)]
-    right = [received_ref[above, 8 * z : 8 * z + 8, :] for z in range(2)]
-    return left, right
+    node = lax.broadcasted_iota(jnp.int32, (8, 128), 0)
+    pairs = jnp.where(node % 2 == 0, spread(own[0:1, 0:128]), spread(own[0:1, 128:256]))
+    for chunk in range(0, 2 * DEVICES, 8):
+        send_ref[chunk : chunk + 8, :] = pairs
+
+
+def device():
+    return lax.axis_index("gx") * N_GZ + lax.axis_index("gz")
+
+
+def tree_sums(received_ref):
+    row = lax.broadcasted_iota(jnp.int32, (8, 128), 0)
+    level = (row % 2) * 8 + lane_iota() // 16
+    mine = lax.shift_right_logical(jnp.full((8, 128), device(), jnp.int32), level)
+    total = jnp.zeros((8, 128), F32)
+    for start in range(0, 2 * DEVICES, 8):
+        other = lax.shift_right_logical(start // 2 + row // 2, level)
+        total = total + jnp.where(other == mine, received_ref[start : start + 8, :], 0.0)
+    first = jnp.sum(jnp.where(row % 2 == 0, total, 0.0), axis=0, keepdims=True)
+    second = jnp.sum(jnp.where(row % 2 == 1, total, 0.0), axis=0, keepdims=True)
+    return first, second
 
 
 def relax(step, count, applied_ref, left_ref, right_ref, rhs_ref, inverse_ref, smooth_ref, update_ref):
@@ -483,11 +435,7 @@
 
 
 def coarse_field(received_ref, factor_ref, table_ref):
-    here = lax.axis_index("gx")
-    first = tree_sum(
-        lambda e: received_ref[e, 0:1, :], N_GX, here, jnp.maximum(level_of_lane(0) - 4, 0)
-    )
-    second = tree_sum(lambda e: received_ref[e, 1:2, :], N_GX, here, level_of_lane(8) - 4)
+    first, second = tree_sums(received_ref)
     columns = jnp.broadcast_to(jnp.concatenate([first, second], axis=1), (8, 256))
     coarse = lax.dot_general(
         columns, factor_ref[...], (((1,), (1,)), ((), ())),
@@ -515,7 +463,7 @@
 def last_sweep(
     applied_ref, left_ref, right_ref, rhs_ref, inverse_ref, smooth_ref, update_ref, rows_ref,
     tree_ref, factor_ref, near_ref, table_ref,
-    precond_ref, out_ref, send_ref,
+    precond_ref, out_ref, low_ref, high_ref, zlow_ref, zhigh_ref, send_ref,
 ):
     smooth, update = relax(
         2, 2, applied_ref, left_ref, right_ref, rhs_ref, inverse_ref, smooth_ref, update_ref
@@ -532,18 +480,39 @@
             start = 8 * (2 * i + z)
             first = first + near_ref[start : start + 8, :] * precond[i][z]
             second = second + applied[i][z] * precond[i][z]
-    extra = two_rows(jnp.sum(first, axis=0, keepdims=True), jnp.sum(second, axis=0, keepdims=True))
-    send_along_z(applied, extra, send_ref)
-
-
-def finish(summed_ref, received_ref, precond_ref, rhs_ref, solution_ref, residual_ref):
-    left, right = x_faces_received(received_ref)
-    image = each(wall, sum_y(sum_x(read(summed_ref), left, right)))
-    extra = received_ref[0, 16:24, :]
-    for e in range(1, N_GX):
-        extra = extra + received_ref[e, 16:24, :]
-    totals = jnp.sum(extra, axis=1, keepdims=True)
-    alpha = spread(totals[0:1, :] / totals[1:2, :])
+    write_x_faces(applied, low_ref, high_ref)
+    write_z_faces(applied, zlow_ref, zhigh_ref)
+    first = first + pltpu.roll(first, 64, 1)
+    second = second + pltpu.roll(second, 64, 1)
+    both = jnp.where(lane_iota() < 64, first, second)
+    both = spread(jnp.sum(both, axis=0, keepdims=True))
+    for chunk in range(0, DEVICES, 8):
+        send_ref[chunk : chunk + 8, :] = both
+
+
+def join_edges(zlow_ref, zhigh_ref, left_ref, right_ref, low_ref, high_ref):
+    for z, node, source, target in ((0, 0, zlow_ref, low_ref), (1, 7, zhigh_ref, high_ref)):
+        row = 8 * z + node
+        target[...] = source[...]
+        target[0:1, :] = source[0:1, :] + left_ref[row : row + 1, :]
+        target[7:8, :] = source[7:8, :] + right_ref[row : row + 1, :]
+
+
+def finish(
+    applied_ref, left_ref, right_ref, before_ref, after_ref, received_ref, precond_ref, rhs_ref,
+    solution_ref, residual_ref,
+):
+    field = sum_x(read(applied_ref), faces(left_ref, 2), faces(right_ref, 2))
+    field = sum_z(field, lambda i: before_ref[i : i + 1, :], lambda i: after_ref[i : i + 1, :])
+    image = each(wall, sum_y(field))
+    total = received_ref[0:8, :]
+    for start in range(8, DEVICES, 8):
+        total = total + received_ref[start : start + 8, :]
+    total = jnp.sum(total, axis=0, keepdims=True)
+    lane = lax.broadcasted_iota(jnp.int32, (1, 128), 1)
+    product = jnp.sum(jnp.where(lane < 64, total, 0.0), axis=1, keepdims=True)
+    curvature = jnp.sum(jnp.where(lane < 64, 0.0, total), axis=1, keepdims=True)
+    alpha = spread(product / curvature)
     write(solution_ref, each(lambda p: alpha * p, read(precond_ref)))
     write(residual_ref, each(lambda r, a: r - alpha * a, read(rhs_ref, 2, 2), image))
 
@@ -572,13 +541,17 @@
     return shifted(high, axis, 1), shifted(low, axis, -1)
 
 
+def send_to_all(value, rows):
+    chunks = value.reshape(DEVICES, rows, 128)
+    return lax.all_to_all(chunks, ("gx", "gz"), 0, 0, tiled=True).reshape(value.shape)
+
+
 def per_device(element_rhs_load, metric, coarse_factor):
-    load = element_rhs_load.reshape(field_shape(2))
     constants = jnp.asarray(TABLE)
     factor = coarse_factor.reshape(10, 32, 16).transpose(1, 0, 2).reshape(32, 160)
     factor = jnp.pad(factor, ((0, 0), (0, 96)))
     near, up, down = run(
-        pack, [(136, 128), (80, 128), (80, 128)], load, metric.reshape(6, 16), constants
+        pack, [(136, 128), (80, 128), (80, 128)], element_rhs_load, metric
     )
     below, far_below = shifted(near, "gz", 1), shifted(up, "gz", 2)
     above, far_above = shifted(near, "gz", -1), shifted(down, "gz", -2)
@@ -588,10 +561,10 @@
     )
     left, right = exchange(low, high, "gx")
     rhs, inverse, smooth, applied, low, high, send = run(
-        begin, [field_shape(6)] * 3 + [field_shape(8)] + [(64, 128)] * 2 + [(N_GZ, 2, 128)],
+        begin, [field_shape(6)] * 3 + [field_shape(8)] + [(64, 128)] * 2 + [(2 * DEVICES, 128)],
         wide, edge, rows, left, right, factor, constants,
     )
-    tree = lax.all_to_all(send, "gz", 0, 0, tiled=True)
+    tree = send_to_all(send, 2)
     left, right = exchange(low, high, "gx")
     update = smooth
     for step, count in ((0, 6), (1, 4)):
@@ -604,18 +577,17 @@
             applied, left, right, rhs, inverse, smooth, update, rows, constants,
         )
         left, right = exchange(low, high, "gx")
-        if step == 0:
-            (send,) = run(lower_tree, [(N_GX, 2, 128)], tree)
-            tree = lax.all_to_all(send, "gx", 0, 0, tiled=True)
-    precond, applied, send = run(
-        last_sweep, [field_shape(2)] * 2 + [(N_GZ, 16, 128)],
+    precond, applied, low, high, zlow, zhigh, send = run(
+        last_sweep, [field_shape(2)] * 2 + [(16, 128)] * 2 + [(8, 128)] * 2 + [(DEVICES, 128)],
         applied, left, right, rhs, inverse, smooth, update, rows, tree, factor, near, constants,
     )
-    received = lax.all_to_all(send, "gz", 0, 0, tiled=True)
-    summed, send = run(middle, [field_shape(2), (N_GX, 24, 128)], applied, received)
-    received = lax.all_to_all(send, "gx", 0, 0, tiled=True)
+    received = send_to_all(send, 1)
+    left, right = exchange(low, high, "gx")
+    zlow, zhigh = run(join_edges, [(8, 128)] * 2, zlow, zhigh, left, right)
+    before, after = exchange(zlow, zhigh, "gz")
     solution_field, residual = run(
-        finish, [field_shape(2)] * 2, summed, received, precond, rhs, last=True
+        finish, [field_shape(2)] * 2,
+        applied, left, right, before, after, received, precond, rhs, last=True,
     )
     shape = element_rhs_load.shape
     return solution_field.reshape(shape), residual.reshape(shape)

time: 129 us -> 138 us (1.070)
  starting transfers between devices: 67.4 us -> 111 us
  blocking collectives: 43.3 us -> 0 us
  waiting for transfers between devices: 9.08 us -> 17.6 us
    all_to_all x2 -> x0, blocking collectives: 43.3 us -> none  [the longest x1 23.5 us: per_device(): received = lax.all_to_all(send, 'gz', 0, 0, tiled=True)]
    ppermute x12 -> x16, starting transfers between devices: 49.3 us -> 74.7 us  [shifted(): lax.ppermute(value, axis, [(i, (i + distance) % count) for i in range(cou...]
    all_to_all x2, starting transfers between devices: 18.1 us -> 36.5 us  [send_to_all(): lax.all_to_all(chunks, ('gx', 'gz'), 0, 0, tiled=True).reshape(value.shape)]
    all_to_all x2, waiting for transfers between devices: 0.01 us -> 8.95 us  [send_to_all(): lax.all_to_all(chunks, ('gx', 'gz'), 0, 0, tiled=True).reshape(value.shape)]
    pallas_call x9 -> x8, Pallas kernels: 5.22 us -> 5.67 us  [run(): pl.pallas_call(kernel, out_shape=outs, in_specs=[spec] * len(operands), o...]
    ppermute x12 -> x16, waiting for transfers between devices: 9.08 us -> 8.66 us  [shifted(): lax.ppermute(value, axis, [(i, (i + distance) % count) for i in range(cou...]
  transfers between devices with their start and end apart: 14 -> 18, of which waited for: 4 -> 9; matrix products, arithmetic and copies ran while one was open for 0% -> 0% of each run, Pallas kernels for 1% -> 1%
where the time goes in v3:
time: 138 us; the launch traced here: 137 us
  starting transfers between devices  111 us (80%)
  waiting for transfers between devices  17.6 us (13%)
  Pallas kernels  5.67 us (4%)
  local copies, waits for them, and re-layouts  1.61 us (1%)
    ppermute x16, starting transfers between devices, shifted(): lax.ppermute(value, axis, [(i, (i + distance) % count) for i in range(cou...  74.7 us
    all_to_all x2, starting transfers between devices, send_to_all(): lax.all_to_all(chunks, ('gx', 'gz'), 0, 0, tiled=True).reshape(value.shape)  36.5 us
    all_to_all x2, waiting for transfers between devices, send_to_all(): lax.all_to_all(chunks, ('gx', 'gz'), 0, 0, tiled=True).reshape(value.shape)  8.95 us
    ppermute x16, waiting for transfers between devices, shifted(): lax.ppermute(value, axis, [(i, (i + distance) % count) for i in range(cou...  8.66 us
    pallas_call x8, Pallas kernels, run(): pl.pallas_call(kernel, out_shape=outs, in_specs=[spec] * len(operands), o...  5.67 us
  transfers between devices with their start and end apart: 18, of which 9 were waited for; matrix products, arithmetic and copies ran while one was open for 0% of the time, Pallas kernels for 1%

profile of v3, /device:TPU:1, one launch (start us, length us, event | category | flops | bytes accessed | tf_op | source)
XLA Modules:
  0.0 136.9 jit_solution(5937627464113019549)
XLA Ops:
  0.6 0.0 copy-start.1
  0.6 0.8 copy-done.1
  1.5 0.7 copy-done.2
  2.2 0.1 shard_map.59
  2.3 12.0 %collective-permute-start.2 = (f32[136,128]{1,0:T(8,128)S(1)}, f32[136,128]{1,0:T(8,128)S(1)}, u32[]{:S(2)}, u32[]{:S(2)}) collective-permute-start(f32[136,128]{1,0:T(8,128)S(1)} %get-tuple-element.38.near_ref), channel_id=1, source_target_pairs={{0,15},{1,0},{2,1},{3,2},{4,3},{5,4},{6,5},{7,6},{8,7},{9,8},{10,9... | collective-permute-start | bytes 208904 | tf_op jit(solution)/shard_map/ppermute | solution.py:537
  14.3 1.9 %collective-permute-start = (f32[136,128]{1,0:T(8,128)S(1)}, f32[136,128]{1,0:T(8,128)S(1)}, u32[]{:S(2)}, u32[]{:S(2)}) collective-permute-start(f32[136,128]{1,0:T(8,128)S(1)} %get-tuple-element.38.near_ref), channel_id=1, source_target_pairs={{0,1},{1,2},{2,3},{3,4},{4,5},{5,6},{6,7},{7,8},{8,9},{9,10},{10,1... | collective-permute-start | bytes 208904 | tf_op jit(solution)/shard_map/ppermute | solution.py:537
  16.2 1.9 %collective-permute-start.1 = (f32[80,128]{1,0:T(8,128)S(1)}, f32[80,128]{1,0:T(8,128)S(1)}, u32[]{:S(2)}, u32[]{:S(2)}) collective-permute-start(f32[80,128]{1,0:T(8,128)S(1)} %get-tuple-element.39), channel_id=1, source_target_pairs={{0,2},{1,3},{2,4},{3,5},{4,6},{5,7},{6,8},{7,9},{8,10},{9,11},{10,... | collective-permute-start | bytes 122888 | tf_op jit(solution)/shard_map/ppermute | solution.py:537
  18.1 0.0 copy-start.3
  18.1 5.6 %collective-permute-start.3 = (f32[80,128]{1,0:T(8,128)S(1)}, f32[80,128]{1,0:T(8,128)S(1)}, u32[]{:S(2)}, u32[]{:S(2)}) collective-permute-start(f32[80,128]{1,0:T(8,128)S(1)} %get-tuple-element.40), channel_id=1, source_target_pairs={{0,14},{1,15},{2,0},{3,1},{4,2},{5,3},{6,4},{7,5},{8,6},{9,7},{10,... | collective-permute-start | bytes 122888 | tf_op jit(solution)/shard_map/ppermute | solution.py:537
  23.7 0.0 collective-permute-done.1.far_below_ref
  23.8 1.1 collective-permute-done.3.far_above_ref
  24.8 0.0 collective-permute-done.2.above_ref
  24.8 0.0 collective-permute-done.below_ref
  24.9 0.0 copy-start
  24.9 5.6 %collective-permute-start.4 = (f32[104,128]{1,0:T(8,128)S(1)}, f32[104,128]{1,0:T(8,128)S(1)}, u32[]{:S(2)}, u32[]{:S(2)}) collective-permute-start(f32[104,128]{1,0:T(8,128)S(1)} %get-tuple-element.44), channel_id=1, source_target_pairs={{0,16},{16,32},{32,48},{48,64},{64,80},{80,96},{96,112},{112,128},... | collective-permute-start | bytes 159752 | tf_op jit(solution)/shard_map/ppermute | solution.py:537
  30.5 1.9 %collective-permute-start.5 = (f32[104,128]{1,0:T(8,128)S(1)}, f32[104,128]{1,0:T(8,128)S(1)}, u32[]{:S(2)}, u32[]{:S(2)}) collective-permute-start(f32[104,128]{1,0:T(8,128)S(1)} %get-tuple-element.45), channel_id=1, source_target_pairs={{0,496},{16,0},{32,16},{48,32},{64,48},{80,64},{96,80},{112,96},{1... | collective-permute-start | bytes 159752 | tf_op jit(solution)/shard_map/ppermute | solution.py:537
  32.5 0.1 copy.8
  32.5 0.0 collective-permute-done.4.left_ref
  32.6 3.4 %collective-permute-done.5.right_ref = f32[104,128]{1,0:T(8,128)S(1)} collective-permute-done((f32[104,128]{1,0:T(8,128)S(1)}, f32[104,128]{1,0:T(8,128)S(1)}, u32[]{:S(2)}, u32[]{:S(2)}) %collective-permute-start.5) | collective-permute-done | bytes 53280 | tf_op jit(solution)/shard_map/ppermute | solution.py:537
  36.0 1.9 %shard_map.61 = (f32[8,6,8,128]{3,2,1,0:T(8,128)S(1)}, f32[8,6,8,128]{3,2,1,0:T(8,128)S(1)}, f32[8,6,8,128]{3,2,1,0:T(8,128)S(1)}, f32[8,8,8,128]{3,2,1,0:T(8,12...) custom-call(f32[8,8,8,128]{3,2,1,0:T(8,128)S(1)} %get-tuple-element.41.load_ref, ...), custom_call_target="tpu_custom_call" | custom-call | tf_op jit(solution)/shard_map/pallas_call | solution.py:530
  37.9 18.1 %all-to-all-start = ((f32[512,2,128]{2,1,0:T(2,128)}), f32[512,2,128]{2,1,0:T(2,128)S(1)}, u32[]{:S(2)}, u32[]{:S(2)}) async-start(f32[512,2,128]{2,1,0:T(2,128)} %bitcast.3), calls=%async_computation | async-start | bytes 1048576 | tf_op jit(solution)/shard_map/all_to_all | solution.py:546
  56.0 3.5 %collective-permute-start.6 = (f32[64,128]{1,0:T(8,128)S(1)}, f32[64,128]{1,0:T(8,128)S(1)}, u32[]{:S(2)}, u32[]{:S(2)}) collective-permute-start(f32[64,128]{1,0:T(8,128)S(1)} %get-tuple-element.47), channel_id=1, source_target_pairs={{0,16},{16,32},{32,48},{48,64},{64,80},{80,96},{96,112},{112,128},... | collective-permute-start | bytes 98312 | tf_op jit(solution)/shard_map/ppermute | solution.py:537
  59.5 4.6 %collective-permute-start.7 = (f32[64,128]{1,0:T(8,128)S(1)}, f32[64,128]{1,0:T(8,128)S(1)}, u32[]{:S(2)}, u32[]{:S(2)}) collective-permute-start(f32[64,128]{1,0:T(8,128)S(1)} %get-tuple-element.48), channel_id=1, source_target_pairs={{0,496},{16,0},{32,16},{48,32},{64,48},{80,64},{96,80},{112,96},{1... | collective-permute-start | bytes 98312 | tf_op jit(solution)/shard_map/ppermute | solution.py:537
  64.1 0.0 collective-permute-done.6.refs_1_
  64.1 1.0 collective-permute-done.7.refs_2_
  65.1 0.7 shard_map.62
  65.8 1.9 %collective-permute-start.8 = (f32[48,128]{1,0:T(8,128)S(1)}, f32[48,128]{1,0:T(8,128)S(1)}, u32[]{:S(2)}, u32[]{:S(2)}) collective-permute-start(f32[48,128]{1,0:T(8,128)S(1)} %get-tuple-element.53), channel_id=1, source_target_pairs={{0,16},{16,32},{32,48},{48,64},{64,80},{80,96},{96,112},{112,128},... | collective-permute-start | bytes 73736 | tf_op jit(solution)/shard_map/ppermute | solution.py:537
  67.7 7.5 %collective-permute-start.9 = (f32[48,128]{1,0:T(8,128)S(1)}, f32[48,128]{1,0:T(8,128)S(1)}, u32[]{:S(2)}, u32[]{:S(2)}) collective-permute-start(f32[48,128]{1,0:T(8,128)S(1)} %get-tuple-element.54), channel_id=1, source_target_pairs={{0,496},{16,0},{32,16},{48,32},{64,48},{80,64},{96,80},{112,96},{1... | collective-permute-start | bytes 73736 | tf_op jit(solution)/shard_map/ppermute | solution.py:537
  75.3 0.0 collective-permute-done.8.refs_1_
  75.3 0.8 collective-permute-done.9.refs_2_
  76.1 0.5 shard_map.63
  76.6 1.9 %collective-permute-start.10 = (f32[32,128]{1,0:T(8,128)S(1)}, f32[32,128]{1,0:T(8,128)S(1)}, u32[]{:S(2)}, u32[]{:S(2)}) collective-permute-start(f32[32,128]{1,0:T(8,128)S(1)} %get-tuple-element.58), channel_id=1, source_target_pairs={{0,16},{16,32},{32,48},{48,64},{64,80},{80,96},{96,112},{112,128},... | collective-permute-start | bytes 49160 | tf_op jit(solution)/shard_map/ppermute | solution.py:537
  78.6 8.1 %collective-permute-start.11 = (f32[32,128]{1,0:T(8,128)S(1)}, f32[32,128]{1,0:T(8,128)S(1)}, u32[]{:S(2)}, u32[]{:S(2)}) collective-permute-start(f32[32,128]{1,0:T(8,128)S(1)} %get-tuple-element.59), channel_id=1, source_target_pairs={{0,496},{16,0},{32,16},{48,32},{64,48},{80,64},{96,80},{112,96},{1... | collective-permute-start | bytes 49160 | tf_op jit(solution)/shard_map/ppermute | solution.py:537
  86.6 0.0 collective-permute-done.10.left_ref
  86.6 0.8 collective-permute-done.11.right_ref
  87.4 4.0 %all-to-all-done = f32[512,2,128]{2,1,0:T(2,128)S(1)} async-done(((f32[512,2,128]{2,1,0:T(2,128)}), f32[512,2,128]{2,1,0:T(2,128)S(1)}, u32[]{:S(2)}, u32[]{:S(2)}) %all-to-all-start) | async-done | bytes 524320 | tf_op jit(solution)/shard_map/all_to_all | solution.py:546
  91.5 1.6 %shard_map.64 = (f32[8,2,8,128]{3,2,1,0:T(8,128)S(1)}, f32[8,2,8,128]{3,2,1,0:T(8,128)S(1)}, f32[16,128]{1,0:T(8,128)S(1)}, f32[16,128]{1,0:T(8,128)S(1)}, f32[8...) custom-call(f32[8,4,8,128]{3,2,1,0:T(8,128)S(1)} %get-tuple-element.57.applied_ref, ...), custom_call_target="tpu_custom_call" | custom-call | tf_op jit(solution)/shard_map/pallas_call | solution.py:530
  93.0 18.4 %all-to-all-start.1 = ((f32[512,1,128]{2,1,0:T(1,128)}), f32[512,1,128]{2,1,0:T(1,128)S(1)}, u32[]{:S(2)}, u32[]{:S(2)}) async-start(f32[512,1,128]{2,1,0:T(1,128)} %bitcast.6), calls=%async_computation.1 | async-start | bytes 524288 | tf_op jit(solution)/shard_map/all_to_all | solution.py:546
  111.4 3.5 %collective-permute-start.12 = (f32[16,128]{1,0:T(8,128)S(1)}, f32[16,128]{1,0:T(8,128)S(1)}, u32[]{:S(2)}, u32[]{:S(2)}) collective-permute-start(f32[16,128]{1,0:T(8,128)S(1)} %get-tuple-element.64), channel_id=1, source_target_pairs={{0,16},{16,32},{32,48},{48,64},{64,80},{80,96},{96,112},{112,128},... | collective-permute-start | bytes 24584 | tf_op jit(solution)/shard_map/ppermute | solution.py:537
  115.0 4.6 %collective-permute-start.13 = (f32[16,128]{1,0:T(8,128)S(1)}, f32[16,128]{1,0:T(8,128)S(1)}, u32[]{:S(2)}, u32[]{:S(2)}) collective-permute-start(f32[16,128]{1,0:T(8,128)S(1)} %get-tuple-element.65), channel_id=1, source_target_pairs={{0,496},{16,0},{32,16},{48,32},{64,48},{80,64},{96,80},{112,96},{1... | collective-permute-start | bytes 24584 | tf_op jit(solution)/shard_map/ppermute | solution.py:537
  119.6 0.0 collective-permute-done.12.left_ref
  119.6 0.8 collective-permute-done.13.right_ref
  120.4 3.1 %collective-permute-start.14 = (f32[8,128]{1,0:T(8,128)S(1)}, f32[8,128]{1,0:T(8,128)S(1)}, u32[]{:S(2)}, u32[]{:S(2)}) collective-permute-start(f32[8,128]{1,0:T(8,128)S(1)} %get-tuple-element.68), channel_id=1, source_target_pairs={{0,1},{1,2},{2,3},{3,4},{4,5},{5,6},{6,7},{7,8},{8,9},{9,10},{10,1... | collective-permute-start | bytes 12296 | tf_op jit(solution)/shard_map/ppermute | solution.py:537
  123.5 6.9 %collective-permute-start.15 = (f32[8,128]{1,0:T(8,128)S(1)}, f32[8,128]{1,0:T(8,128)S(1)}, u32[]{:S(2)}, u32[]{:S(2)}) collective-permute-start(f32[8,128]{1,0:T(8,128)S(1)} %get-tuple-element.69), channel_id=1, source_target_pairs={{0,15},{1,0},{2,1},{3,2},{4,3},{5,4},{6,5},{7,6},{8,7},{9,8},{10,9... | collective-permute-start | bytes 12296 | tf_op jit(solution)/shard_map/ppermute | solution.py:537
  130.5 0.0 collective-permute-done.14.before_ref
  130.5 0.7 collective-permute-done.15.after_ref
  131.2 4.9 %all-to-all-done.1 = f32[512,1,128]{2,1,0:T(1,128)S(1)} async-done(((f32[512,1,128]{2,1,0:T(1,128)}), f32[512,1,128]{2,1,0:T(1,128)S(1)}, u32[]{:S(2)}, u32[]{:S(2)}) %all-to-all-start.1) | async-done | bytes 262176 | tf_op jit(solution)/shard_map/all_to_all | solution.py:546
  136.1 0.8 shard_map.66
  (6 shorter events, 0.1 us)
Async XLA Ops:
  0.6 0.8 copy-start.1
  1.5 0.7 copy-start.2
  2.3 22.5 %collective-permute-start.2 = (f32[136,128]{1,0:T(8,128)S(1)}, f32[136,128]{1,0:T(8,128)S(1)}, u32[]{:S(2)}, u32[]{:S(2)}) collective-permute-start(f32[136,128]{1,0:T(8,128)S(1)} %get-tuple-element.38.near_ref), channel_id=1, source_target_pairs={{0,15},{1,0},{2,1},{3,2},{4,3},{5,4},{6,5},{7,6},{8,7},{9,8},{10,9... | collective-permute-start | bytes 208904 | tf_op jit(solution)/shard_map/ppermute | solution.py:537
  14.3 10.6 %collective-permute-start = (f32[136,128]{1,0:T(8,128)S(1)}, f32[136,128]{1,0:T(8,128)S(1)}, u32[]{:S(2)}, u32[]{:S(2)}) collective-permute-start(f32[136,128]{1,0:T(8,128)S(1)} %get-tuple-element.38.near_ref), channel_id=1, source_target_pairs={{0,1},{1,2},{2,3},{3,4},{4,5},{5,6},{6,7},{7,8},{8,9},{9,10},{10,1... | collective-permute-start | bytes 208904 | tf_op jit(solution)/shard_map/ppermute | solution.py:537
  16.2 7.6 %collective-permute-start.1 = (f32[80,128]{1,0:T(8,128)S(1)}, f32[80,128]{1,0:T(8,128)S(1)}, u32[]{:S(2)}, u32[]{:S(2)}) collective-permute-start(f32[80,128]{1,0:T(8,128)S(1)} %get-tuple-element.39), channel_id=1, source_target_pairs={{0,2},{1,3},{2,4},{3,5},{4,6},{5,7},{6,8},{7,9},{8,10},{9,11},{10,... | collective-permute-start | bytes 122888 | tf_op jit(solution)/shard_map/ppermute | solution.py:537
  18.1 14.3 %copy-start.3 = (f32[1,1,10,32,16]{3,4,2,1,0:T(8,128)S(1)}, f32[1,1,10,32,16]{3,4,2,1,0:T(8,128)}, u32[]{:S(2)}) copy-start(f32[1,1,10,32,16]{3,4,2,1,0:T(8,128)} %param.6) | copy-start | bytes 61444
  18.1 6.7 %collective-permute-start.3 = (f32[80,128]{1,0:T(8,128)S(1)}, f32[80,128]{1,0:T(8,128)S(1)}, u32[]{:S(2)}, u32[]{:S(2)}) collective-permute-start(f32[80,128]{1,0:T(8,128)S(1)} %get-tuple-element.40), channel_id=1, source_target_pairs={{0,14},{1,15},{2,0},{3,1},{4,2},{5,3},{6,4},{7,5},{8,6},{9,7},{10,... | collective-permute-start | bytes 122888 | tf_op jit(solution)/shard_map/ppermute | solution.py:537
  24.9 11.1 %copy-start = (f32[240,128]{1,0:T(8,128)S(1)}, f32[240,128]{1,0:T(8,128)}, u32[]{:S(2)}) copy-start(f32[240,128]{1,0:T(8,128)} %constant.5.clone.table_ref.refs_8_) | copy-start | bytes 368644
  24.9 7.7 %collective-permute-start.4 = (f32[104,128]{1,0:T(8,128)S(1)}, f32[104,128]{1,0:T(8,128)S(1)}, u32[]{:S(2)}, u32[]{:S(2)}) collective-permute-start(f32[104,128]{1,0:T(8,128)S(1)} %get-tuple-element.44), channel_id=1, source_target_pairs={{0,16},{16,32},{32,48},{48,64},{64,80},{80,96},{96,112},{112,128},... | collective-permute-start | bytes 159752 | tf_op jit(solution)/shard_map/ppermute | solution.py:537
  30.5 5.5 %collective-permute-start.5 = (f32[104,128]{1,0:T(8,128)S(1)}, f32[104,128]{1,0:T(8,128)S(1)}, u32[]{:S(2)}, u32[]{:S(2)}) collective-permute-start(f32[104,128]{1,0:T(8,128)S(1)} %get-tuple-element.45), channel_id=1, source_target_pairs={{0,496},{16,0},{32,16},{48,32},{64,48},{80,64},{96,80},{112,96},{1... | collective-permute-start | bytes 159752 | tf_op jit(solution)/shard_map/ppermute | solution.py:537
  37.9 53.6 %all-to-all-start = ((f32[512,2,128]{2,1,0:T(2,128)}), f32[512,2,128]{2,1,0:T(2,128)S(1)}, u32[]{:S(2)}, u32[]{:S(2)}) async-start(f32[512,2,128]{2,1,0:T(2,128)} %bitcast.3), calls=%async_computation | async-start | bytes 1048576 | tf_op jit(solution)/shard_map/all_to_all | solution.py:546
  56.0 8.1 %collective-permute-start.6 = (f32[64,128]{1,0:T(8,128)S(1)}, f32[64,128]{1,0:T(8,128)S(1)}, u32[]{:S(2)}, u32[]{:S(2)}) collective-permute-start(f32[64,128]{1,0:T(8,128)S(1)} %get-tuple-element.47), channel_id=1, source_target_pairs={{0,16},{16,32},{32,48},{48,64},{64,80},{80,96},{96,112},{112,128},... | collective-permute-start | bytes 98312 | tf_op jit(solution)/shard_map/ppermute | solution.py:537
  59.5 5.6 %collective-permute-start.7 = (f32[64,128]{1,0:T(8,128)S(1)}, f32[64,128]{1,0:T(8,128)S(1)}, u32[]{:S(2)}, u32[]{:S(2)}) collective-permute-start(f32[64,128]{1,0:T(8,128)S(1)} %get-tuple-element.48), channel_id=1, source_target_pairs={{0,496},{16,0},{32,16},{48,32},{64,48},{80,64},{96,80},{112,96},{1... | collective-permute-start | bytes 98312 | tf_op jit(solution)/shard_map/ppermute | solution.py:537
  65.8 9.5 %collective-permute-start.8 = (f32[48,128]{1,0:T(8,128)S(1)}, f32[48,128]{1,0:T(8,128)S(1)}, u32[]{:S(2)}, u32[]{:S(2)}) collective-permute-start(f32[48,128]{1,0:T(8,128)S(1)} %get-tuple-element.53), channel_id=1, source_target_pairs={{0,16},{16,32},{32,48},{48,64},{64,80},{80,96},{96,112},{112,128},... | collective-permute-start | bytes 73736 | tf_op jit(solution)/shard_map/ppermute | solution.py:537
  67.7 8.4 %collective-permute-start.9 = (f32[48,128]{1,0:T(8,128)S(1)}, f32[48,128]{1,0:T(8,128)S(1)}, u32[]{:S(2)}, u32[]{:S(2)}) collective-permute-start(f32[48,128]{1,0:T(8,128)S(1)} %get-tuple-element.54), channel_id=1, source_target_pairs={{0,496},{16,0},{32,16},{48,32},{64,48},{80,64},{96,80},{112,96},{1... | collective-permute-start | bytes 73736 | tf_op jit(solution)/shard_map/ppermute | solution.py:537
  76.6 10.0 %collective-permute-start.10 = (f32[32,128]{1,0:T(8,128)S(1)}, f32[32,128]{1,0:T(8,128)S(1)}, u32[]{:S(2)}, u32[]{:S(2)}) collective-permute-start(f32[32,128]{1,0:T(8,128)S(1)} %get-tuple-element.58), channel_id=1, source_target_pairs={{0,16},{16,32},{32,48},{48,64},{64,80},{80,96},{96,112},{112,128},... | collective-permute-start | bytes 49160 | tf_op jit(solution)/shard_map/ppermute | solution.py:537
  78.6 8.9 %collective-permute-start.11 = (f32[32,128]{1,0:T(8,128)S(1)}, f32[32,128]{1,0:T(8,128)S(1)}, u32[]{:S(2)}, u32[]{:S(2)}) collective-permute-start(f32[32,128]{1,0:T(8,128)S(1)} %get-tuple-element.59), channel_id=1, source_target_pairs={{0,496},{16,0},{32,16},{48,32},{64,48},{80,64},{96,80},{112,96},{1... | collective-permute-start | bytes 49160 | tf_op jit(solution)/shard_map/ppermute | solution.py:537
  93.0 43.1 %all-to-all-start.1 = ((f32[512,1,128]{2,1,0:T(1,128)}), f32[512,1,128]{2,1,0:T(1,128)S(1)}, u32[]{:S(2)}, u32[]{:S(2)}) async-start(f32[512,1,128]{2,1,0:T(1,128)} %bitcast.6), calls=%async_computation.1 | async-start | bytes 524288 | tf_op jit(solution)/shard_map/all_to_all | solution.py:546
  111.4 8.1 %collective-permute-start.12 = (f32[16,128]{1,0:T(8,128)S(1)}, f32[16,128]{1,0:T(8,128)S(1)}, u32[]{:S(2)}, u32[]{:S(2)}) collective-permute-start(f32[16,128]{1,0:T(8,128)S(1)} %get-tuple-element.64), channel_id=1, source_target_pairs={{0,16},{16,32},{32,48},{48,64},{64,80},{80,96},{96,112},{112,128},... | collective-permute-start | bytes 24584 | tf_op jit(solution)/shard_map/ppermute | solution.py:537
  115.0 5.4 %collective-permute-start.13 = (f32[16,128]{1,0:T(8,128)S(1)}, f32[16,128]{1,0:T(8,128)S(1)}, u32[]{:S(2)}, u32[]{:S(2)}) collective-permute-start(f32[16,128]{1,0:T(8,128)S(1)} %get-tuple-element.65), channel_id=1, source_target_pairs={{0,496},{16,0},{32,16},{48,32},{64,48},{80,64},{96,80},{112,96},{1... | collective-permute-start | bytes 24584 | tf_op jit(solution)/shard_map/ppermute | solution.py:537
  120.4 10.1 %collective-permute-start.14 = (f32[8,128]{1,0:T(8,128)S(1)}, f32[8,128]{1,0:T(8,128)S(1)}, u32[]{:S(2)}, u32[]{:S(2)}) collective-permute-start(f32[8,128]{1,0:T(8,128)S(1)} %get-tuple-element.68), channel_id=1, source_target_pairs={{0,1},{1,2},{2,3},{3,4},{4,5},{5,6},{6,7},{7,8},{8,9},{9,10},{10,1... | collective-permute-start | bytes 12296 | tf_op jit(solution)/shard_map/ppermute | solution.py:537
  123.5 7.6 %collective-permute-start.15 = (f32[8,128]{1,0:T(8,128)S(1)}, f32[8,128]{1,0:T(8,128)S(1)}, u32[]{:S(2)}, u32[]{:S(2)}) collective-permute-start(f32[8,128]{1,0:T(8,128)S(1)} %get-tuple-element.69), channel_id=1, source_target_pairs={{0,15},{1,0},{2,1},{3,2},{4,3},{5,4},{6,5},{7,6},{8,7},{9,8},{10,9... | collective-permute-start | bytes 12296 | tf_op jit(solution)/shard_map/ppermute | solution.py:537

commit v4 on v2

--- a/solution.py
+++ b/solution.py
@@ -87,7 +87,6 @@
         "wl": np.ones((8, 1)) * w_l,
         "wj": w_j * ones,
         "mult": EDGE[:, None] * across[None, :],
-        "expand": np.kron(np.eye(16), np.ones((1, 8))),
         "modes": np.tile(ALONG_Y, (4, 1)),
     }
     for b in range(2):
@@ -240,40 +239,69 @@
         sum_of_x, sum_of_rest = part_x, part_rest
         if i in (0, 7):
             side = left_ref if i == 0 else right_ref
-            side_x, side_rest = diagonal_parts(side, FACE_METRIC, column, table_ref)
+            side_x, side_rest = diagonal_parts(side, Facross_refE_METRIC, column, table_ref)
             sum_of_x, sum_of_rest = part_x + side_x, part_rest + side_rest
         out.append(KD[i] * sum_of_x + W[i] * sum_of_rest)
     return out
 
 
-def write_x_faces(field, low_ref, high_ref):
+class Faces:
+    def __init__(self, across_ref, within_ref):
+        self.odd = lax.rem(lax.axis_index("gx"), 2) == 1
+        self.across, self.within = across_ref, within_ref
+
+    def put(self, first, last, low, high):
+        self.across[first:last, :] = jnp.where(self.odd, high, low)
+        self.within[first:last, :] = jnp.where(self.odd, low, high)
+
+
+class Side:
+    def __init__(self, across_ref, within_ref, right):
+        odd = lax.rem(lax.axis_index("gx"), 2) == 1
+        self.across = odd if right else jnp.logical_not(odd)
+        self.across_ref, self.within_ref = across_ref, within_ref
+
+    def __getitem__(self, where):
+        return jnp.where(self.across, self.across_ref[where], self.within_ref[where])
+
+
+def sides(across_ref, within_ref):
+    return Side(across_ref, within_ref, False), Side(across_ref, within_ref, True)
+
+
+def write_x_faces(field, across_ref, within_ref):
+    out = Faces(across_ref, within_ref)
     for c in range(len(field[0])):
-        low_ref[8 * c : 8 * c + 8, :] = field[0][c]
-        high_ref[8 * c : 8 * c + 8, :] = field[7][c]
+        out.put(8 * c, 8 * c + 8, field[0][c], field[7][c])
 
 
 def faces(ref, count):
     return [ref[8 * c : 8 * c + 8, :] for c in range(count)]
 
 
-def pack(load_ref, metric_ref, table_ref, near_ref, up_ref, down_ref):
-    expanded = jnp.dot(
-        metric_ref[...], table(table_ref, "expand"), precision=HIGHEST, preferred_element_type=F32
-    )
+def pack(load_ref, metric_ref, near_ref, up_ref, down_ref):
+    element = lax.broadcasted_iota(jnp.int32, (16, 128), 0)
+    lane = lax.broadcasted_iota(jnp.int32, (16, 128), 1)
+    expand = jnp.where(element == lane // 8, 1.0, 0.0)
     for ref, start in ((near_ref, 128), (up_ref, 72), (down_ref, 72)):
-        ref[start : start + 6, :] = expanded
         ref[start + 6 : start + 8, :] = jnp.zeros((2, 128), F32)
+    for m in range(3):
+        expanded = jnp.dot(
+            metric_ref[m, 0], expand, precision=HIGHEST, preferred_element_type=F32
+        )
+        for ref, start in ((near_ref, 128), (up_ref, 72), (down_ref, 72)):
+            ref[start + 2 * m : start + 2 * m + 2, :] = expanded
     for i in range(8):
         for z in range(2):
-            near_ref[8 * (2 * i + z) : 8 * (2 * i + z) + 8, :] = load_ref[i, z]
-        up_ref[8 * i : 8 * i + 8, :] = load_ref[i, 1]
-        up_ref[64 + i : 65 + i, :] = load_ref[i, 0, 7:8, :]
-        down_ref[8 * i : 8 * i + 8, :] = load_ref[i, 0]
-        down_ref[64 + i : 65 + i, :] = load_ref[i, 1, 0:1, :]
-
-
-FACE_METRIC = 72
-FACE_ROWS = 104
+            near_ref[8 * (2 * i + z) : 8 * (2 * i + z) + 8, :] = load_ref[0, i, z]
+        up_ref[8 * i : 8 * i + 8, :] = load_ref[0, i, 1]
+        up_ref[64 + i : 65 + i, :] = load_ref[0, i, 0, 7:8, :]
+        down_ref[8 * i : 8 * i + 8, :] = load_ref[0, i, 0]
+        down_ref[64 + i : 65 + i, :] = load_ref[0, i, 1, 0:1, :]
+
+
+Facross_refE_METRIC = 72
+Facross_refE_ROWS = 104
 
 
 def gather(
@@ -299,25 +327,14 @@
             rows_ref[row : row + 2, :] = source[start + 2 * m : start + 2 * m + 2, :]
     rows_ref[30:32, :] = jnp.zeros((2, 128), F32)
     rows = rows_ref[...]
-    for face, ref in ((0, low_ref), (7, high_ref)):
-        for c in range(8):
-            ref[8 * c : 8 * c + 8, :] = load_ref[face, c]
-        ref[64:65, :] = far_below_ref[64 + face : 65 + face, :]
-        ref[65:66, :] = far_above_ref[64 + face : 65 + face, :]
+    out = Faces(low_ref, high_ref)
+    for c in range(8):
+        out.put(8 * c, 8 * c + 8, load_ref[0, c], load_ref[7, c])
+    for row, ref in ((64, far_below_ref), (65, far_above_ref)):
+        out.put(row, row + 1, ref[64:65, :], ref[71:72, :])
+    for ref in (low_ref, high_ref):
         ref[66:72, :] = jnp.zeros((6, 128), F32)
-        ref[FACE_METRIC:FACE_ROWS, :] = rows
-
-
-def send_along_z(field, extra, send_ref):
-    here = lax.axis_index("gz")
-    above = lax.rem(here + 1, N_GZ)
-    for i in range(8):
-        for chunk in range(N_GZ):
-            send_ref[chunk, i : i + 1, :] = jnp.where(
-                above == chunk, field[i][1][7:8, :], field[i][0][0:1, :]
-            )
-    for chunk in range(N_GZ):
-        send_ref[chunk, 8:16, :] = extra
+        ref[Facross_refE_METRIC:Facross_refE_ROWS, :] = rows
 
 
 def send_along_x(field, extra, send_ref):
@@ -331,15 +348,18 @@
         send_ref[chunk, 16:24, :] = extra
 
 
-def two_rows(first, second):
-    node = lax.broadcasted_iota(jnp.int32, (8, 128), 0)
-    return jnp.where(node == 0, spread(first), jnp.where(node == 1, spread(second), 0.0))
+def write_z_faces(field, low_ref, high_ref):
+    for i in range(8):
+        low_ref[i : i + 1, :] = field[i][0][0:1, :]
+        high_ref[i : i + 1, :] = field[i][-1][7:8, :]
 
 
 def begin(
-    load_ref, edge_ref, rows_ref, left_ref, right_ref, factor_ref, table_ref,
-    rhs_ref, inverse_ref, smooth_ref, applied_ref, low_ref, high_ref, send_ref,
+    load_ref, edge_ref, rows_ref, across_ref, within_ref, factor_ref, table_ref,
+    rhs_ref, inverse_ref, smooth_ref, applied_ref, across_out, within_out, send_ref,
 ):
+    left_ref, right_ref = sides(across_ref, within_ref)
+
     def edge(which):
         start = 8 * which
 
@@ -366,7 +386,7 @@
     write(smooth_ref, [row[1:7] for row in smooth])
     applied = element_apply(smooth, -3, rows_ref, table_ref)
     write(applied_ref, applied)
-    write_x_faces(applied, low_ref, high_ref)
+    write_x_faces(applied, across_out, within_out)
 
     mult = table(table_ref, "mult")
     weighted = [[rhs[i][3 + z] * (mult * float(EDGE[i])) for z in range(2)] for i in range(8)]
@@ -431,20 +451,6 @@
             send_ref[chunk, row : row + 1, :] = total
 
 
-def middle(applied_ref, received_ref, summed_ref, send_ref):
-    below, above = neighbours("gz", N_GZ)
-    field = sum_z(
-        read(applied_ref),
-        lambda i: received_ref[below, i : i + 1, :],
-        lambda i: received_ref[above, i : i + 1, :],
-    )
-    write(summed_ref, field)
-    extra = received_ref[0, 8:16, :]
-    for e in range(1, N_GZ):
-        extra = extra + received_ref[e, 8:16, :]
-    send_along_x(field, extra, send_ref)
-
-
 def x_faces_received(received_ref):
     below, above = neighbours("gx", N_GX)
     left = [received_ref[below, 8 * z : 8 * z + 8, :] for z in range(2)]
@@ -452,7 +458,8 @@
     return left, right
 
 
-def relax(step, count, applied_ref, left_ref, right_ref, rhs_ref, inverse_ref, smooth_ref, update_ref):
+def relax(step, count, applied_ref, across_ref, within_ref, rhs_ref, inverse_ref, smooth_ref, update_ref):
+    left_ref, right_ref = sides(across_ref, within_ref)
     field = sum_x(
         read(applied_ref, 0, count + 2), faces(left_ref, count + 2), faces(right_ref, count + 2)
     )
@@ -469,11 +476,11 @@
 
 
 def sweep(
-    applied_ref, left_ref, right_ref, rhs_ref, inverse_ref, smooth_ref, update_ref, rows_ref, table_ref,
+    applied_ref, across_ref, within_ref, rhs_ref, inverse_ref, smooth_ref, update_ref, rows_ref, table_ref,
     next_ref, next_update_ref, out_ref, low_ref, high_ref, *, step, count,
 ):
     smooth, update = relax(
-        step, count, applied_ref, left_ref, right_ref, rhs_ref, inverse_ref, smooth_ref, update_ref
+        step, count, applied_ref, across_ref, within_ref, rhs_ref, inverse_ref, smooth_ref, update_ref
     )
     write(next_ref, smooth)
     write(next_update_ref, update)
@@ -513,12 +520,12 @@
 
 
 def last_sweep(
-    applied_ref, left_ref, right_ref, rhs_ref, inverse_ref, smooth_ref, update_ref, rows_ref,
+    applied_ref, across_ref, within_ref, rhs_ref, inverse_ref, smooth_ref, update_ref, rows_ref,
     tree_ref, factor_ref, near_ref, table_ref,
     precond_ref, out_ref, send_ref,
 ):
     smooth, update = relax(
-        2, 2, applied_ref, left_ref, right_ref, rhs_ref, inverse_ref, smooth_ref, update_ref
+        2, 2, applied_ref, across_ref, within_ref, rhs_ref, inverse_ref, smooth_ref, update_ref
     )
     coarse = coarse_field(tree_ref, factor_ref, table_ref)
     precond = each(lambda s, c: s + c, smooth, coarse)
@@ -532,18 +539,35 @@
             start = 8 * (2 * i + z)
             first = first + near_ref[start : start + 8, :] * precond[i][z]
             second = second + applied[i][z] * precond[i][z]
-    extra = two_rows(jnp.sum(first, axis=0, keepdims=True), jnp.sum(second, axis=0, keepdims=True))
-    send_along_z(applied, extra, send_ref)
-
-
-def finish(summed_ref, received_ref, precond_ref, rhs_ref, solution_ref, residual_ref):
-    left, right = x_faces_received(received_ref)
-    image = each(wall, sum_y(sum_x(read(summed_ref), left, right)))
-    extra = received_ref[0, 16:24, :]
+    first = first + pltpu.roll(first, 64, 1)
+    second = second + pltpu.roll(second, 64, 1)
+    both = jnp.where(lane_iota() < 64, first, second)
+    send_along_x(applied, spread(jnp.sum(both, axis=0, keepdims=True)), send_ref)
+
+
+def middle(applied_ref, received_ref, summed_ref, low_ref, high_ref, send_ref):
+    field = sum_x(read(applied_ref), *x_faces_received(received_ref))
+    write(summed_ref, field)
+    write_z_faces(field, low_ref, high_ref)
+    total = received_ref[0, 16:24, :]
     for e in range(1, N_GX):
-        extra = extra + received_ref[e, 16:24, :]
-    totals = jnp.sum(extra, axis=1, keepdims=True)
-    alpha = spread(totals[0:1, :] / totals[1:2, :])
+        total = total + received_ref[e, 16:24, :]
+    send_ref[0:8, :] = total
+    send_ref[8:16, :] = total
+
+
+def finish(
+    summed_ref, before_ref, after_ref, received_ref, precond_ref, rhs_ref, solution_ref, residual_ref
+):
+    field = sum_z(
+        read(summed_ref), lambda i: before_ref[i : i + 1, :], lambda i: after_ref[i : i + 1, :]
+    )
+    image = each(wall, sum_y(field))
+    total = jnp.sum(received_ref[0:8, :] + received_ref[8:16, :], axis=0, keepdims=True)
+    lane = lax.broadcasted_iota(jnp.int32, (1, 128), 1)
+    product = jnp.sum(jnp.where(lane < 64, total, 0.0), axis=1, keepdims=True)
+    curvature = jnp.sum(jnp.where(lane < 64, 0.0, total), axis=1, keepdims=True)
+    alpha = spread(product / curvature)
     write(solution_ref, each(lambda p: alpha * p, read(precond_ref)))
     write(residual_ref, each(lambda r, a: r - alpha * a, read(rhs_ref, 2, 2), image))
 
@@ -568,31 +592,34 @@
     return lax.ppermute(value, axis, [(i, (i + distance) % count) for i in range(count)])
 
 
-def exchange(low, high, axis):
-    return shifted(high, axis, 1), shifted(low, axis, -1)
+def swap_x(across, within):
+    count = lax.axis_size("gx")
+    over = [(i, (((i - 1) % count) ^ 1) + 1) for i in range(count)]
+    over = [(i, target % count) for i, target in over]
+    inside = [(i, i ^ 1) for i in range(count)]
+    return lax.ppermute(across, "gx", over), lax.ppermute(within, "gx", inside)
 
 
 def per_device(element_rhs_load, metric, coarse_factor):
-    load = element_rhs_load.reshape(field_shape(2))
     constants = jnp.asarray(TABLE)
     factor = coarse_factor.reshape(10, 32, 16).transpose(1, 0, 2).reshape(32, 160)
     factor = jnp.pad(factor, ((0, 0), (0, 96)))
     near, up, down = run(
-        pack, [(136, 128), (80, 128), (80, 128)], load, metric.reshape(6, 16), constants
+        pack, [(136, 128), (80, 128), (80, 128)], element_rhs_load, metric
     )
     below, far_below = shifted(near, "gz", 1), shifted(up, "gz", 2)
     above, far_above = shifted(near, "gz", -1), shifted(down, "gz", -2)
     wide, edge, rows, low, high = run(
-        gather, [field_shape(8), (16, 128), (32, 128)] + [(FACE_ROWS, 128)] * 2,
+        gather, [field_shape(8), (16, 128), (32, 128)] + [(Facross_refE_ROWS, 128)] * 2,
         near, below, far_below, above, far_above,
     )
-    left, right = exchange(low, high, "gx")
+    left, right = swap_x(low, high)
     rhs, inverse, smooth, applied, low, high, send = run(
         begin, [field_shape(6)] * 3 + [field_shape(8)] + [(64, 128)] * 2 + [(N_GZ, 2, 128)],
         wide, edge, rows, left, right, factor, constants,
     )
     tree = lax.all_to_all(send, "gz", 0, 0, tiled=True)
-    left, right = exchange(low, high, "gx")
+    left, right = swap_x(low, high)
     update = smooth
     for step, count in ((0, 6), (1, 4)):
 
@@ -603,19 +630,23 @@
             stage, [field_shape(count)] * 3 + [(8 * count, 128)] * 2,
             applied, left, right, rhs, inverse, smooth, update, rows, constants,
         )
-        left, right = exchange(low, high, "gx")
+        left, right = swap_x(low, high)
         if step == 0:
             (send,) = run(lower_tree, [(N_GX, 2, 128)], tree)
             tree = lax.all_to_all(send, "gx", 0, 0, tiled=True)
     precond, applied, send = run(
-        last_sweep, [field_shape(2)] * 2 + [(N_GZ, 16, 128)],
+        last_sweep, [field_shape(2)] * 2 + [(N_GX, 24, 128)],
         applied, left, right, rhs, inverse, smooth, update, rows, tree, factor, near, constants,
     )
-    received = lax.all_to_all(send, "gz", 0, 0, tiled=True)
-    summed, send = run(middle, [field_shape(2), (N_GX, 24, 128)], applied, received)
     received = lax.all_to_all(send, "gx", 0, 0, tiled=True)
+    summed, low, high, send = run(
+        middle, [field_shape(2)] + [(8, 128)] * 2 + [(N_GZ, 128)], applied, received
+    )
+    received = lax.all_to_all(send.reshape(N_GZ, 1, 128), "gz", 0, 0, tiled=True)
+    before, after = shifted(high, "gz", 1), shifted(low, "gz", -1)
     solution_field, residual = run(
-        finish, [field_shape(2)] * 2, summed, received, precond, rhs, last=True
+        finish, [field_shape(2)] * 2,
+        summed, before, after, received.reshape(N_GZ, 128), precond, rhs, last=True,
     )
     shape = element_rhs_load.shape
     return solution_field.reshape(shape), residual.reshape(shape)

time: 129 us -> 120 us (0.930)
  blocking collectives: 43.3 us -> 15.3 us
  starting transfers between devices: 67.4 us -> 87 us
    ppermute x0 -> x8, starting transfers between devices: none -> 34.2 us  [the longest x4 21 us: swap_x(): lax.ppermute(within, 'gx', inside)]
    all_to_all x1 -> x0, blocking collectives: 23.5 us -> none  [per_device(): received = lax.all_to_all(send, 'gz', 0, 0, tiled=True)]
    ppermute x12 -> x6, starting transfers between devices: 49.3 us -> 27.9 us  [shifted(): lax.ppermute(value, axis, [(i, (i + distance) % count) for i in range(cou...]
    all_to_all x0 -> x1, starting transfers between devices: none -> 11.7 us  [per_device(): lax.all_to_all(send.reshape(N_GZ, 1, 128), 'gz', 0, 0, tiled=True)]
    ppermute x12 -> x6, waiting for transfers between devices: 9.08 us -> 2.48 us  [shifted(): lax.ppermute(value, axis, [(i, (i + distance) % count) for i in range(cou...]
    all_to_all x1, blocking collectives: 19.8 us -> 15.3 us  [per_device(): received = lax.all_to_all(send, 'gx', 0, 0, tiled=True)]
    all_to_all x1, starting transfers between devices: 8.57 us -> 4.22 us  [per_device(): tree = lax.all_to_all(send, 'gx', 0, 0, tiled=True)]
    all_to_all x0 -> x1, waiting for transfers between devices: none -> 3.31 us  [per_device(): lax.all_to_all(send.reshape(N_GZ, 1, 128), 'gz', 0, 0, tiled=True)]
  transfers between devices with their start and end apart: 14 -> 17, of which waited for: 4 -> 6; matrix products, arithmetic and copies ran while one was open for 0% -> 0% of each run, Pallas kernels for 1% -> 2%
where the time goes in v4:
time: 120 us; the launch traced here: 119 us
  starting transfers between devices  87 us (72%)
  blocking collectives  15.3 us (13%)
  waiting for transfers between devices  8.2 us (7%)
  Pallas kernels  5.89 us (5%)
  local copies, waits for them, and re-layouts  1.61 us (1%)
    ppermute x6, starting transfers between devices, shifted(): lax.ppermute(value, axis, [(i, (i + distance) % count) for i in range(cou...  27.9 us
    ppermute x4, starting transfers between devices, swap_x(): lax.ppermute(within, 'gx', inside)  21 us
    all_to_all x1, blocking collectives, per_device(): received = lax.all_to_all(send, 'gx', 0, 0, tiled=True)  15.3 us
    ppermute x4, starting transfers between devices, swap_x(): lax.ppermute(across, 'gx', over)  13.2 us
    all_to_all x1, starting transfers between devices, per_device(): lax.all_to_all(send.reshape(N_GZ, 1, 128), 'gz', 0, 0, tiled=True)  11.7 us
    all_to_all x1, starting transfers between devices, per_device(): tree = lax.all_to_all(send, 'gz', 0, 0, tiled=True)  8.96 us
    pallas_call x9, Pallas kernels, run(): pl.pallas_call(kernel, out_shape=outs, in_specs=[spec] * len(operands), o...  5.89 us
    all_to_all x1, starting transfers between devices, per_device(): tree = lax.all_to_all(send, 'gx', 0, 0, tiled=True)  4.22 us
  transfers between devices with their start and end apart: 17, of which 6 were waited for; matrix products, arithmetic and copies ran while one was open for 0% of the time, Pallas kernels for 2%

profile of v4, /device:TPU:1, one launch (start us, length us, event | category | flops | bytes accessed | tf_op | source)
XLA Modules:
  0.0 118.8 jit_solution(3017379236817358744)
XLA Ops:
  0.6 0.8 copy-done.1
  1.5 0.7 copy-done.2
  2.2 0.1 shard_map.59
  2.3 4.4 %collective-permute-start = (f32[136,128]{1,0:T(8,128)S(1)}, f32[136,128]{1,0:T(8,128)S(1)}, u32[]{:S(2)}, u32[]{:S(2)}) collective-permute-start(f32[136,128]{1,0:T(8,128)S(1)} %get-tuple-element.36.near_ref), channel_id=1, source_target_pairs={{0,1},{1,2},{2,3},{3,4},{4,5},{5,6},{6,7},{7,8},{8,9},{9,10},{10,1... | collective-permute-start | bytes 208904 | tf_op jit(solution)/shard_map/ppermute | solution.py:592
  6.7 9.5 %collective-permute-start.2 = (f32[136,128]{1,0:T(8,128)S(1)}, f32[136,128]{1,0:T(8,128)S(1)}, u32[]{:S(2)}, u32[]{:S(2)}) collective-permute-start(f32[136,128]{1,0:T(8,128)S(1)} %get-tuple-element.36.near_ref), channel_id=1, source_target_pairs={{0,15},{1,0},{2,1},{3,2},{4,3},{5,4},{6,5},{7,6},{8,7},{9,8},{10,9... | collective-permute-start | bytes 208904 | tf_op jit(solution)/shard_map/ppermute | solution.py:592
  16.2 1.9 %collective-permute-start.1 = (f32[80,128]{1,0:T(8,128)S(1)}, f32[80,128]{1,0:T(8,128)S(1)}, u32[]{:S(2)}, u32[]{:S(2)}) collective-permute-start(f32[80,128]{1,0:T(8,128)S(1)} %get-tuple-element.37), channel_id=1, source_target_pairs={{0,2},{1,3},{2,4},{3,5},{4,6},{5,7},{6,8},{7,9},{8,10},{9,11},{10,... | collective-permute-start | bytes 122888 | tf_op jit(solution)/shard_map/ppermute | solution.py:592
  18.1 0.0 copy-start.3
  18.1 5.6 %collective-permute-start.3 = (f32[80,128]{1,0:T(8,128)S(1)}, f32[80,128]{1,0:T(8,128)S(1)}, u32[]{:S(2)}, u32[]{:S(2)}) collective-permute-start(f32[80,128]{1,0:T(8,128)S(1)} %get-tuple-element.38), channel_id=1, source_target_pairs={{0,14},{1,15},{2,0},{3,1},{4,2},{5,3},{6,4},{7,5},{8,6},{9,7},{10,... | collective-permute-start | bytes 122888 | tf_op jit(solution)/shard_map/ppermute | solution.py:592
  23.7 0.0 collective-permute-done.1.far_below_ref
  23.8 1.1 collective-permute-done.3.far_above_ref
  24.8 0.0 collective-permute-done.below_ref
  24.8 0.0 collective-permute-done.2.above_ref
  24.9 0.0 copy-start
  24.9 5.3 %collective-permute-start.4 = (f32[104,128]{1,0:T(8,128)S(1)}, f32[104,128]{1,0:T(8,128)S(1)}, u32[]{:S(2)}, u32[]{:S(2)}) collective-permute-start(f32[104,128]{1,0:T(8,128)S(1)} %get-tuple-element.42), channel_id=1, source_target_pairs={{0,496},{16,32},{32,16},{48,64},{64,48},{80,96},{96,80},{112,128},... | collective-permute-start | bytes 159752 | tf_op jit(solution)/shard_map/ppermute | solution.py:600
  30.2 4.0 %collective-permute-start.5 = (f32[104,128]{1,0:T(8,128)S(1)}, f32[104,128]{1,0:T(8,128)S(1)}, u32[]{:S(2)}, u32[]{:S(2)}) collective-permute-start(f32[104,128]{1,0:T(8,128)S(1)} %get-tuple-element.43), channel_id=1, source_target_pairs={{0,16},{16,0},{32,48},{48,32},{64,80},{80,64},{96,112},{112,96},{1... | collective-permute-start | bytes 159752 | tf_op jit(solution)/shard_map/ppermute | solution.py:600
  34.2 0.1 copy.8
  34.3 0.0 collective-permute-done.4.across_ref
  34.3 0.8 collective-permute-done.5.within_ref
  35.0 1.7 %shard_map.61 = (f32[8,6,8,128]{3,2,1,0:T(8,128)S(1)}, f32[8,6,8,128]{3,2,1,0:T(8,128)S(1)}, f32[8,6,8,128]{3,2,1,0:T(8,128)S(1)}, f32[8,8,8,128]{3,2,1,0:T(8,12...) custom-call(f32[8,8,8,128]{3,2,1,0:T(8,128)S(1)} %get-tuple-element.39.load_ref, ...), custom_call_target="tpu_custom_call" | custom-call | tf_op jit(solution)/shard_map/pallas_call | solution.py:585
  36.7 9.0 %all-to-all-start = ((f32[16,2,128]{2,1,0:T(2,128)}), f32[16,2,128]{2,1,0:T(2,128)S(1)}, u32[]{:S(2)}, u32[]{:S(2)}) async-start(f32[16,2,128]{2,1,0:T(2,128)} %get-tuple-element.60), calls=%async_computation | async-start | bytes 32768 | tf_op jit(solution)/shard_map/all_to_all | solution.py:621
  45.7 2.4 %collective-permute-start.6 = (f32[64,128]{1,0:T(8,128)S(1)}, f32[64,128]{1,0:T(8,128)S(1)}, u32[]{:S(2)}, u32[]{:S(2)}) collective-permute-start(f32[64,128]{1,0:T(8,128)S(1)} %get-tuple-element.45), channel_id=1, source_target_pairs={{0,496},{16,32},{32,16},{48,64},{64,48},{80,96},{96,80},{112,128},... | collective-permute-start | bytes 98312 | tf_op jit(solution)/shard_map/ppermute | solution.py:600
  48.1 5.5 %collective-permute-start.7 = (f32[64,128]{1,0:T(8,128)S(1)}, f32[64,128]{1,0:T(8,128)S(1)}, u32[]{:S(2)}, u32[]{:S(2)}) collective-permute-start(f32[64,128]{1,0:T(8,128)S(1)} %get-tuple-element.46), channel_id=1, source_target_pairs={{0,16},{16,0},{32,48},{48,32},{64,80},{80,64},{96,112},{112,96},{1... | collective-permute-start | bytes 98312 | tf_op jit(solution)/shard_map/ppermute | solution.py:600
  53.6 0.0 collective-permute-done.6.refs_1_
  53.6 0.8 collective-permute-done.7.refs_2_
  54.4 0.7 shard_map.62
  55.1 1.9 %collective-permute-start.8 = (f32[48,128]{1,0:T(8,128)S(1)}, f32[48,128]{1,0:T(8,128)S(1)}, u32[]{:S(2)}, u32[]{:S(2)}) collective-permute-start(f32[48,128]{1,0:T(8,128)S(1)} %get-tuple-element.51), channel_id=1, source_target_pairs={{0,496},{16,32},{32,16},{48,64},{64,48},{80,96},{96,80},{112,128},... | collective-permute-start | bytes 73736 | tf_op jit(solution)/shard_map/ppermute | solution.py:600
  57.1 6.1 %collective-permute-start.9 = (f32[48,128]{1,0:T(8,128)S(1)}, f32[48,128]{1,0:T(8,128)S(1)}, u32[]{:S(2)}, u32[]{:S(2)}) collective-permute-start(f32[48,128]{1,0:T(8,128)S(1)} %get-tuple-element.52), channel_id=1, source_target_pairs={{0,16},{16,0},{32,48},{48,32},{64,80},{80,64},{96,112},{112,96},{1... | collective-permute-start | bytes 73736 | tf_op jit(solution)/shard_map/ppermute | solution.py:600
  63.1 0.0 all-to-all-done.received_ref
  63.2 0.7 shard_map.64
  63.8 4.2 %all-to-all-start.1 = ((f32[32,2,128]{2,1,0:T(2,128)}), f32[32,2,128]{2,1,0:T(2,128)S(1)}, u32[]{:S(2)}, u32[]{:S(2)}) async-start(f32[32,2,128]{2,1,0:T(2,128)} %shard_map.64), calls=%async_computation.1 | async-start | bytes 65536 | tf_op jit(solution)/shard_map/all_to_all | solution.py:636
  68.0 0.0 collective-permute-done.8.refs_1_
  68.1 0.0 collective-permute-done.9.refs_2_
  68.1 0.5 shard_map.63
  68.6 3.5 %collective-permute-start.10 = (f32[32,128]{1,0:T(8,128)S(1)}, f32[32,128]{1,0:T(8,128)S(1)}, u32[]{:S(2)}, u32[]{:S(2)}) collective-permute-start(f32[32,128]{1,0:T(8,128)S(1)} %get-tuple-element.56), channel_id=1, source_target_pairs={{0,496},{16,32},{32,16},{48,64},{64,48},{80,96},{96,80},{112,128},... | collective-permute-start | bytes 49160 | tf_op jit(solution)/shard_map/ppermute | solution.py:600
  72.2 5.5 %collective-permute-start.11 = (f32[32,128]{1,0:T(8,128)S(1)}, f32[32,128]{1,0:T(8,128)S(1)}, u32[]{:S(2)}, u32[]{:S(2)}) collective-permute-start(f32[32,128]{1,0:T(8,128)S(1)} %get-tuple-element.57), channel_id=1, source_target_pairs={{0,16},{16,0},{32,48},{48,32},{64,80},{80,64},{96,112},{112,96},{1... | collective-permute-start | bytes 49160 | tf_op jit(solution)/shard_map/ppermute | solution.py:600
  77.6 0.0 collective-permute-done.10.across_ref
  77.6 0.8 collective-permute-done.11.within_ref
  78.5 0.0 all-to-all-done.1.tree_ref
  78.5 0.8 shard_map.65
  79.2 15.3 %all_to_all.20.received_ref = f32[32,24,128]{2,1,0:T(8,128)S(1)} all-to-all(f32[32,24,128]{2,1,0:T(8,128)S(1)} %get-tuple-element.62), channel_id=1, replica_groups=mesh['gx'=32,'gz'=16] {'gx'}, dimensions={0} | all-to-all | bytes 786432 | tf_op jit(solution)/shard_map/all_to_all | solution.py:641
  94.5 0.6 shard_map.66
  95.1 11.7 %all-to-all-start.3 = ((f32[16,1,128]{2,1,0:T(1,128)}), f32[16,1,128]{2,1,0:T(1,128)S(1)}, u32[]{:S(2)}, u32[]{:S(2)}) async-start(f32[16,1,128]{2,1,0:T(1,128)} %bitcast.4), calls=%async_computation.3 | async-start | bytes 16384 | tf_op jit(solution)/shard_map/all_to_all | solution.py:645
  106.9 3.3 %collective-permute-start.12 = (f32[8,128]{1,0:T(8,128)S(1)}, f32[8,128]{1,0:T(8,128)S(1)}, u32[]{:S(2)}, u32[]{:S(2)}) collective-permute-start(f32[8,128]{1,0:T(8,128)S(1)} %get-tuple-element.64), channel_id=1, source_target_pairs={{0,1},{1,2},{2,3},{3,4},{4,5},{5,6},{6,7},{7,8},{8,9},{9,10},{10,1... | collective-permute-start | bytes 12296 | tf_op jit(solution)/shard_map/ppermute | solution.py:592
  110.1 3.2 %collective-permute-start.13 = (f32[8,128]{1,0:T(8,128)S(1)}, f32[8,128]{1,0:T(8,128)S(1)}, u32[]{:S(2)}, u32[]{:S(2)}) collective-permute-start(f32[8,128]{1,0:T(8,128)S(1)} %get-tuple-element.65), channel_id=1, source_target_pairs={{0,15},{1,0},{2,1},{3,2},{4,3},{5,4},{6,5},{7,6},{8,7},{9,8},{10,9... | collective-permute-start | bytes 12296 | tf_op jit(solution)/shard_map/ppermute | solution.py:592
  113.4 0.0 collective-permute-done.12.before_ref
  113.4 1.4 %collective-permute-done.13.after_ref = f32[8,128]{1,0:T(8,128)S(1)} collective-permute-done((f32[8,128]{1,0:T(8,128)S(1)}, f32[8,128]{1,0:T(8,128)S(1)}, u32[]{:S(2)}, u32[]{:S(2)}) %collective-permute-start.13) | collective-permute-done | bytes 4128 | tf_op jit(solution)/shard_map/ppermute | solution.py:592
  114.8 3.3 %all-to-all-done.3 = f32[16,1,128]{2,1,0:T(1,128)S(1)} async-done(((f32[16,1,128]{2,1,0:T(1,128)}), f32[16,1,128]{2,1,0:T(1,128)S(1)}, u32[]{:S(2)}, u32[]{:S(2)}) %all-to-all-start.3) | async-done | bytes 8224 | tf_op jit(solution)/shard_map/all_to_all | solution.py:645
  118.1 0.8 shard_map.67
  (6 shorter events, 0.1 us)
Async XLA Ops:
  0.6 0.8 copy-start.1
  1.5 0.7 copy-start.2
  2.3 22.5 %collective-permute-start = (f32[136,128]{1,0:T(8,128)S(1)}, f32[136,128]{1,0:T(8,128)S(1)}, u32[]{:S(2)}, u32[]{:S(2)}) collective-permute-start(f32[136,128]{1,0:T(8,128)S(1)} %get-tuple-element.36.near_ref), channel_id=1, source_target_pairs={{0,1},{1,2},{2,3},{3,4},{4,5},{5,6},{6,7},{7,8},{8,9},{9,10},{10,1... | collective-permute-start | bytes 208904 | tf_op jit(solution)/shard_map/ppermute | solution.py:592
  6.7 18.1 %collective-permute-start.2 = (f32[136,128]{1,0:T(8,128)S(1)}, f32[136,128]{1,0:T(8,128)S(1)}, u32[]{:S(2)}, u32[]{:S(2)}) collective-permute-start(f32[136,128]{1,0:T(8,128)S(1)} %get-tuple-element.36.near_ref), channel_id=1, source_target_pairs={{0,15},{1,0},{2,1},{3,2},{4,3},{5,4},{6,5},{7,6},{8,7},{9,8},{10,9... | collective-permute-start | bytes 208904 | tf_op jit(solution)/shard_map/ppermute | solution.py:592
  16.2 7.6 %collective-permute-start.1 = (f32[80,128]{1,0:T(8,128)S(1)}, f32[80,128]{1,0:T(8,128)S(1)}, u32[]{:S(2)}, u32[]{:S(2)}) collective-permute-start(f32[80,128]{1,0:T(8,128)S(1)} %get-tuple-element.37), channel_id=1, source_target_pairs={{0,2},{1,3},{2,4},{3,5},{4,6},{5,7},{6,8},{7,9},{8,10},{9,11},{10,... | collective-permute-start | bytes 122888 | tf_op jit(solution)/shard_map/ppermute | solution.py:592
  18.1 16.1 %copy-start.3 = (f32[1,1,10,32,16]{3,4,2,1,0:T(8,128)S(1)}, f32[1,1,10,32,16]{3,4,2,1,0:T(8,128)}, u32[]{:S(2)}) copy-start(f32[1,1,10,32,16]{3,4,2,1,0:T(8,128)} %param.6) | copy-start | bytes 61444
  18.1 6.7 %collective-permute-start.3 = (f32[80,128]{1,0:T(8,128)S(1)}, f32[80,128]{1,0:T(8,128)S(1)}, u32[]{:S(2)}, u32[]{:S(2)}) collective-permute-start(f32[80,128]{1,0:T(8,128)S(1)} %get-tuple-element.38), channel_id=1, source_target_pairs={{0,14},{1,15},{2,0},{3,1},{4,2},{5,3},{6,4},{7,5},{8,6},{9,7},{10,... | collective-permute-start | bytes 122888 | tf_op jit(solution)/shard_map/ppermute | solution.py:592
  24.9 10.2 %copy-start = (f32[240,128]{1,0:T(8,128)S(1)}, f32[240,128]{1,0:T(8,128)}, u32[]{:S(2)}) copy-start(f32[240,128]{1,0:T(8,128)} %constant.5.clone.table_ref.refs_8_) | copy-start | bytes 368644
  24.9 9.4 %collective-permute-start.4 = (f32[104,128]{1,0:T(8,128)S(1)}, f32[104,128]{1,0:T(8,128)S(1)}, u32[]{:S(2)}, u32[]{:S(2)}) collective-permute-start(f32[104,128]{1,0:T(8,128)S(1)} %get-tuple-element.42), channel_id=1, source_target_pairs={{0,496},{16,32},{32,16},{48,64},{64,48},{80,96},{96,80},{112,128},... | collective-permute-start | bytes 159752 | tf_op jit(solution)/shard_map/ppermute | solution.py:600
  30.2 4.8 %collective-permute-start.5 = (f32[104,128]{1,0:T(8,128)S(1)}, f32[104,128]{1,0:T(8,128)S(1)}, u32[]{:S(2)}, u32[]{:S(2)}) collective-permute-start(f32[104,128]{1,0:T(8,128)S(1)} %get-tuple-element.43), channel_id=1, source_target_pairs={{0,16},{16,0},{32,48},{48,32},{64,80},{80,64},{96,112},{112,96},{1... | collective-permute-start | bytes 159752 | tf_op jit(solution)/shard_map/ppermute | solution.py:600
  36.7 26.4 %all-to-all-start = ((f32[16,2,128]{2,1,0:T(2,128)}), f32[16,2,128]{2,1,0:T(2,128)S(1)}, u32[]{:S(2)}, u32[]{:S(2)}) async-start(f32[16,2,128]{2,1,0:T(2,128)} %get-tuple-element.60), calls=%async_computation | async-start | bytes 32768 | tf_op jit(solution)/shard_map/all_to_all | solution.py:621
  45.7 7.9 %collective-permute-start.6 = (f32[64,128]{1,0:T(8,128)S(1)}, f32[64,128]{1,0:T(8,128)S(1)}, u32[]{:S(2)}, u32[]{:S(2)}) collective-permute-start(f32[64,128]{1,0:T(8,128)S(1)} %get-tuple-element.45), channel_id=1, source_target_pairs={{0,496},{16,32},{32,16},{48,64},{64,48},{80,96},{96,80},{112,128},... | collective-permute-start | bytes 98312 | tf_op jit(solution)/shard_map/ppermute | solution.py:600
  48.1 6.3 %collective-permute-start.7 = (f32[64,128]{1,0:T(8,128)S(1)}, f32[64,128]{1,0:T(8,128)S(1)}, u32[]{:S(2)}, u32[]{:S(2)}) collective-permute-start(f32[64,128]{1,0:T(8,128)S(1)} %get-tuple-element.46), channel_id=1, source_target_pairs={{0,16},{16,0},{32,48},{48,32},{64,80},{80,64},{96,112},{112,96},{1... | collective-permute-start | bytes 98312 | tf_op jit(solution)/shard_map/ppermute | solution.py:600
  55.1 12.9 %collective-permute-start.8 = (f32[48,128]{1,0:T(8,128)S(1)}, f32[48,128]{1,0:T(8,128)S(1)}, u32[]{:S(2)}, u32[]{:S(2)}) collective-permute-start(f32[48,128]{1,0:T(8,128)S(1)} %get-tuple-element.51), channel_id=1, source_target_pairs={{0,496},{16,32},{32,16},{48,64},{64,48},{80,96},{96,80},{112,128},... | collective-permute-start | bytes 73736 | tf_op jit(solution)/shard_map/ppermute | solution.py:600
  57.1 11.0 %collective-permute-start.9 = (f32[48,128]{1,0:T(8,128)S(1)}, f32[48,128]{1,0:T(8,128)S(1)}, u32[]{:S(2)}, u32[]{:S(2)}) collective-permute-start(f32[48,128]{1,0:T(8,128)S(1)} %get-tuple-element.52), channel_id=1, source_target_pairs={{0,16},{16,0},{32,48},{48,32},{64,80},{80,64},{96,112},{112,96},{1... | collective-permute-start | bytes 73736 | tf_op jit(solution)/shard_map/ppermute | solution.py:600
  63.8 14.6 %all-to-all-start.1 = ((f32[32,2,128]{2,1,0:T(2,128)}), f32[32,2,128]{2,1,0:T(2,128)S(1)}, u32[]{:S(2)}, u32[]{:S(2)}) async-start(f32[32,2,128]{2,1,0:T(2,128)} %shard_map.64), calls=%async_computation.1 | async-start | bytes 65536 | tf_op jit(solution)/shard_map/all_to_all | solution.py:636
  68.6 9.0 %collective-permute-start.10 = (f32[32,128]{1,0:T(8,128)S(1)}, f32[32,128]{1,0:T(8,128)S(1)}, u32[]{:S(2)}, u32[]{:S(2)}) collective-permute-start(f32[32,128]{1,0:T(8,128)S(1)} %get-tuple-element.56), channel_id=1, source_target_pairs={{0,496},{16,32},{32,16},{48,64},{64,48},{80,96},{96,80},{112,128},... | collective-permute-start | bytes 49160 | tf_op jit(solution)/shard_map/ppermute | solution.py:600
  72.2 6.3 %collective-permute-start.11 = (f32[32,128]{1,0:T(8,128)S(1)}, f32[32,128]{1,0:T(8,128)S(1)}, u32[]{:S(2)}, u32[]{:S(2)}) collective-permute-start(f32[32,128]{1,0:T(8,128)S(1)} %get-tuple-element.57), channel_id=1, source_target_pairs={{0,16},{16,0},{32,48},{48,32},{64,80},{80,64},{96,112},{112,96},{1... | collective-permute-start | bytes 49160 | tf_op jit(solution)/shard_map/ppermute | solution.py:600
  95.1 23.0 %all-to-all-start.3 = ((f32[16,1,128]{2,1,0:T(1,128)}), f32[16,1,128]{2,1,0:T(1,128)S(1)}, u32[]{:S(2)}, u32[]{:S(2)}) async-start(f32[16,1,128]{2,1,0:T(1,128)} %bitcast.4), calls=%async_computation.3 | async-start | bytes 16384 | tf_op jit(solution)/shard_map/all_to_all | solution.py:645
  106.9 6.5 %collective-permute-start.12 = (f32[8,128]{1,0:T(8,128)S(1)}, f32[8,128]{1,0:T(8,128)S(1)}, u32[]{:S(2)}, u32[]{:S(2)}) collective-permute-start(f32[8,128]{1,0:T(8,128)S(1)} %get-tuple-element.64), channel_id=1, source_target_pairs={{0,1},{1,2},{2,3},{3,4},{4,5},{5,6},{6,7},{7,8},{8,9},{9,10},{10,1... | collective-permute-start | bytes 12296 | tf_op jit(solution)/shard_map/ppermute | solution.py:592
  110.1 4.6 %collective-permute-start.13 = (f32[8,128]{1,0:T(8,128)S(1)}, f32[8,128]{1,0:T(8,128)S(1)}, u32[]{:S(2)}, u32[]{:S(2)}) collective-permute-start(f32[8,128]{1,0:T(8,128)S(1)} %get-tuple-element.65), channel_id=1, source_target_pairs={{0,15},{1,0},{2,1},{3,2},{4,3},{5,4},{6,5},{7,6},{8,7},{9,8},{10,9... | collective-permute-start | bytes 12296 | tf_op jit(solution)/shard_map/ppermute | solution.py:592

commit v5 on v4

--- a/solution.py
+++ b/solution.py
@@ -67,7 +67,6 @@
 ALONG_X = np.stack([np.sin(np.pi * mode * positions(1)) for mode in (1, 2)])
 ALONG_Z = np.stack([np.sin(np.pi * mode * positions(2)) for mode in (1, 2)])
 ALONG_Y = np.stack([np.sin(np.pi * mode * positions(16)) for mode in range(1, 9)])
-EDGE = np.array([0.5] + [1.0] * 6 + [0.5])
 
 
 def build_tables():
@@ -76,9 +75,6 @@
     w_j = WEIGHTS[:, None]
     k_j = KDIAG[:, None]
     ones = np.ones((1, 128))
-    across = np.ones(128)
-    across[8::8] = 0.5
-    across[7:127:8] = 0.5
     pieces = {
         "stiff": np.kron(np.eye(16), STIFF),
         "ww": w_j * w_l,
@@ -86,7 +82,6 @@
         "wk": w_j * k_l,
         "wl": np.ones((8, 1)) * w_l,
         "wj": w_j * ones,
-        "mult": EDGE[:, None] * across[None, :],
         "modes": np.tile(ALONG_Y, (4, 1)),
     }
     for b in range(2):
@@ -337,26 +332,72 @@
         ref[Facross_refE_METRIC:Facross_refE_ROWS, :] = rows
 
 
-def send_along_x(field, extra, send_ref):
+def with_sums(face, first, second):
+    lane = lane_iota()
+    return jnp.where(lane == 0, first, jnp.where(lane == 127, second, face))
+
+
+def send_along_x(field, first, second, send_ref):
     here = lax.axis_index("gx")
     above = lax.rem(here + 1, N_GX)
+    low = [with_sums(field[0][0], first, second), field[0][1]]
+    high = [with_sums(field[7][0], first, second), field[7][1]]
     for chunk in range(N_GX):
         for z in range(2):
-            send_ref[chunk, 8 * z : 8 * z + 8, :] = jnp.where(
-                above == chunk, field[7][z], field[0][z]
+            send_ref[chunk, 8 * z : 8 * z + 8, :] = jnp.where(above == chunk, high[z], low[z])
+
+
+def send_along_z(field, sums, send_ref):
+    here = lax.axis_index("gz")
+    above = lax.rem(here + 1, N_GZ)
+    node = lax.broadcasted_iota(jnp.int32, (8, 128), 0)
+    low = high = jnp.zeros((8, 128), F32)
+    for i in range(8):
+        low = jnp.where(node == i, spread(field[i][0][0:1, :]), low)
+        high = jnp.where(node == i, spread(field[i][1][7:8, :]), high)
+    low, high = with_sums(low, sums, sums), with_sums(high, sums, sums)
+    for chunk in range(N_GZ):
+        send_ref[chunk] = jnp.where(above == chunk, high, low)
+
+
+def coarse_start(load_ref, factor_ref, table_ref, send_ref):
+    parts = []
+    load = [[wall(load_ref[0, i, z]) for z in range(2)] for i in range(8)]
+    for a in range(2):
+        along_x = []
+        for z in range(2):
+            total = float(ALONG_X[a, 0]) * load[0][z]
+            for i in range(1, 8):
+                total = total + float(ALONG_X[a, i]) * load[i][z]
+            along_x.append(total)
+        for b in range(2):
+            both = (
+                table(table_ref, f"bz{b}0") * along_x[0] + table(table_ref, f"bz{b}1") * along_x[1]
             )
-        send_ref[chunk, 16:24, :] = extra
-
-
-def write_z_faces(field, low_ref, high_ref):
-    for i in range(8):
-        low_ref[i : i + 1, :] = field[i][0][0:1, :]
-        high_ref[i : i + 1, :] = field[i][-1][7:8, :]
+            parts.append(jnp.sum(both, axis=0, keepdims=True))
+    node = lax.broadcasted_iota(jnp.int32, (8, 128), 0)
+    stacked = jnp.zeros((8, 128), F32)
+    for index, part in enumerate(parts):
+        stacked = jnp.where(node == index, spread(part), stacked)
+    modes = lax.dot_general(
+        stacked, table(table_ref, "modes"), (((1,), (1,)), ((), ())),
+        precision=HIGHEST, preferred_element_type=F32,
+    )
+    owner = lax.broadcasted_iota(jnp.int32, (8, 32), 1) // 8
+    row = lax.broadcasted_iota(jnp.int32, (8, 32), 0)
+    coarse_rhs = jnp.sum(jnp.where(owner == row, modes, 0.0), axis=0, keepdims=True)
+    own = jnp.dot(
+        jnp.broadcast_to(coarse_rhs, (8, 32)), factor_ref[...],
+        precision=HIGHEST, preferred_element_type=F32,
+    )
+    for chunk in range(N_GZ):
+        send_ref[chunk, 0:1, :] = own[0:1, 0:128]
+        send_ref[chunk, 1:2, :] = own[0:1, 128:256]
 
 
 def begin(
-    load_ref, edge_ref, rows_ref, across_ref, within_ref, factor_ref, table_ref,
-    rhs_ref, inverse_ref, smooth_ref, applied_ref, across_out, within_out, send_ref,
+    load_ref, edge_ref, rows_ref, across_ref, within_ref, table_ref,
+    rhs_ref, inverse_ref, smooth_ref, applied_ref, across_out, within_out,
 ):
     left_ref, right_ref = sides(across_ref, within_ref)
 
@@ -388,40 +429,6 @@
     write(applied_ref, applied)
     write_x_faces(applied, across_out, within_out)
 
-    mult = table(table_ref, "mult")
-    weighted = [[rhs[i][3 + z] * (mult * float(EDGE[i])) for z in range(2)] for i in range(8)]
-    parts = []
-    for a in range(2):
-        along_x = []
-        for z in range(2):
-            total = float(ALONG_X[a, 0]) * weighted[0][z]
-            for i in range(1, 8):
-                total = total + float(ALONG_X[a, i]) * weighted[i][z]
-            along_x.append(total)
-        for b in range(2):
-            both = (
-                table(table_ref, f"bz{b}0") * along_x[0] + table(table_ref, f"bz{b}1") * along_x[1]
-            )
-            parts.append(jnp.sum(both, axis=0, keepdims=True))
-    node = lax.broadcasted_iota(jnp.int32, (8, 128), 0)
-    stacked = jnp.zeros((8, 128), F32)
-    for index, part in enumerate(parts):
-        stacked = jnp.where(node == index, spread(part), stacked)
-    modes = lax.dot_general(
-        stacked, table(table_ref, "modes"), (((1,), (1,)), ((), ())),
-        precision=HIGHEST, preferred_element_type=F32,
-    )
-    owner = lax.broadcasted_iota(jnp.int32, (8, 32), 1) // 8
-    row = lax.broadcasted_iota(jnp.int32, (8, 32), 0)
-    coarse_rhs = jnp.sum(jnp.where(owner == row, modes, 0.0), axis=0, keepdims=True)
-    own = jnp.dot(
-        jnp.broadcast_to(coarse_rhs, (8, 32)), factor_ref[...],
-        precision=HIGHEST, preferred_element_type=F32,
-    )
-    for chunk in range(N_GZ):
-        send_ref[chunk, 0:1, :] = own[0:1, 0:128]
-        send_ref[chunk, 1:2, :] = own[0:1, 128:256]
-
 
 def level_of_lane(first):
     return first + lax.broadcasted_iota(jnp.int32, (1, 128), 1) // 16
@@ -539,35 +546,36 @@
             start = 8 * (2 * i + z)
             first = first + near_ref[start : start + 8, :] * precond[i][z]
             second = second + applied[i][z] * precond[i][z]
-    first = first + pltpu.roll(first, 64, 1)
-    second = second + pltpu.roll(second, 64, 1)
-    both = jnp.where(lane_iota() < 64, first, second)
-    send_along_x(applied, spread(jnp.sum(both, axis=0, keepdims=True)), send_ref)
-
-
-def middle(applied_ref, received_ref, summed_ref, low_ref, high_ref, send_ref):
+    send_along_x(
+        applied,
+        jnp.sum(first, axis=1, keepdims=True),
+        jnp.sum(second, axis=1, keepdims=True),
+        send_ref,
+    )
+
+
+def middle(applied_ref, received_ref, summed_ref, send_ref):
     field = sum_x(read(applied_ref), *x_faces_received(received_ref))
     write(summed_ref, field)
-    write_z_faces(field, low_ref, high_ref)
-    total = received_ref[0, 16:24, :]
+    sums = received_ref[0, 0:8, :]
     for e in range(1, N_GX):
-        total = total + received_ref[e, 16:24, :]
-    send_ref[0:8, :] = total
-    send_ref[8:16, :] = total
-
-
-def finish(
-    summed_ref, before_ref, after_ref, received_ref, precond_ref, rhs_ref, solution_ref, residual_ref
-):
+        sums = sums + received_ref[e, 0:8, :]
+    send_along_z(field, sums, send_ref)
+
+
+def finish(summed_ref, received_ref, precond_ref, rhs_ref, solution_ref, residual_ref):
+    below, above = neighbours("gz", N_GZ)
     field = sum_z(
-        read(summed_ref), lambda i: before_ref[i : i + 1, :], lambda i: after_ref[i : i + 1, :]
+        read(summed_ref),
+        lambda i: received_ref[below, i : i + 1, :],
+        lambda i: received_ref[above, i : i + 1, :],
     )
     image = each(wall, sum_y(field))
-    total = jnp.sum(received_ref[0:8, :] + received_ref[8:16, :], axis=0, keepdims=True)
-    lane = lax.broadcasted_iota(jnp.int32, (1, 128), 1)
-    product = jnp.sum(jnp.where(lane < 64, total, 0.0), axis=1, keepdims=True)
-    curvature = jnp.sum(jnp.where(lane < 64, 0.0, total), axis=1, keepdims=True)
-    alpha = spread(product / curvature)
+    sums = received_ref[0]
+    for e in range(1, N_GZ):
+        sums = sums + received_ref[e]
+    sums = jnp.sum(sums, axis=0, keepdims=True)
+    alpha = spread(sums[:, 0:1] / sums[:, 127:128])
     write(solution_ref, each(lambda p: alpha * p, read(precond_ref)))
     write(residual_ref, each(lambda r, a: r - alpha * a, read(rhs_ref, 2, 2), image))
 
@@ -604,6 +612,8 @@
     constants = jnp.asarray(TABLE)
     factor = coarse_factor.reshape(10, 32, 16).transpose(1, 0, 2).reshape(32, 160)
     factor = jnp.pad(factor, ((0, 0), (0, 96)))
+    (send,) = run(coarse_start, [(N_GZ, 2, 128)], element_rhs_load, factor, constants)
+    tree = lax.all_to_all(send, "gz", 0, 0, tiled=True)
     near, up, down = run(
         pack, [(136, 128), (80, 128), (80, 128)], element_rhs_load, metric
     )
@@ -614,12 +624,13 @@
         near, below, far_below, above, far_above,
     )
     left, right = swap_x(low, high)
-    rhs, inverse, smooth, applied, low, high, send = run(
-        begin, [field_shape(6)] * 3 + [field_shape(8)] + [(64, 128)] * 2 + [(N_GZ, 2, 128)],
-        wide, edge, rows, left, right, factor, constants,
-    )
-    tree = lax.all_to_all(send, "gz", 0, 0, tiled=True)
+    rhs, inverse, smooth, applied, low, high = run(
+        begin, [field_shape(6)] * 3 + [field_shape(8)] + [(64, 128)] * 2,
+        wide, edge, rows, left, right, constants,
+    )
     left, right = swap_x(low, high)
+    (send,) = run(lower_tree, [(N_GX, 2, 128)], tree)
+    tree = lax.all_to_all(send, "gx", 0, 0, tiled=True)
     update = smooth
     for step, count in ((0, 6), (1, 4)):
 
@@ -631,22 +642,15 @@
             applied, left, right, rhs, inverse, smooth, update, rows, constants,
         )
         left, right = swap_x(low, high)
-        if step == 0:
-            (send,) = run(lower_tree, [(N_GX, 2, 128)], tree)
-            tree = lax.all_to_all(send, "gx", 0, 0, tiled=True)
     precond, applied, send = run(
-        last_sweep, [field_shape(2)] * 2 + [(N_GX, 24, 128)],
+        last_sweep, [field_shape(2)] * 2 + [(N_GX, 16, 128)],
         applied, left, right, rhs, inverse, smooth, update, rows, tree, factor, near, constants,
     )
     received = lax.all_to_all(send, "gx", 0, 0, tiled=True)
-    summed, low, high, send = run(
-        middle, [field_shape(2)] + [(8, 128)] * 2 + [(N_GZ, 128)], applied, received
-    )
-    received = lax.all_to_all(send.reshape(N_GZ, 1, 128), "gz", 0, 0, tiled=True)
-    before, after = shifted(high, "gz", 1), shifted(low, "gz", -1)
+    summed, send = run(middle, [field_shape(2), (N_GZ, 8, 128)], applied, received)
+    received = lax.all_to_all(send, "gz", 0, 0, tiled=True)
     solution_field, residual = run(
-        finish, [field_shape(2)] * 2,
-        summed, before, after, received.reshape(N_GZ, 128), precond, rhs, last=True,
+        finish, [field_shape(2)] * 2, summed, received, precond, rhs, last=True
     )
     shape = element_rhs_load.shape
     return solution_field.reshape(shape), residual.reshape(shape)

time: 120 us -> 116 us (0.967)
  blocking collectives: 15.3 us -> 37.1 us
  starting transfers between devices: 87 us -> 67.3 us
  waiting for transfers between devices: 8.2 us -> 2.72 us
    all_to_all x0 -> x1, blocking collectives: none -> 23.1 us  [per_device(): received = lax.all_to_all(send, 'gz', 0, 0, tiled=True)]
    all_to_all x1 -> x0, starting transfers between devices: 11.7 us -> none  [per_device(): lax.all_to_all(send.reshape(N_GZ, 1, 128), 'gz', 0, 0, tiled=True)]
    ppermute x6 -> x4, starting transfers between devices: 27.9 us -> 21.4 us  [shifted(): lax.ppermute(value, axis, [(i, (i + distance) % count) for i in range(cou...]
    all_to_all x1 -> x0, waiting for transfers between devices: 3.31 us -> none  [per_device(): lax.all_to_all(send.reshape(N_GZ, 1, 128), 'gz', 0, 0, tiled=True)]
    ppermute x4, starting transfers between devices: 21 us -> 19.6 us  [swap_x(): lax.ppermute(within, 'gx', inside)]
    ppermute x6 -> x4, waiting for transfers between devices: 2.48 us -> 1.08 us  [shifted(): lax.ppermute(value, axis, [(i, (i + distance) % count) for i in range(cou...]
    all_to_all x1, blocking collectives: 15.3 us -> 14 us  [per_device(): received = lax.all_to_all(send, 'gx', 0, 0, tiled=True)]
    pallas_call x9 -> x10, Pallas kernels: 5.89 us -> 5.52 us  [run(): pl.pallas_call(kernel, out_shape=outs, in_specs=[spec] * len(operands), o...]
  transfers between devices with their start and end apart: 17 -> 14, of which waited for: 6 -> 3; matrix products, arithmetic and copies ran while one was open for 0% -> 0% of each run, Pallas kernels for 2% -> 3%
where the time goes in v5:
time: 116 us; the launch traced here: 115 us
  starting transfers between devices  67.3 us (58%)
  blocking collectives  37.1 us (32%)
  Pallas kernels  5.52 us (5%)
  waiting for transfers between devices  2.72 us (2%)
  local copies, waits for them, and re-layouts  1.61 us (1%)
    all_to_all x1, blocking collectives, per_device(): received = lax.all_to_all(send, 'gz', 0, 0, tiled=True)  23.1 us
    ppermute x4, starting transfers between devices, shifted(): lax.ppermute(value, axis, [(i, (i + distance) % count) for i in range(cou...  21.4 us
    ppermute x4, starting transfers between devices, swap_x(): lax.ppermute(within, 'gx', inside)  19.6 us
    all_to_all x1, blocking collectives, per_device(): received = lax.all_to_all(send, 'gx', 0, 0, tiled=True)  14 us
    ppermute x4, starting transfers between devices, swap_x(): lax.ppermute(across, 'gx', over)  13.2 us
    all_to_all x1, starting transfers between devices, per_device(): tree = lax.all_to_all(send, 'gz', 0, 0, tiled=True)  8.96 us
    pallas_call x10, Pallas kernels, run(): pl.pallas_call(kernel, out_shape=outs, in_specs=[spec] * len(operands), o...  5.52 us
    all_to_all x1, starting transfers between devices, per_device(): tree = lax.all_to_all(send, 'gx', 0, 0, tiled=True)  4.21 us
  transfers between devices with their start and end apart: 14, of which 3 were waited for; matrix products, arithmetic and copies ran while one was open for 0% of the time, Pallas kernels for 3%

profile of v5, /device:TPU:1, one launch (start us, length us, event | category | flops | bytes accessed | tf_op | source)
XLA Modules:
  0.0 115.2 jit_solution(3724682458923228722)
XLA Ops:
  0.6 0.0 copy-start.1
  0.6 0.8 copy-done.1
  1.5 0.0 copy-start.2
  1.5 0.7 copy-done.2
  2.2 0.1 shard_map.59
  2.3 4.4 %collective-permute-start = (f32[136,128]{1,0:T(8,128)S(1)}, f32[136,128]{1,0:T(8,128)S(1)}, u32[]{:S(2)}, u32[]{:S(2)}) collective-permute-start(f32[136,128]{1,0:T(8,128)S(1)} %get-tuple-element.33.near_ref), channel_id=1, source_target_pairs={{0,1},{1,2},{2,3},{3,4},{4,5},{5,6},{6,7},{7,8},{8,9},{9,10},{10,1... | collective-permute-start | bytes 208904 | tf_op jit(solution)/shard_map/ppermute | solution.py:600
  6.7 9.5 %collective-permute-start.2 = (f32[136,128]{1,0:T(8,128)S(1)}, f32[136,128]{1,0:T(8,128)S(1)}, u32[]{:S(2)}, u32[]{:S(2)}) collective-permute-start(f32[136,128]{1,0:T(8,128)S(1)} %get-tuple-element.33.near_ref), channel_id=1, source_target_pairs={{0,15},{1,0},{2,1},{3,2},{4,3},{5,4},{6,5},{7,6},{8,7},{9,8},{10,9... | collective-permute-start | bytes 208904 | tf_op jit(solution)/shard_map/ppermute | solution.py:600
  16.2 1.9 %collective-permute-start.1 = (f32[80,128]{1,0:T(8,128)S(1)}, f32[80,128]{1,0:T(8,128)S(1)}, u32[]{:S(2)}, u32[]{:S(2)}) collective-permute-start(f32[80,128]{1,0:T(8,128)S(1)} %get-tuple-element.34), channel_id=1, source_target_pairs={{0,2},{1,3},{2,4},{3,5},{4,6},{5,7},{6,8},{7,9},{8,10},{9,11},{10,... | collective-permute-start | bytes 122888 | tf_op jit(solution)/shard_map/ppermute | solution.py:600
  18.1 0.0 copy-start.3
  18.1 5.6 %collective-permute-start.3 = (f32[80,128]{1,0:T(8,128)S(1)}, f32[80,128]{1,0:T(8,128)S(1)}, u32[]{:S(2)}, u32[]{:S(2)}) collective-permute-start(f32[80,128]{1,0:T(8,128)S(1)} %get-tuple-element.35), channel_id=1, source_target_pairs={{0,14},{1,15},{2,0},{3,1},{4,2},{5,3},{6,4},{7,5},{8,6},{9,7},{10,... | collective-permute-start | bytes 122888 | tf_op jit(solution)/shard_map/ppermute | solution.py:600
  23.7 0.0 collective-permute-done.1.far_below_ref
  23.8 1.1 collective-permute-done.3.far_above_ref
  24.8 0.0 collective-permute-done.below_ref
  24.8 0.0 collective-permute-done.2.above_ref
  24.9 0.0 copy-start
  24.9 5.3 %collective-permute-start.4 = (f32[104,128]{1,0:T(8,128)S(1)}, f32[104,128]{1,0:T(8,128)S(1)}, u32[]{:S(2)}, u32[]{:S(2)}) collective-permute-start(f32[104,128]{1,0:T(8,128)S(1)} %get-tuple-element.39), channel_id=1, source_target_pairs={{0,496},{16,32},{32,16},{48,64},{64,48},{80,96},{96,80},{112,128},... | collective-permute-start | bytes 159752 | tf_op jit(solution)/shard_map/ppermute | solution.py:608
  30.2 4.0 %collective-permute-start.5 = (f32[104,128]{1,0:T(8,128)S(1)}, f32[104,128]{1,0:T(8,128)S(1)}, u32[]{:S(2)}, u32[]{:S(2)}) collective-permute-start(f32[104,128]{1,0:T(8,128)S(1)} %get-tuple-element.40), channel_id=1, source_target_pairs={{0,16},{16,0},{32,48},{48,32},{64,80},{80,64},{96,112},{112,96},{1... | collective-permute-start | bytes 159752 | tf_op jit(solution)/shard_map/ppermute | solution.py:608
  34.2 0.0 copy-done.3
  34.2 0.1 copy.7
  34.3 0.0 copy-done
  34.3 0.9 shard_map.64
  35.2 9.0 %all-to-all-start = ((f32[16,2,128]{2,1,0:T(2,128)}), f32[16,2,128]{2,1,0:T(2,128)S(1)}, u32[]{:S(2)}, u32[]{:S(2)}) async-start(f32[16,2,128]{2,1,0:T(2,128)} %shard_map.64), calls=%async_computation | async-start | bytes 32768 | tf_op jit(solution)/shard_map/all_to_all | solution.py:616
  44.2 0.0 collective-permute-done.4.across_ref
  44.2 0.0 collective-permute-done.5.within_ref
  44.2 0.9 shard_map.61
  45.1 2.4 %collective-permute-start.6 = (f32[64,128]{1,0:T(8,128)S(1)}, f32[64,128]{1,0:T(8,128)S(1)}, u32[]{:S(2)}, u32[]{:S(2)}) collective-permute-start(f32[64,128]{1,0:T(8,128)S(1)} %get-tuple-element.42), channel_id=1, source_target_pairs={{0,496},{16,32},{32,16},{48,64},{64,48},{80,96},{96,80},{112,128},... | collective-permute-start | bytes 98312 | tf_op jit(solution)/shard_map/ppermute | solution.py:608
  47.5 4.1 %collective-permute-start.7 = (f32[64,128]{1,0:T(8,128)S(1)}, f32[64,128]{1,0:T(8,128)S(1)}, u32[]{:S(2)}, u32[]{:S(2)}) collective-permute-start(f32[64,128]{1,0:T(8,128)S(1)} %get-tuple-element.43), channel_id=1, source_target_pairs={{0,16},{16,0},{32,48},{48,32},{64,80},{80,64},{96,112},{112,96},{1... | collective-permute-start | bytes 98312 | tf_op jit(solution)/shard_map/ppermute | solution.py:608
  51.6 0.0 collective-permute-done.6.refs_1_
  51.6 0.8 collective-permute-done.7.refs_2_
  52.5 0.7 shard_map.62
  53.2 1.9 %collective-permute-start.8 = (f32[48,128]{1,0:T(8,128)S(1)}, f32[48,128]{1,0:T(8,128)S(1)}, u32[]{:S(2)}, u32[]{:S(2)}) collective-permute-start(f32[48,128]{1,0:T(8,128)S(1)} %get-tuple-element.48), channel_id=1, source_target_pairs={{0,496},{16,32},{32,16},{48,64},{64,48},{80,96},{96,80},{112,128},... | collective-permute-start | bytes 73736 | tf_op jit(solution)/shard_map/ppermute | solution.py:608
  55.1 6.1 %collective-permute-start.9 = (f32[48,128]{1,0:T(8,128)S(1)}, f32[48,128]{1,0:T(8,128)S(1)}, u32[]{:S(2)}, u32[]{:S(2)}) collective-permute-start(f32[48,128]{1,0:T(8,128)S(1)} %get-tuple-element.49), channel_id=1, source_target_pairs={{0,16},{16,0},{32,48},{48,32},{64,80},{80,64},{96,112},{112,96},{1... | collective-permute-start | bytes 73736 | tf_op jit(solution)/shard_map/ppermute | solution.py:608
  61.2 0.0 all-to-all-done.received_ref
  61.2 0.7 shard_map.65
  61.9 4.2 %all-to-all-start.1 = ((f32[32,2,128]{2,1,0:T(2,128)}), f32[32,2,128]{2,1,0:T(2,128)S(1)}, u32[]{:S(2)}, u32[]{:S(2)}) async-start(f32[32,2,128]{2,1,0:T(2,128)} %shard_map.65), calls=%async_computation.1 | async-start | bytes 65536 | tf_op jit(solution)/shard_map/all_to_all | solution.py:633
  66.1 0.0 collective-permute-done.8.refs_1_
  66.1 0.0 collective-permute-done.9.refs_2_
  66.1 0.5 shard_map.63
  66.6 3.5 %collective-permute-start.10 = (f32[32,128]{1,0:T(8,128)S(1)}, f32[32,128]{1,0:T(8,128)S(1)}, u32[]{:S(2)}, u32[]{:S(2)}) collective-permute-start(f32[32,128]{1,0:T(8,128)S(1)} %get-tuple-element.53), channel_id=1, source_target_pairs={{0,496},{16,32},{32,16},{48,64},{64,48},{80,96},{96,80},{112,128},... | collective-permute-start | bytes 49160 | tf_op jit(solution)/shard_map/ppermute | solution.py:608
  70.2 5.5 %collective-permute-start.11 = (f32[32,128]{1,0:T(8,128)S(1)}, f32[32,128]{1,0:T(8,128)S(1)}, u32[]{:S(2)}, u32[]{:S(2)}) collective-permute-start(f32[32,128]{1,0:T(8,128)S(1)} %get-tuple-element.54), channel_id=1, source_target_pairs={{0,16},{16,0},{32,48},{48,32},{64,80},{80,64},{96,112},{112,96},{1... | collective-permute-start | bytes 49160 | tf_op jit(solution)/shard_map/ppermute | solution.py:608
  75.7 0.0 all-to-all-done.1.tree_ref
  75.7 0.0 collective-permute-done.10.across_ref
  75.7 0.8 collective-permute-done.11.within_ref
  76.5 0.8 shard_map.66
  77.2 14.0 %all_to_all.20.received_ref = f32[32,16,128]{2,1,0:T(8,128)S(1)} all-to-all(f32[32,16,128]{2,1,0:T(8,128)S(1)} %get-tuple-element.58), channel_id=1, replica_groups=mesh['gx'=32,'gz'=16] {'gx'}, dimensions={0} | all-to-all | bytes 524288 | tf_op jit(solution)/shard_map/all_to_all | solution.py:649
  91.2 23.1 %all_to_all.21.received_ref = f32[16,8,128]{2,1,0:T(8,128)S(1)} all-to-all(f32[16,8,128]{2,1,0:T(8,128)S(1)} %get-tuple-element.60), channel_id=1, replica_groups=mesh['gx'=32,'gz'=16] {'gz'}, dimensions={0} | all-to-all | bytes 131072 | tf_op jit(solution)/shard_map/all_to_all | solution.py:651
  114.4 0.8 shard_map.68
  (3 shorter events, 0.1 us)
Async XLA Ops:
  0.6 0.8 copy-start.1
  1.5 0.7 copy-start.2
  2.3 22.5 %collective-permute-start = (f32[136,128]{1,0:T(8,128)S(1)}, f32[136,128]{1,0:T(8,128)S(1)}, u32[]{:S(2)}, u32[]{:S(2)}) collective-permute-start(f32[136,128]{1,0:T(8,128)S(1)} %get-tuple-element.33.near_ref), channel_id=1, source_target_pairs={{0,1},{1,2},{2,3},{3,4},{4,5},{5,6},{6,7},{7,8},{8,9},{9,10},{10,1... | collective-permute-start | bytes 208904 | tf_op jit(solution)/shard_map/ppermute | solution.py:600
  6.7 18.1 %collective-permute-start.2 = (f32[136,128]{1,0:T(8,128)S(1)}, f32[136,128]{1,0:T(8,128)S(1)}, u32[]{:S(2)}, u32[]{:S(2)}) collective-permute-start(f32[136,128]{1,0:T(8,128)S(1)} %get-tuple-element.33.near_ref), channel_id=1, source_target_pairs={{0,15},{1,0},{2,1},{3,2},{4,3},{5,4},{6,5},{7,6},{8,7},{9,8},{10,9... | collective-permute-start | bytes 208904 | tf_op jit(solution)/shard_map/ppermute | solution.py:600
  16.2 7.6 %collective-permute-start.1 = (f32[80,128]{1,0:T(8,128)S(1)}, f32[80,128]{1,0:T(8,128)S(1)}, u32[]{:S(2)}, u32[]{:S(2)}) collective-permute-start(f32[80,128]{1,0:T(8,128)S(1)} %get-tuple-element.34), channel_id=1, source_target_pairs={{0,2},{1,3},{2,4},{3,5},{4,6},{5,7},{6,8},{7,9},{8,10},{9,11},{10,... | collective-permute-start | bytes 122888 | tf_op jit(solution)/shard_map/ppermute | solution.py:600
  18.1 16.1 %copy-start.3 = (f32[1,1,10,32,16]{3,4,2,1,0:T(8,128)S(1)}, f32[1,1,10,32,16]{3,4,2,1,0:T(8,128)}, u32[]{:S(2)}) copy-start(f32[1,1,10,32,16]{3,4,2,1,0:T(8,128)} %param.6) | copy-start | bytes 61444
  18.1 6.7 %collective-permute-start.3 = (f32[80,128]{1,0:T(8,128)S(1)}, f32[80,128]{1,0:T(8,128)S(1)}, u32[]{:S(2)}, u32[]{:S(2)}) collective-permute-start(f32[80,128]{1,0:T(8,128)S(1)} %get-tuple-element.35), channel_id=1, source_target_pairs={{0,14},{1,15},{2,0},{3,1},{4,2},{5,3},{6,4},{7,5},{8,6},{9,7},{10,... | collective-permute-start | bytes 122888 | tf_op jit(solution)/shard_map/ppermute | solution.py:600
  24.9 9.4 %copy-start = (f32[232,128]{1,0:T(8,128)S(1)}, f32[232,128]{1,0:T(8,128)}, u32[]{:S(2)}) copy-start(f32[232,128]{1,0:T(8,128)} %constant.5.clone.table_ref.refs_8_) | copy-start | bytes 356356
  24.9 19.3 %collective-permute-start.4 = (f32[104,128]{1,0:T(8,128)S(1)}, f32[104,128]{1,0:T(8,128)S(1)}, u32[]{:S(2)}, u32[]{:S(2)}) collective-permute-start(f32[104,128]{1,0:T(8,128)S(1)} %get-tuple-element.39), channel_id=1, source_target_pairs={{0,496},{16,32},{32,16},{48,64},{64,48},{80,96},{96,80},{112,128},... | collective-permute-start | bytes 159752 | tf_op jit(solution)/shard_map/ppermute | solution.py:608
  30.2 14.0 %collective-permute-start.5 = (f32[104,128]{1,0:T(8,128)S(1)}, f32[104,128]{1,0:T(8,128)S(1)}, u32[]{:S(2)}, u32[]{:S(2)}) collective-permute-start(f32[104,128]{1,0:T(8,128)S(1)} %get-tuple-element.40), channel_id=1, source_target_pairs={{0,16},{16,0},{32,48},{48,32},{64,80},{80,64},{96,112},{112,96},{1... | collective-permute-start | bytes 159752 | tf_op jit(solution)/shard_map/ppermute | solution.py:608
  35.2 26.0 %all-to-all-start = ((f32[16,2,128]{2,1,0:T(2,128)}), f32[16,2,128]{2,1,0:T(2,128)S(1)}, u32[]{:S(2)}, u32[]{:S(2)}) async-start(f32[16,2,128]{2,1,0:T(2,128)} %shard_map.64), calls=%async_computation | async-start | bytes 32768 | tf_op jit(solution)/shard_map/all_to_all | solution.py:616
  45.1 6.5 %collective-permute-start.6 = (f32[64,128]{1,0:T(8,128)S(1)}, f32[64,128]{1,0:T(8,128)S(1)}, u32[]{:S(2)}, u32[]{:S(2)}) collective-permute-start(f32[64,128]{1,0:T(8,128)S(1)} %get-tuple-element.42), channel_id=1, source_target_pairs={{0,496},{16,32},{32,16},{48,64},{64,48},{80,96},{96,80},{112,128},... | collective-permute-start | bytes 98312 | tf_op jit(solution)/shard_map/ppermute | solution.py:608
  47.5 4.9 %collective-permute-start.7 = (f32[64,128]{1,0:T(8,128)S(1)}, f32[64,128]{1,0:T(8,128)S(1)}, u32[]{:S(2)}, u32[]{:S(2)}) collective-permute-start(f32[64,128]{1,0:T(8,128)S(1)} %get-tuple-element.43), channel_id=1, source_target_pairs={{0,16},{16,0},{32,48},{48,32},{64,80},{80,64},{96,112},{112,96},{1... | collective-permute-start | bytes 98312 | tf_op jit(solution)/shard_map/ppermute | solution.py:608
  53.2 12.9 %collective-permute-start.8 = (f32[48,128]{1,0:T(8,128)S(1)}, f32[48,128]{1,0:T(8,128)S(1)}, u32[]{:S(2)}, u32[]{:S(2)}) collective-permute-start(f32[48,128]{1,0:T(8,128)S(1)} %get-tuple-element.48), channel_id=1, source_target_pairs={{0,496},{16,32},{32,16},{48,64},{64,48},{80,96},{96,80},{112,128},... | collective-permute-start | bytes 73736 | tf_op jit(solution)/shard_map/ppermute | solution.py:608
  55.1 11.0 %collective-permute-start.9 = (f32[48,128]{1,0:T(8,128)S(1)}, f32[48,128]{1,0:T(8,128)S(1)}, u32[]{:S(2)}, u32[]{:S(2)}) collective-permute-start(f32[48,128]{1,0:T(8,128)S(1)} %get-tuple-element.49), channel_id=1, source_target_pairs={{0,16},{16,0},{32,48},{48,32},{64,80},{80,64},{96,112},{112,96},{1... | collective-permute-start | bytes 73736 | tf_op jit(solution)/shard_map/ppermute | solution.py:608
  61.9 13.8 %all-to-all-start.1 = ((f32[32,2,128]{2,1,0:T(2,128)}), f32[32,2,128]{2,1,0:T(2,128)S(1)}, u32[]{:S(2)}, u32[]{:S(2)}) async-start(f32[32,2,128]{2,1,0:T(2,128)} %shard_map.65), calls=%async_computation.1 | async-start | bytes 65536 | tf_op jit(solution)/shard_map/all_to_all | solution.py:633
  66.6 9.0 %collective-permute-start.10 = (f32[32,128]{1,0:T(8,128)S(1)}, f32[32,128]{1,0:T(8,128)S(1)}, u32[]{:S(2)}, u32[]{:S(2)}) collective-permute-start(f32[32,128]{1,0:T(8,128)S(1)} %get-tuple-element.53), channel_id=1, source_target_pairs={{0,496},{16,32},{32,16},{48,64},{64,48},{80,96},{96,80},{112,128},... | collective-permute-start | bytes 49160 | tf_op jit(solution)/shard_map/ppermute | solution.py:608
  70.2 6.3 %collective-permute-start.11 = (f32[32,128]{1,0:T(8,128)S(1)}, f32[32,128]{1,0:T(8,128)S(1)}, u32[]{:S(2)}, u32[]{:S(2)}) collective-permute-start(f32[32,128]{1,0:T(8,128)S(1)} %get-tuple-element.54), channel_id=1, source_target_pairs={{0,16},{16,0},{32,48},{48,32},{64,80},{80,64},{96,112},{112,96},{1... | collective-permute-start | bytes 49160 | tf_op jit(solution)/shard_map/ppermute | solution.py:608

commit v6 on v5

--- a/solution.py
+++ b/solution.py
@@ -11,6 +11,8 @@
 N_GZ = 16
 F32 = jnp.float32
 HIGHEST = lax.Precision.HIGHEST
+TREE_Z, TREE_X = 0, 0
+END_Z, END_X = 9, 20
 
 cheb_high = 2.0
 cheb_low = 0.1
@@ -344,7 +346,9 @@
     high = [with_sums(field[7][0], first, second), field[7][1]]
     for chunk in range(N_GX):
         for z in range(2):
-            send_ref[chunk, 8 * z : 8 * z + 8, :] = jnp.where(above == chunk, high[z], low[z])
+            send_ref[chunk, 8 * z : 8 * z + 8, :] = jnp.where(
+                above == (chunk + END_X) % N_GX, high[z], low[z]
+            )
 
 
 def send_along_z(field, sums, send_ref):
@@ -357,7 +361,7 @@
         high = jnp.where(node == i, spread(field[i][1][7:8, :]), high)
     low, high = with_sums(low, sums, sums), with_sums(high, sums, sums)
     for chunk in range(N_GZ):
-        send_ref[chunk] = jnp.where(above == chunk, high, low)
+        send_ref[chunk] = jnp.where(above == (chunk + END_Z) % N_GZ, high, low)
 
 
 def coarse_start(load_ref, factor_ref, table_ref, send_ref):
@@ -390,9 +394,7 @@
         jnp.broadcast_to(coarse_rhs, (8, 32)), factor_ref[...],
         precision=HIGHEST, preferred_element_type=F32,
     )
-    for chunk in range(N_GZ):
-        send_ref[chunk, 0:1, :] = own[0:1, 0:128]
-        send_ref[chunk, 1:2, :] = own[0:1, 128:256]
+    write_pairs(send_ref, own[0:1, 0:128], own[0:1, 128:256])
 
 
 def begin(
@@ -430,36 +432,39 @@
     write_x_faces(applied, across_out, within_out)
 
 
-def level_of_lane(first):
-    return first + lax.broadcasted_iota(jnp.int32, (1, 128), 1) // 16
-
-
-def tree_sum(rows_of, count, here, shift):
-    total = jnp.zeros((1, 128), F32)
-    mine = lax.shift_right_logical(jnp.full((1, 128), here, jnp.int32), shift)
-    for e in range(count):
-        other = lax.shift_right_logical(jnp.full((1, 128), e, jnp.int32), shift)
-        total = total + jnp.where(other == mine, rows_of(e), 0.0)
-    return total
-
-
-def neighbours(axis, count):
-    here = lax.axis_index(axis)
+def write_pairs(ref, first, second):
+    row = lax.broadcasted_iota(jnp.int32, (8, 128), 0)
+    pairs = jnp.where(row % 2 == 0, spread(first), spread(second))
+    for start in range(0, ref.shape[0], 8):
+        ref[start : start + 8, :] = pairs
+
+
+def tree_sums(ref, here, skipped, head):
+    row = lax.broadcasted_iota(jnp.int32, (8, 128), 0)
+    level = (row % 2) * 8 + lane_iota() // 16
+    shift = jnp.maximum(level - skipped, 0)
+    mine = lax.shift_right_logical(jnp.full((8, 128), here, jnp.int32), shift)
+    total = jnp.zeros((8, 128), F32)
+    for start in range(0, ref.shape[0], 8):
+        device = (head + start // 2 + row // 2) % (ref.shape[0] // 2)
+        other = lax.shift_right_logical(device, shift)
+        total = total + jnp.where(other == mine, ref[start : start + 8, :], 0.0)
+    first = jnp.sum(jnp.where(row % 2 == 0, total, 0.0), axis=0, keepdims=True)
+    second = jnp.sum(jnp.where(row % 2 == 1, total, 0.0), axis=0, keepdims=True)
+    return first, second
+
+
+def neighbours(axis, count, head):
+    here = lax.axis_index(axis) + count - head
     return lax.rem(here + count - 1, count), lax.rem(here + 1, count)
 
 
 def lower_tree(received_ref, send_ref):
-    here = lax.axis_index("gz")
-    for row in range(2):
-        total = tree_sum(
-            lambda e: received_ref[e, row : row + 1, :], N_GZ, here, level_of_lane(8 * row)
-        )
-        for chunk in range(N_GX):
-            send_ref[chunk, row : row + 1, :] = total
+    write_pairs(send_ref, *tree_sums(received_ref, lax.axis_index("gz"), 0, TREE_Z))
 
 
 def x_faces_received(received_ref):
-    below, above = neighbours("gx", N_GX)
+    below, above = neighbours("gx", N_GX, END_X)
     left = [received_ref[below, 8 * z : 8 * z + 8, :] for z in range(2)]
     right = [received_ref[above, 8 * z : 8 * z + 8, :] for z in range(2)]
     return left, right
@@ -497,11 +502,7 @@
 
 
 def coarse_field(received_ref, factor_ref, table_ref):
-    here = lax.axis_index("gx")
-    first = tree_sum(
-        lambda e: received_ref[e, 0:1, :], N_GX, here, jnp.maximum(level_of_lane(0) - 4, 0)
-    )
-    second = tree_sum(lambda e: received_ref[e, 1:2, :], N_GX, here, level_of_lane(8) - 4)
+    first, second = tree_sums(received_ref, lax.axis_index("gx"), 4, TREE_X)
     columns = jnp.broadcast_to(jnp.concatenate([first, second], axis=1), (8, 256))
     coarse = lax.dot_general(
         columns, factor_ref[...], (((1,), (1,)), ((), ())),
@@ -564,7 +565,7 @@
 
 
 def finish(summed_ref, received_ref, precond_ref, rhs_ref, solution_ref, residual_ref):
-    below, above = neighbours("gz", N_GZ)
+    below, above = neighbours("gz", N_GZ, END_Z)
     field = sum_z(
         read(summed_ref),
         lambda i: received_ref[below, i : i + 1, :],
@@ -584,12 +585,13 @@
     return (8, count, 8, 128)
 
 
-def run(kernel, shapes, *operands, last=False):
+def run(kernel, shapes, *operands, first=False, last=False):
     spec = pl.BlockSpec(memory_space=pltpu.VMEM)
     outs = [
         jax.ShapeDtypeStruct(shape, F32) if last else pltpu.VMEM(shape, F32) for shape in shapes
     ]
-    operands = [pltpu.with_memory_space_constraint(value, pltpu.VMEM) for value in operands]
+    if not first:
+        operands = [pltpu.with_memory_space_constraint(value, pltpu.VMEM) for value in operands]
     return pl.pallas_call(
         kernel, out_shape=outs, in_specs=[spec] * len(operands), out_specs=[spec] * len(outs)
     )(*operands)
@@ -608,14 +610,22 @@
     return lax.ppermute(across, "gx", over), lax.ppermute(within, "gx", inside)
 
 
+def send_chunks(chunks, axis, head):
+    count = lax.axis_size(axis)
+    group = [(head + k) % count for k in range(count)]
+    return lax.all_to_all(chunks, axis, 0, 0, tiled=True, axis_index_groups=[group])
+
+
+def send_pairs(pairs, axis, head):
+    return send_chunks(pairs.reshape(-1, 2, 128), axis, head).reshape(pairs.shape)
+
+
 def per_device(element_rhs_load, metric, coarse_factor):
     constants = jnp.asarray(TABLE)
     factor = coarse_factor.reshape(10, 32, 16).transpose(1, 0, 2).reshape(32, 160)
     factor = jnp.pad(factor, ((0, 0), (0, 96)))
-    (send,) = run(coarse_start, [(N_GZ, 2, 128)], element_rhs_load, factor, constants)
-    tree = lax.all_to_all(send, "gz", 0, 0, tiled=True)
     near, up, down = run(
-        pack, [(136, 128), (80, 128), (80, 128)], element_rhs_load, metric
+        pack, [(136, 128), (80, 128), (80, 128)], element_rhs_load, metric, first=True
     )
     below, far_below = shifted(near, "gz", 1), shifted(up, "gz", 2)
     above, far_above = shifted(near, "gz", -1), shifted(down, "gz", -2)
@@ -629,8 +639,10 @@
         wide, edge, rows, left, right, constants,
     )
     left, right = swap_x(low, high)
-    (send,) = run(lower_tree, [(N_GX, 2, 128)], tree)
-    tree = lax.all_to_all(send, "gx", 0, 0, tiled=True)
+    (send,) = run(coarse_start, [(2 * N_GZ, 128)], element_rhs_load, factor, constants)
+    tree = send_pairs(send, "gz", TREE_Z)
+    (send,) = run(lower_tree, [(2 * N_GX, 128)], tree)
+    tree = send_pairs(send, "gx", TREE_X)
     update = smooth
     for step, count in ((0, 6), (1, 4)):
 
@@ -646,9 +658,9 @@
         last_sweep, [field_shape(2)] * 2 + [(N_GX, 16, 128)],
         applied, left, right, rhs, inverse, smooth, update, rows, tree, factor, near, constants,
     )
-    received = lax.all_to_all(send, "gx", 0, 0, tiled=True)
+    received = send_chunks(send, "gx", END_X)
     summed, send = run(middle, [field_shape(2), (N_GZ, 8, 128)], applied, received)
-    received = lax.all_to_all(send, "gz", 0, 0, tiled=True)
+    received = send_chunks(send, "gz", END_Z)
     solution_field, residual = run(
         finish, [field_shape(2)] * 2, summed, received, precond, rhs, last=True
     )

time: 116 us -> 106 us (0.914)
  blocking collectives: 37.1 us -> 27.1 us
    all_to_all x2, blocking collectives: 37.1 us -> 27.1 us  [send_chunks(): lax.all_to_all(chunks, axis, 0, 0, tiled=True, axis_index_groups=[group])]
  transfers between devices with their start and end apart: 14 -> 14, of which waited for: 3 -> 3; matrix products, arithmetic and copies ran while one was open for 0% -> 0% of each run, Pallas kernels for 3% -> 4%
where the time goes in v6:
time: 106 us; the launch traced here: 105 us
  starting transfers between devices  67.3 us (63%)
  blocking collectives  27.1 us (26%)
  Pallas kernels  6.33 us (6%)
  waiting for transfers between devices  2.72 us (3%)
    all_to_all x2, blocking collectives, send_chunks(): lax.all_to_all(chunks, axis, 0, 0, tiled=True, axis_index_groups=[group])  27.1 us
    ppermute x4, starting transfers between devices, shifted(): lax.ppermute(value, axis, [(i, (i + distance) % count) for i in range(cou...  21.4 us
    ppermute x4, starting transfers between devices, swap_x(): lax.ppermute(within, 'gx', inside)  19.6 us
    ppermute x4, starting transfers between devices, swap_x(): lax.ppermute(across, 'gx', over)  13.2 us
    all_to_all x2, starting transfers between devices, send_chunks(): lax.all_to_all(chunks, axis, 0, 0, tiled=True, axis_index_groups=[group])  13.2 us
    pallas_call x10, Pallas kernels, run(): pl.pallas_call(kernel, out_shape=outs, in_specs=[spec] * len(operands), o...  6.33 us
  transfers between devices with their start and end apart: 14, of which 3 were waited for; matrix products, arithmetic and copies ran while one was open for 0% of the time, Pallas kernels for 4%

profile of v6, /device:TPU:1, one launch (start us, length us, event | category | flops | bytes accessed | tf_op | source)
XLA Modules:
  0.0 105.3 jit_solution(9926408451951492670)
XLA Ops:
  0.6 1.0 shard_map.59
  1.6 4.4 %collective-permute-start = (f32[136,128]{1,0:T(8,128)S(1)}, f32[136,128]{1,0:T(8,128)S(1)}, u32[]{:S(2)}, u32[]{:S(2)}) collective-permute-start(f32[136,128]{1,0:T(8,128)S(1)} %get-tuple-element.33.near_ref), channel_id=1, source_target_pairs={{0,1},{1,2},{2,3},{3,4},{4,5},{5,6},{6,7},{7,8},{8,9},{9,10},{10,1... | collective-permute-start | bytes 208904 | tf_op jit(solution)/shard_map/ppermute | solution.py:602
  6.0 9.5 %collective-permute-start.2 = (f32[136,128]{1,0:T(8,128)S(1)}, f32[136,128]{1,0:T(8,128)S(1)}, u32[]{:S(2)}, u32[]{:S(2)}) collective-permute-start(f32[136,128]{1,0:T(8,128)S(1)} %get-tuple-element.33.near_ref), channel_id=1, source_target_pairs={{0,15},{1,0},{2,1},{3,2},{4,3},{5,4},{6,5},{7,6},{8,7},{9,8},{10,9... | collective-permute-start | bytes 208904 | tf_op jit(solution)/shard_map/ppermute | solution.py:602
  15.5 1.9 %collective-permute-start.1 = (f32[80,128]{1,0:T(8,128)S(1)}, f32[80,128]{1,0:T(8,128)S(1)}, u32[]{:S(2)}, u32[]{:S(2)}) collective-permute-start(f32[80,128]{1,0:T(8,128)S(1)} %get-tuple-element.34), channel_id=1, source_target_pairs={{0,2},{1,3},{2,4},{3,5},{4,6},{5,7},{6,8},{7,9},{8,10},{9,11},{10,... | collective-permute-start | bytes 122888 | tf_op jit(solution)/shard_map/ppermute | solution.py:602
  17.5 0.0 copy-start.2
  17.5 5.6 %collective-permute-start.3 = (f32[80,128]{1,0:T(8,128)S(1)}, f32[80,128]{1,0:T(8,128)S(1)}, u32[]{:S(2)}, u32[]{:S(2)}) collective-permute-start(f32[80,128]{1,0:T(8,128)S(1)} %get-tuple-element.35), channel_id=1, source_target_pairs={{0,14},{1,15},{2,0},{3,1},{4,2},{5,3},{6,4},{7,5},{8,6},{9,7},{10,... | collective-permute-start | bytes 122888 | tf_op jit(solution)/shard_map/ppermute | solution.py:602
  23.1 0.0 collective-permute-done.1.far_below_ref
  23.1 1.1 %collective-permute-done.3.far_above_ref = f32[80,128]{1,0:T(8,128)S(1)} collective-permute-done((f32[80,128]{1,0:T(8,128)S(1)}, f32[80,128]{1,0:T(8,128)S(1)}, u32[]{:S(2)}, u32[]{:S(2)}) %collective-permute-start.3) | collective-permute-done | bytes 40992 | tf_op jit(solution)/shard_map/ppermute | solution.py:602
  24.2 0.0 collective-permute-done.below_ref
  24.2 0.0 collective-permute-done.2.above_ref
  24.2 0.0 copy-start
  24.2 5.3 %collective-permute-start.4 = (f32[104,128]{1,0:T(8,128)S(1)}, f32[104,128]{1,0:T(8,128)S(1)}, u32[]{:S(2)}, u32[]{:S(2)}) collective-permute-start(f32[104,128]{1,0:T(8,128)S(1)} %get-tuple-element.39), channel_id=1, source_target_pairs={{0,496},{16,32},{32,16},{48,64},{64,48},{80,96},{96,80},{112,128},... | collective-permute-start | bytes 159752 | tf_op jit(solution)/shard_map/ppermute | solution.py:610
  29.5 4.0 %collective-permute-start.5 = (f32[104,128]{1,0:T(8,128)S(1)}, f32[104,128]{1,0:T(8,128)S(1)}, u32[]{:S(2)}, u32[]{:S(2)}) collective-permute-start(f32[104,128]{1,0:T(8,128)S(1)} %get-tuple-element.40), channel_id=1, source_target_pairs={{0,16},{16,0},{32,48},{48,32},{64,80},{80,64},{96,112},{112,96},{1... | collective-permute-start | bytes 159752 | tf_op jit(solution)/shard_map/ppermute | solution.py:610
  33.5 0.0 copy-done.2
  33.5 0.0 copy-start.1
  33.5 0.1 copy.7
  33.6 0.0 copy-done
  33.6 0.7 copy-done.1
  34.4 0.9 shard_map.64
  35.3 9.0 %all-to-all-start = ((f32[16,2,128]{2,1,0:T(2,128)}), f32[16,2,128]{2,1,0:T(2,128)S(1)}, u32[]{:S(2)}, u32[]{:S(2)}) async-start(f32[16,2,128]{2,1,0:T(2,128)} %bitcast.3), calls=%async_computation | async-start | bytes 32768 | tf_op jit(solution)/shard_map/all_to_all | solution.py:616
  44.3 0.0 collective-permute-done.4.across_ref
  44.3 0.0 collective-permute-done.5.within_ref
  44.3 0.9 shard_map.61
  45.2 2.4 %collective-permute-start.6 = (f32[64,128]{1,0:T(8,128)S(1)}, f32[64,128]{1,0:T(8,128)S(1)}, u32[]{:S(2)}, u32[]{:S(2)}) collective-permute-start(f32[64,128]{1,0:T(8,128)S(1)} %get-tuple-element.42), channel_id=1, source_target_pairs={{0,496},{16,32},{32,16},{48,64},{64,48},{80,96},{96,80},{112,128},... | collective-permute-start | bytes 98312 | tf_op jit(solution)/shard_map/ppermute | solution.py:610
  47.6 4.1 %collective-permute-start.7 = (f32[64,128]{1,0:T(8,128)S(1)}, f32[64,128]{1,0:T(8,128)S(1)}, u32[]{:S(2)}, u32[]{:S(2)}) collective-permute-start(f32[64,128]{1,0:T(8,128)S(1)} %get-tuple-element.43), channel_id=1, source_target_pairs={{0,16},{16,0},{32,48},{48,32},{64,80},{80,64},{96,112},{112,96},{1... | collective-permute-start | bytes 98312 | tf_op jit(solution)/shard_map/ppermute | solution.py:610
  51.7 0.0 collective-permute-done.6.refs_1_
  51.7 0.8 collective-permute-done.7.refs_2_
  52.5 0.7 shard_map.62
  53.2 1.9 %collective-permute-start.8 = (f32[48,128]{1,0:T(8,128)S(1)}, f32[48,128]{1,0:T(8,128)S(1)}, u32[]{:S(2)}, u32[]{:S(2)}) collective-permute-start(f32[48,128]{1,0:T(8,128)S(1)} %get-tuple-element.48), channel_id=1, source_target_pairs={{0,496},{16,32},{32,16},{48,64},{64,48},{80,96},{96,80},{112,128},... | collective-permute-start | bytes 73736 | tf_op jit(solution)/shard_map/ppermute | solution.py:610
  55.2 6.1 %collective-permute-start.9 = (f32[48,128]{1,0:T(8,128)S(1)}, f32[48,128]{1,0:T(8,128)S(1)}, u32[]{:S(2)}, u32[]{:S(2)}) collective-permute-start(f32[48,128]{1,0:T(8,128)S(1)} %get-tuple-element.49), channel_id=1, source_target_pairs={{0,16},{16,0},{32,48},{48,32},{64,80},{80,64},{96,112},{112,96},{1... | collective-permute-start | bytes 73736 | tf_op jit(solution)/shard_map/ppermute | solution.py:610
  61.3 0.0 all-to-all-done
  61.3 0.6 shard_map.65
  61.9 4.2 %all-to-all-start.1 = ((f32[32,2,128]{2,1,0:T(2,128)}), f32[32,2,128]{2,1,0:T(2,128)S(1)}, u32[]{:S(2)}, u32[]{:S(2)}) async-start(f32[32,2,128]{2,1,0:T(2,128)} %bitcast.5), calls=%async_computation.1 | async-start | bytes 65536 | tf_op jit(solution)/shard_map/all_to_all | solution.py:616
  66.1 0.0 collective-permute-done.8.refs_1_
  66.1 0.0 collective-permute-done.9.refs_2_
  66.2 0.5 shard_map.63
  66.7 3.5 %collective-permute-start.10 = (f32[32,128]{1,0:T(8,128)S(1)}, f32[32,128]{1,0:T(8,128)S(1)}, u32[]{:S(2)}, u32[]{:S(2)}) collective-permute-start(f32[32,128]{1,0:T(8,128)S(1)} %get-tuple-element.53), channel_id=1, source_target_pairs={{0,496},{16,32},{32,16},{48,64},{64,48},{80,96},{96,80},{112,128},... | collective-permute-start | bytes 49160 | tf_op jit(solution)/shard_map/ppermute | solution.py:610
  70.3 5.5 %collective-permute-start.11 = (f32[32,128]{1,0:T(8,128)S(1)}, f32[32,128]{1,0:T(8,128)S(1)}, u32[]{:S(2)}, u32[]{:S(2)}) collective-permute-start(f32[32,128]{1,0:T(8,128)S(1)} %get-tuple-element.54), channel_id=1, source_target_pairs={{0,16},{16,0},{32,48},{48,32},{64,80},{80,64},{96,112},{112,96},{1... | collective-permute-start | bytes 49160 | tf_op jit(solution)/shard_map/ppermute | solution.py:610
  75.7 0.0 all-to-all-done.1
  75.7 0.0 collective-permute-done.10.across_ref
  75.7 0.8 collective-permute-done.11.within_ref
  76.5 0.7 shard_map.66
  77.3 11.2 %all_to_all.20.received_ref = f32[32,16,128]{2,1,0:T(8,128)S(1)} all-to-all(f32[32,16,128]{2,1,0:T(8,128)S(1)} %get-tuple-element.58), channel_id=1, replica_groups={{320,336,352,368,384,400,416,432,448,464,480,496,0,16,32,48,64,80,96,11..., dimensions={0} | all-to-all | bytes 524288 | tf_op jit(solution)/shard_map/all_to_all | solution.py:616
  88.5 15.9 %all_to_all.21.received_ref = f32[16,8,128]{2,1,0:T(8,128)S(1)} all-to-all(f32[16,8,128]{2,1,0:T(8,128)S(1)} %get-tuple-element.60), channel_id=1, replica_groups={{9,10,11,12,13,14,15,0,1,2,3,4,5,6,7,8},{25,26,27,28,29,30,31,16,17,18,..., dimensions={0} | all-to-all | bytes 131072 | tf_op jit(solution)/shard_map/all_to_all | solution.py:616
  104.5 0.8 shard_map.68
  (3 shorter events, 0.1 us)
Async XLA Ops:
  1.6 22.5 %collective-permute-start = (f32[136,128]{1,0:T(8,128)S(1)}, f32[136,128]{1,0:T(8,128)S(1)}, u32[]{:S(2)}, u32[]{:S(2)}) collective-permute-start(f32[136,128]{1,0:T(8,128)S(1)} %get-tuple-element.33.near_ref), channel_id=1, source_target_pairs={{0,1},{1,2},{2,3},{3,4},{4,5},{5,6},{6,7},{7,8},{8,9},{9,10},{10,1... | collective-permute-start | bytes 208904 | tf_op jit(solution)/shard_map/ppermute | solution.py:602
  6.0 18.1 %collective-permute-start.2 = (f32[136,128]{1,0:T(8,128)S(1)}, f32[136,128]{1,0:T(8,128)S(1)}, u32[]{:S(2)}, u32[]{:S(2)}) collective-permute-start(f32[136,128]{1,0:T(8,128)S(1)} %get-tuple-element.33.near_ref), channel_id=1, source_target_pairs={{0,15},{1,0},{2,1},{3,2},{4,3},{5,4},{6,5},{7,6},{8,7},{9,8},{10,9... | collective-permute-start | bytes 208904 | tf_op jit(solution)/shard_map/ppermute | solution.py:602
  15.5 7.6 %collective-permute-start.1 = (f32[80,128]{1,0:T(8,128)S(1)}, f32[80,128]{1,0:T(8,128)S(1)}, u32[]{:S(2)}, u32[]{:S(2)}) collective-permute-start(f32[80,128]{1,0:T(8,128)S(1)} %get-tuple-element.34), channel_id=1, source_target_pairs={{0,2},{1,3},{2,4},{3,5},{4,6},{5,7},{6,8},{7,9},{8,10},{9,11},{10,... | collective-permute-start | bytes 122888 | tf_op jit(solution)/shard_map/ppermute | solution.py:602
  17.5 16.1 %copy-start.2 = (f32[1,1,10,32,16]{3,4,2,1,0:T(8,128)S(1)}, f32[1,1,10,32,16]{3,4,2,1,0:T(8,128)}, u32[]{:S(2)}) copy-start(f32[1,1,10,32,16]{3,4,2,1,0:T(8,128)} %param.6) | copy-start | bytes 61444
  17.5 6.7 %collective-permute-start.3 = (f32[80,128]{1,0:T(8,128)S(1)}, f32[80,128]{1,0:T(8,128)S(1)}, u32[]{:S(2)}, u32[]{:S(2)}) collective-permute-start(f32[80,128]{1,0:T(8,128)S(1)} %get-tuple-element.35), channel_id=1, source_target_pairs={{0,14},{1,15},{2,0},{3,1},{4,2},{5,3},{6,4},{7,5},{8,6},{9,7},{10,... | collective-permute-start | bytes 122888 | tf_op jit(solution)/shard_map/ppermute | solution.py:602
  24.2 9.4 %copy-start = (f32[232,128]{1,0:T(8,128)S(1)}, f32[232,128]{1,0:T(8,128)}, u32[]{:S(2)}) copy-start(f32[232,128]{1,0:T(8,128)} %constant.5.clone.table_ref.refs_8_) | copy-start | bytes 356356
  24.2 20.0 %collective-permute-start.4 = (f32[104,128]{1,0:T(8,128)S(1)}, f32[104,128]{1,0:T(8,128)S(1)}, u32[]{:S(2)}, u32[]{:S(2)}) collective-permute-start(f32[104,128]{1,0:T(8,128)S(1)} %get-tuple-element.39), channel_id=1, source_target_pairs={{0,496},{16,32},{32,16},{48,64},{64,48},{80,96},{96,80},{112,128},... | collective-permute-start | bytes 159752 | tf_op jit(solution)/shard_map/ppermute | solution.py:610
  29.5 14.7 %collective-permute-start.5 = (f32[104,128]{1,0:T(8,128)S(1)}, f32[104,128]{1,0:T(8,128)S(1)}, u32[]{:S(2)}, u32[]{:S(2)}) collective-permute-start(f32[104,128]{1,0:T(8,128)S(1)} %get-tuple-element.40), channel_id=1, source_target_pairs={{0,16},{16,0},{32,48},{48,32},{64,80},{80,64},{96,112},{112,96},{1... | collective-permute-start | bytes 159752 | tf_op jit(solution)/shard_map/ppermute | solution.py:610
  33.5 0.8 copy-start.1
  35.3 26.0 %all-to-all-start = ((f32[16,2,128]{2,1,0:T(2,128)}), f32[16,2,128]{2,1,0:T(2,128)S(1)}, u32[]{:S(2)}, u32[]{:S(2)}) async-start(f32[16,2,128]{2,1,0:T(2,128)} %bitcast.3), calls=%async_computation | async-start | bytes 32768 | tf_op jit(solution)/shard_map/all_to_all | solution.py:616
  45.2 6.5 %collective-permute-start.6 = (f32[64,128]{1,0:T(8,128)S(1)}, f32[64,128]{1,0:T(8,128)S(1)}, u32[]{:S(2)}, u32[]{:S(2)}) collective-permute-start(f32[64,128]{1,0:T(8,128)S(1)} %get-tuple-element.42), channel_id=1, source_target_pairs={{0,496},{16,32},{32,16},{48,64},{64,48},{80,96},{96,80},{112,128},... | collective-permute-start | bytes 98312 | tf_op jit(solution)/shard_map/ppermute | solution.py:610
  47.6 4.9 %collective-permute-start.7 = (f32[64,128]{1,0:T(8,128)S(1)}, f32[64,128]{1,0:T(8,128)S(1)}, u32[]{:S(2)}, u32[]{:S(2)}) collective-permute-start(f32[64,128]{1,0:T(8,128)S(1)} %get-tuple-element.43), channel_id=1, source_target_pairs={{0,16},{16,0},{32,48},{48,32},{64,80},{80,64},{96,112},{112,96},{1... | collective-permute-start | bytes 98312 | tf_op jit(solution)/shard_map/ppermute | solution.py:610
  53.2 12.9 %collective-permute-start.8 = (f32[48,128]{1,0:T(8,128)S(1)}, f32[48,128]{1,0:T(8,128)S(1)}, u32[]{:S(2)}, u32[]{:S(2)}) collective-permute-start(f32[48,128]{1,0:T(8,128)S(1)} %get-tuple-element.48), channel_id=1, source_target_pairs={{0,496},{16,32},{32,16},{48,64},{64,48},{80,96},{96,80},{112,128},... | collective-permute-start | bytes 73736 | tf_op jit(solution)/shard_map/ppermute | solution.py:610
  55.2 11.0 %collective-permute-start.9 = (f32[48,128]{1,0:T(8,128)S(1)}, f32[48,128]{1,0:T(8,128)S(1)}, u32[]{:S(2)}, u32[]{:S(2)}) collective-permute-start(f32[48,128]{1,0:T(8,128)S(1)} %get-tuple-element.49), channel_id=1, source_target_pairs={{0,16},{16,0},{32,48},{48,32},{64,80},{80,64},{96,112},{112,96},{1... | collective-permute-start | bytes 73736 | tf_op jit(solution)/shard_map/ppermute | solution.py:610
  61.9 13.8 %all-to-all-start.1 = ((f32[32,2,128]{2,1,0:T(2,128)}), f32[32,2,128]{2,1,0:T(2,128)S(1)}, u32[]{:S(2)}, u32[]{:S(2)}) async-start(f32[32,2,128]{2,1,0:T(2,128)} %bitcast.5), calls=%async_computation.1 | async-start | bytes 65536 | tf_op jit(solution)/shard_map/all_to_all | solution.py:616
  66.7 9.0 %collective-permute-start.10 = (f32[32,128]{1,0:T(8,128)S(1)}, f32[32,128]{1,0:T(8,128)S(1)}, u32[]{:S(2)}, u32[]{:S(2)}) collective-permute-start(f32[32,128]{1,0:T(8,128)S(1)} %get-tuple-element.53), channel_id=1, source_target_pairs={{0,496},{16,32},{32,16},{48,64},{64,48},{80,96},{96,80},{112,128},... | collective-permute-start | bytes 49160 | tf_op jit(solution)/shard_map/ppermute | solution.py:610
  70.3 6.3 %collective-permute-start.11 = (f32[32,128]{1,0:T(8,128)S(1)}, f32[32,128]{1,0:T(8,128)S(1)}, u32[]{:S(2)}, u32[]{:S(2)}) collective-permute-start(f32[32,128]{1,0:T(8,128)S(1)} %get-tuple-element.54), channel_id=1, source_target_pairs={{0,16},{16,0},{32,48},{48,32},{64,80},{80,64},{96,112},{112,96},{1... | collective-permute-start | bytes 49160 | tf_op jit(solution)/shard_map/ppermute | solution.py:610

commit v7 on v6

--- a/solution.py
+++ b/solution.py
@@ -201,9 +201,13 @@
     count = len(field[0])
     stiff = table(table_ref, "stiff")
     out = [[None] * count for i in range(8)]
+    columns = [jnp.concatenate([field[i][c] for i in range(8)], axis=0) for c in range(count)]
+    along_y = jnp.dot(
+        jnp.concatenate(columns, axis=0), stiff, precision=HIGHEST, preferred_element_type=F32
+    )
     for c in range(count):
-        stacked = jnp.concatenate([field[i][c] for i in range(8)], axis=0)
-        along_l = jnp.dot(stacked, stiff, precision=HIGHEST, preferred_element_type=F32)
+        stacked = columns[c]
+        along_l = along_y[64 * c : 64 * c + 64, :]
         along_j = jnp.dot(
             stiff[0:64, 0:64], stacked, precision=HIGHEST, preferred_element_type=F32
         )
@@ -252,6 +256,14 @@
         self.within[first:last, :] = jnp.where(self.odd, low, high)
 
 
+class Either:
+    def __init__(self, first, first_ref, second_ref):
+        self.first, self.first_ref, self.second_ref = first, first_ref, second_ref
+
+    def __getitem__(self, where):
+        return jnp.where(self.first, self.first_ref[where], self.second_ref[where])
+
+
 class Side:
     def __init__(self, across_ref, within_ref, right):
         odd = lax.rem(lax.axis_index("gx"), 2) == 1
@@ -276,25 +288,28 @@
     return [ref[8 * c : 8 * c + 8, :] for c in range(count)]
 
 
-def pack(load_ref, metric_ref, near_ref, up_ref, down_ref):
+def pack(load_ref, metric_ref, near_ref, inner_ref, outer_ref):
+    begins = lax.rem(lax.axis_index("gz"), 4) < 2
     element = lax.broadcasted_iota(jnp.int32, (16, 128), 0)
     lane = lax.broadcasted_iota(jnp.int32, (16, 128), 1)
     expand = jnp.where(element == lane // 8, 1.0, 0.0)
-    for ref, start in ((near_ref, 128), (up_ref, 72), (down_ref, 72)):
+    for ref, start in ((near_ref, 128), (inner_ref, 72), (outer_ref, 72)):
         ref[start + 6 : start + 8, :] = jnp.zeros((2, 128), F32)
     for m in range(3):
         expanded = jnp.dot(
             metric_ref[m, 0], expand, precision=HIGHEST, preferred_element_type=F32
         )
-        for ref, start in ((near_ref, 128), (up_ref, 72), (down_ref, 72)):
+        for ref, start in ((near_ref, 128), (inner_ref, 72), (outer_ref, 72)):
             ref[start + 2 * m : start + 2 * m + 2, :] = expanded
     for i in range(8):
         for z in range(2):
             near_ref[8 * (2 * i + z) : 8 * (2 * i + z) + 8, :] = load_ref[0, i, z]
-        up_ref[8 * i : 8 * i + 8, :] = load_ref[0, i, 1]
-        up_ref[64 + i : 65 + i, :] = load_ref[0, i, 0, 7:8, :]
-        down_ref[8 * i : 8 * i + 8, :] = load_ref[0, i, 0]
-        down_ref[64 + i : 65 + i, :] = load_ref[0, i, 1, 0:1, :]
+        rows = slice(8 * i, 8 * i + 8)
+        inner_ref[rows, :] = jnp.where(begins, load_ref[0, i, 1], load_ref[0, i, 0])
+        outer_ref[rows, :] = jnp.where(begins, load_ref[0, i, 0], load_ref[0, i, 1])
+        up, down = load_ref[0, i, 0, 7:8, :], load_ref[0, i, 1, 0:1, :]
+        inner_ref[64 + i : 65 + i, :] = jnp.where(begins, up, down)
+        outer_ref[64 + i : 65 + i, :] = jnp.where(begins, down, up)
 
 
 Facross_refE_METRIC = 72
@@ -302,9 +317,14 @@
 
 
 def gather(
-    near_ref, below_ref, far_below_ref, above_ref, far_above_ref,
+    near_ref, even_ref, odd_ref, inner_ref, outer_ref, earlier_ref,
     load_ref, edge_ref, rows_ref, low_ref, high_ref,
 ):
+    place = lax.axis_index("gz")
+    above_ref = Either(lax.rem(place, 2) == 0, even_ref, odd_ref)
+    below_ref = Either(lax.rem(place, 2) == 1, even_ref, odd_ref)
+    far_above_ref = Either(lax.rem(place, 4) < 2, inner_ref, outer_ref)
+    far_below_ref = Either(lax.rem(place, 4) >= 2, inner_ref, outer_ref)
     for i in range(8):
         load_ref[i, 0] = far_below_ref[8 * i : 8 * i + 8, :]
         load_ref[i, 7] = far_above_ref[8 * i : 8 * i + 8, :]
@@ -364,9 +384,14 @@
         send_ref[chunk] = jnp.where(above == (chunk + END_Z) % N_GZ, high, low)
 
 
-def coarse_start(load_ref, factor_ref, table_ref, send_ref):
+def near_rows(near_ref, i, z):
+    start = 8 * (2 * i + z)
+    return near_ref[start : start + 8, :]
+
+
+def coarse_start(near_ref, factor_ref, table_ref, send_ref):
     parts = []
-    load = [[wall(load_ref[0, i, z]) for z in range(2)] for i in range(8)]
+    load = [[wall(near_rows(near_ref, i, z)) for z in range(2)] for i in range(8)]
     for a in range(2):
         along_x = []
         for z in range(2):
@@ -544,8 +569,7 @@
     second = jnp.zeros((8, 128), F32)
     for i in range(8):
         for z in range(2):
-            start = 8 * (2 * i + z)
-            first = first + near_ref[start : start + 8, :] * precond[i][z]
+            first = first + near_rows(near_ref, i, z) * precond[i][z]
             second = second + applied[i][z] * precond[i][z]
     send_along_x(
         applied,
@@ -597,9 +621,10 @@
     )(*operands)
 
 
-def shifted(value, axis, distance):
-    count = lax.axis_size(axis)
-    return lax.ppermute(value, axis, [(i, (i + distance) % count) for i in range(count)])
+def swap_z(value, distance, first=0):
+    count = lax.axis_size("gz")
+    pairs = [(i, (((i - first) % count ^ distance) + first) % count) for i in range(count)]
+    return lax.ppermute(value, "gz", pairs)
 
 
 def swap_x(across, within):
@@ -624,14 +649,16 @@
     constants = jnp.asarray(TABLE)
     factor = coarse_factor.reshape(10, 32, 16).transpose(1, 0, 2).reshape(32, 160)
     factor = jnp.pad(factor, ((0, 0), (0, 96)))
-    near, up, down = run(
+    near, inner, outer = run(
         pack, [(136, 128), (80, 128), (80, 128)], element_rhs_load, metric, first=True
     )
-    below, far_below = shifted(near, "gz", 1), shifted(up, "gz", 2)
-    above, far_above = shifted(near, "gz", -1), shifted(down, "gz", -2)
+    near_even, near_odd = swap_z(near, 1), swap_z(near, 1, 1)
+    far_inner, far_outer = swap_z(inner, 2), swap_z(outer, 2, 2)
+    (send,) = run(coarse_start, [(2 * N_GZ, 128)], near, factor, constants)
+    tree = send_pairs(send, "gz", TREE_Z)
     wide, edge, rows, low, high = run(
         gather, [field_shape(8), (16, 128), (32, 128)] + [(Facross_refE_ROWS, 128)] * 2,
-        near, below, far_below, above, far_above,
+        near, near_even, near_odd, far_inner, far_outer, send,
     )
     left, right = swap_x(low, high)
     rhs, inverse, smooth, applied, low, high = run(
@@ -639,8 +666,6 @@
         wide, edge, rows, left, right, constants,
     )
     left, right = swap_x(low, high)
-    (send,) = run(coarse_start, [(2 * N_GZ, 128)], element_rhs_load, factor, constants)
-    tree = send_pairs(send, "gz", TREE_Z)
     (send,) = run(lower_tree, [(2 * N_GX, 128)], tree)
     tree = send_pairs(send, "gx", TREE_X)
     update = smooth

time: 106 us -> 104 us (0.981)
  starting transfers between devices: 67.3 us -> 65.9 us
  waiting for transfers between devices: 2.72 us -> 1.65 us
    all_to_all x2, starting transfers between devices: 13.2 us -> 11.3 us  [send_chunks(): lax.all_to_all(chunks, axis, 0, 0, tiled=True, axis_index_groups=[group])]
    ppermute x4, waiting for transfers between devices: 1.08 us -> 0.01 us  [swap_z(): return lax.ppermute(value, 'gz', pairs)]
  transfers between devices with their start and end apart: 14 -> 14, of which waited for: 3 -> 2; matrix products, arithmetic and copies ran while one was open for 0% -> 1% of each run, Pallas kernels for 4% -> 3%
where the time goes in v7:
time: 104 us; the launch traced here: 103 us
  starting transfers between devices  65.9 us (63%)
  blocking collectives  27.1 us (26%)
  Pallas kernels  6.81 us (7%)
  waiting for transfers between devices  1.65 us (2%)
    all_to_all x2, blocking collectives, send_chunks(): lax.all_to_all(chunks, axis, 0, 0, tiled=True, axis_index_groups=[group])  27.1 us
    ppermute x4, starting transfers between devices, swap_z(): return lax.ppermute(value, 'gz', pairs)  22 us
    ppermute x4, starting transfers between devices, swap_x(): lax.ppermute(within, 'gx', inside)  19.8 us
    ppermute x4, starting transfers between devices, swap_x(): lax.ppermute(across, 'gx', over)  12.8 us
    all_to_all x2, starting transfers between devices, send_chunks(): lax.all_to_all(chunks, axis, 0, 0, tiled=True, axis_index_groups=[group])  11.3 us
    pallas_call x10, Pallas kernels, run(): pl.pallas_call(kernel, out_shape=outs, in_specs=[spec] * len(operands), o...  6.81 us
  transfers between devices with their start and end apart: 14, of which 2 were waited for; matrix products, arithmetic and copies ran while one was open for 1% of the time, Pallas kernels for 3%

profile of v7, /device:TPU:1, one launch (start us, length us, event | category | flops | bytes accessed | tf_op | source)
XLA Modules:
  0.0 103.4 jit_solution(15264347593340737124)
XLA Ops:
  0.6 0.0 copy-start
  0.6 1.0 shard_map.59
  1.7 4.4 %collective-permute-start = (f32[136,128]{1,0:T(8,128)S(1)}, f32[136,128]{1,0:T(8,128)S(1)}, u32[]{:S(2)}, u32[]{:S(2)}) collective-permute-start(f32[136,128]{1,0:T(8,128)S(1)} %get-tuple-element.33.near_ref), channel_id=1, source_target_pairs={{0,1},{1,0},{2,3},{3,2},{4,5},{5,4},{6,7},{7,6},{8,9},{9,8},{10,11... | collective-permute-start | bytes 208904 | tf_op jit(solution)/shard_map/ppermute | solution.py:627
  6.1 10.2 %collective-permute-start.1 = (f32[136,128]{1,0:T(8,128)S(1)}, f32[136,128]{1,0:T(8,128)S(1)}, u32[]{:S(2)}, u32[]{:S(2)}) collective-permute-start(f32[136,128]{1,0:T(8,128)S(1)} %get-tuple-element.33.near_ref), channel_id=1, source_target_pairs={{0,15},{1,2},{2,1},{3,4},{4,3},{5,6},{6,5},{7,8},{8,7},{9,10},{10,... | collective-permute-start | bytes 208904 | tf_op jit(solution)/shard_map/ppermute | solution.py:627
  16.3 1.9 %collective-permute-start.2 = (f32[80,128]{1,0:T(8,128)S(1)}, f32[80,128]{1,0:T(8,128)S(1)}, u32[]{:S(2)}, u32[]{:S(2)}) collective-permute-start(f32[80,128]{1,0:T(8,128)S(1)} %get-tuple-element.34), channel_id=1, source_target_pairs={{0,2},{1,3},{2,0},{3,1},{4,6},{5,7},{6,4},{7,5},{8,10},{9,11},{10,... | collective-permute-start | bytes 122888 | tf_op jit(solution)/shard_map/ppermute | solution.py:627
  18.2 5.5 %collective-permute-start.3 = (f32[80,128]{1,0:T(8,128)S(1)}, f32[80,128]{1,0:T(8,128)S(1)}, u32[]{:S(2)}, u32[]{:S(2)}) collective-permute-start(f32[80,128]{1,0:T(8,128)S(1)} %get-tuple-element.35), channel_id=1, source_target_pairs={{0,14},{1,15},{2,4},{3,5},{4,2},{5,3},{6,8},{7,9},{8,6},{9,7},{10,... | collective-permute-start | bytes 122888 | tf_op jit(solution)/shard_map/ppermute | solution.py:627
  23.7 1.0 copy.7
  24.6 0.0 copy-done
  24.7 0.9 shard_map.60.earlier_ref
  25.6 0.0 collective-permute-done.2.inner_ref
  25.6 0.0 collective-permute-done.3.outer_ref
  25.6 0.0 collective-permute-done.even_ref
  25.6 0.0 collective-permute-done.1.odd_ref
  25.6 0.8 shard_map.61
  26.4 4.9 %collective-permute-start.4 = (f32[104,128]{1,0:T(8,128)S(1)}, f32[104,128]{1,0:T(8,128)S(1)}, u32[]{:S(2)}, u32[]{:S(2)}) collective-permute-start(f32[104,128]{1,0:T(8,128)S(1)} %get-tuple-element.39), channel_id=1, source_target_pairs={{0,496},{16,32},{32,16},{48,64},{64,48},{80,96},{96,80},{112,128},... | collective-permute-start | bytes 159752 | tf_op jit(solution)/shard_map/ppermute | solution.py:635
  31.3 4.2 %collective-permute-start.5 = (f32[104,128]{1,0:T(8,128)S(1)}, f32[104,128]{1,0:T(8,128)S(1)}, u32[]{:S(2)}, u32[]{:S(2)}) collective-permute-start(f32[104,128]{1,0:T(8,128)S(1)} %get-tuple-element.40), channel_id=1, source_target_pairs={{0,16},{16,0},{32,48},{48,32},{64,80},{80,64},{96,112},{112,96},{1... | collective-permute-start | bytes 159752 | tf_op jit(solution)/shard_map/ppermute | solution.py:635
  35.5 7.1 %all-to-all-start = ((f32[16,2,128]{2,1,0:T(2,128)}), f32[16,2,128]{2,1,0:T(2,128)S(1)}, u32[]{:S(2)}, u32[]{:S(2)}) async-start(f32[16,2,128]{2,1,0:T(2,128)} %bitcast.3), calls=%async_computation | async-start | bytes 32768 | tf_op jit(solution)/shard_map/all_to_all | solution.py:641
  42.6 0.0 collective-permute-done.4.across_ref
  42.7 0.0 collective-permute-done.5.within_ref
  42.7 0.8 shard_map.62
  43.5 2.4 %collective-permute-start.6 = (f32[64,128]{1,0:T(8,128)S(1)}, f32[64,128]{1,0:T(8,128)S(1)}, u32[]{:S(2)}, u32[]{:S(2)}) collective-permute-start(f32[64,128]{1,0:T(8,128)S(1)} %get-tuple-element.42), channel_id=1, source_target_pairs={{0,496},{16,32},{32,16},{48,64},{64,48},{80,96},{96,80},{112,128},... | collective-permute-start | bytes 98312 | tf_op jit(solution)/shard_map/ppermute | solution.py:635
  45.9 4.1 %collective-permute-start.7 = (f32[64,128]{1,0:T(8,128)S(1)}, f32[64,128]{1,0:T(8,128)S(1)}, u32[]{:S(2)}, u32[]{:S(2)}) collective-permute-start(f32[64,128]{1,0:T(8,128)S(1)} %get-tuple-element.43), channel_id=1, source_target_pairs={{0,16},{16,0},{32,48},{48,32},{64,80},{80,64},{96,112},{112,96},{1... | collective-permute-start | bytes 98312 | tf_op jit(solution)/shard_map/ppermute | solution.py:635
  50.0 0.0 collective-permute-done.6.refs_1_
  50.0 0.8 collective-permute-done.7.refs_2_
  50.9 0.6 shard_map.63
  51.5 1.9 %collective-permute-start.8 = (f32[48,128]{1,0:T(8,128)S(1)}, f32[48,128]{1,0:T(8,128)S(1)}, u32[]{:S(2)}, u32[]{:S(2)}) collective-permute-start(f32[48,128]{1,0:T(8,128)S(1)} %get-tuple-element.48), channel_id=1, source_target_pairs={{0,496},{16,32},{32,16},{48,64},{64,48},{80,96},{96,80},{112,128},... | collective-permute-start | bytes 73736 | tf_op jit(solution)/shard_map/ppermute | solution.py:635
  53.4 6.1 %collective-permute-start.9 = (f32[48,128]{1,0:T(8,128)S(1)}, f32[48,128]{1,0:T(8,128)S(1)}, u32[]{:S(2)}, u32[]{:S(2)}) collective-permute-start(f32[48,128]{1,0:T(8,128)S(1)} %get-tuple-element.49), channel_id=1, source_target_pairs={{0,16},{16,0},{32,48},{48,32},{64,80},{80,64},{96,112},{112,96},{1... | collective-permute-start | bytes 73736 | tf_op jit(solution)/shard_map/ppermute | solution.py:635
  59.5 0.0 all-to-all-done
  59.5 0.6 shard_map.65
  60.1 4.2 %all-to-all-start.1 = ((f32[32,2,128]{2,1,0:T(2,128)}), f32[32,2,128]{2,1,0:T(2,128)S(1)}, u32[]{:S(2)}, u32[]{:S(2)}) async-start(f32[32,2,128]{2,1,0:T(2,128)} %bitcast.5), calls=%async_computation.1 | async-start | bytes 65536 | tf_op jit(solution)/shard_map/all_to_all | solution.py:641
  64.4 0.0 collective-permute-done.8.refs_1_
  64.4 0.0 collective-permute-done.9.refs_2_
  64.4 0.5 shard_map.64
  64.8 3.5 %collective-permute-start.10 = (f32[32,128]{1,0:T(8,128)S(1)}, f32[32,128]{1,0:T(8,128)S(1)}, u32[]{:S(2)}, u32[]{:S(2)}) collective-permute-start(f32[32,128]{1,0:T(8,128)S(1)} %get-tuple-element.53), channel_id=1, source_target_pairs={{0,496},{16,32},{32,16},{48,64},{64,48},{80,96},{96,80},{112,128},... | collective-permute-start | bytes 49160 | tf_op jit(solution)/shard_map/ppermute | solution.py:635
  68.4 5.5 %collective-permute-start.11 = (f32[32,128]{1,0:T(8,128)S(1)}, f32[32,128]{1,0:T(8,128)S(1)}, u32[]{:S(2)}, u32[]{:S(2)}) collective-permute-start(f32[32,128]{1,0:T(8,128)S(1)} %get-tuple-element.54), channel_id=1, source_target_pairs={{0,16},{16,0},{32,48},{48,32},{64,80},{80,64},{96,112},{112,96},{1... | collective-permute-start | bytes 49160 | tf_op jit(solution)/shard_map/ppermute | solution.py:635
  73.9 0.0 all-to-all-done.1
  73.9 0.0 collective-permute-done.10.across_ref
  73.9 0.8 collective-permute-done.11.within_ref
  74.7 0.7 shard_map.66
  75.4 11.2 %all_to_all.20.received_ref = f32[32,16,128]{2,1,0:T(8,128)S(1)} all-to-all(f32[32,16,128]{2,1,0:T(8,128)S(1)} %get-tuple-element.58), channel_id=1, replica_groups={{320,336,352,368,384,400,416,432,448,464,480,496,0,16,32,48,64,80,96,11..., dimensions={0} | all-to-all | bytes 524288 | tf_op jit(solution)/shard_map/all_to_all | solution.py:641
  86.6 15.9 %all_to_all.21.received_ref = f32[16,8,128]{2,1,0:T(8,128)S(1)} all-to-all(f32[16,8,128]{2,1,0:T(8,128)S(1)} %get-tuple-element.60), channel_id=1, replica_groups={{9,10,11,12,13,14,15,0,1,2,3,4,5,6,7,8},{25,26,27,28,29,30,31,16,17,18,..., dimensions={0} | all-to-all | bytes 131072 | tf_op jit(solution)/shard_map/all_to_all | solution.py:641
  102.6 0.8 shard_map.68
  (2 shorter events, 0.1 us)
Async XLA Ops:
  0.6 24.0 %copy-start = (f32[232,128]{1,0:T(8,128)S(1)}, f32[232,128]{1,0:T(8,128)}, u32[]{:S(2)}) copy-start(f32[232,128]{1,0:T(8,128)} %constant.5.clone.table_ref.refs_8_) | copy-start | bytes 356356
  1.7 23.9 %collective-permute-start = (f32[136,128]{1,0:T(8,128)S(1)}, f32[136,128]{1,0:T(8,128)S(1)}, u32[]{:S(2)}, u32[]{:S(2)}) collective-permute-start(f32[136,128]{1,0:T(8,128)S(1)} %get-tuple-element.33.near_ref), channel_id=1, source_target_pairs={{0,1},{1,0},{2,3},{3,2},{4,5},{5,4},{6,7},{7,6},{8,9},{9,8},{10,11... | collective-permute-start | bytes 208904 | tf_op jit(solution)/shard_map/ppermute | solution.py:627
  6.1 19.5 %collective-permute-start.1 = (f32[136,128]{1,0:T(8,128)S(1)}, f32[136,128]{1,0:T(8,128)S(1)}, u32[]{:S(2)}, u32[]{:S(2)}) collective-permute-start(f32[136,128]{1,0:T(8,128)S(1)} %get-tuple-element.33.near_ref), channel_id=1, source_target_pairs={{0,15},{1,2},{2,1},{3,4},{4,3},{5,6},{6,5},{7,8},{8,7},{9,10},{10,... | collective-permute-start | bytes 208904 | tf_op jit(solution)/shard_map/ppermute | solution.py:627
  16.3 9.3 %collective-permute-start.2 = (f32[80,128]{1,0:T(8,128)S(1)}, f32[80,128]{1,0:T(8,128)S(1)}, u32[]{:S(2)}, u32[]{:S(2)}) collective-permute-start(f32[80,128]{1,0:T(8,128)S(1)} %get-tuple-element.34), channel_id=1, source_target_pairs={{0,2},{1,3},{2,0},{3,1},{4,6},{5,7},{6,4},{7,5},{8,10},{9,11},{10,... | collective-permute-start | bytes 122888 | tf_op jit(solution)/shard_map/ppermute | solution.py:627
  18.2 7.4 %collective-permute-start.3 = (f32[80,128]{1,0:T(8,128)S(1)}, f32[80,128]{1,0:T(8,128)S(1)}, u32[]{:S(2)}, u32[]{:S(2)}) collective-permute-start(f32[80,128]{1,0:T(8,128)S(1)} %get-tuple-element.35), channel_id=1, source_target_pairs={{0,14},{1,15},{2,4},{3,5},{4,2},{5,3},{6,8},{7,9},{8,6},{9,7},{10,... | collective-permute-start | bytes 122888 | tf_op jit(solution)/shard_map/ppermute | solution.py:627
  26.4 16.3 %collective-permute-start.4 = (f32[104,128]{1,0:T(8,128)S(1)}, f32[104,128]{1,0:T(8,128)S(1)}, u32[]{:S(2)}, u32[]{:S(2)}) collective-permute-start(f32[104,128]{1,0:T(8,128)S(1)} %get-tuple-element.39), channel_id=1, source_target_pairs={{0,496},{16,32},{32,16},{48,64},{64,48},{80,96},{96,80},{112,128},... | collective-permute-start | bytes 159752 | tf_op jit(solution)/shard_map/ppermute | solution.py:635
  31.3 11.3 %collective-permute-start.5 = (f32[104,128]{1,0:T(8,128)S(1)}, f32[104,128]{1,0:T(8,128)S(1)}, u32[]{:S(2)}, u32[]{:S(2)}) collective-permute-start(f32[104,128]{1,0:T(8,128)S(1)} %get-tuple-element.40), channel_id=1, source_target_pairs={{0,16},{16,0},{32,48},{48,32},{64,80},{80,64},{96,112},{112,96},{1... | collective-permute-start | bytes 159752 | tf_op jit(solution)/shard_map/ppermute | solution.py:635
  35.5 23.9 %all-to-all-start = ((f32[16,2,128]{2,1,0:T(2,128)}), f32[16,2,128]{2,1,0:T(2,128)S(1)}, u32[]{:S(2)}, u32[]{:S(2)}) async-start(f32[16,2,128]{2,1,0:T(2,128)} %bitcast.3), calls=%async_computation | async-start | bytes 32768 | tf_op jit(solution)/shard_map/all_to_all | solution.py:641
  43.5 6.5 %collective-permute-start.6 = (f32[64,128]{1,0:T(8,128)S(1)}, f32[64,128]{1,0:T(8,128)S(1)}, u32[]{:S(2)}, u32[]{:S(2)}) collective-permute-start(f32[64,128]{1,0:T(8,128)S(1)} %get-tuple-element.42), channel_id=1, source_target_pairs={{0,496},{16,32},{32,16},{48,64},{64,48},{80,96},{96,80},{112,128},... | collective-permute-start | bytes 98312 | tf_op jit(solution)/shard_map/ppermute | solution.py:635
  45.9 4.9 %collective-permute-start.7 = (f32[64,128]{1,0:T(8,128)S(1)}, f32[64,128]{1,0:T(8,128)S(1)}, u32[]{:S(2)}, u32[]{:S(2)}) collective-permute-start(f32[64,128]{1,0:T(8,128)S(1)} %get-tuple-element.43), channel_id=1, source_target_pairs={{0,16},{16,0},{32,48},{48,32},{64,80},{80,64},{96,112},{112,96},{1... | collective-permute-start | bytes 98312 | tf_op jit(solution)/shard_map/ppermute | solution.py:635
  51.5 12.9 %collective-permute-start.8 = (f32[48,128]{1,0:T(8,128)S(1)}, f32[48,128]{1,0:T(8,128)S(1)}, u32[]{:S(2)}, u32[]{:S(2)}) collective-permute-start(f32[48,128]{1,0:T(8,128)S(1)} %get-tuple-element.48), channel_id=1, source_target_pairs={{0,496},{16,32},{32,16},{48,64},{64,48},{80,96},{96,80},{112,128},... | collective-permute-start | bytes 73736 | tf_op jit(solution)/shard_map/ppermute | solution.py:635
  53.4 11.0 %collective-permute-start.9 = (f32[48,128]{1,0:T(8,128)S(1)}, f32[48,128]{1,0:T(8,128)S(1)}, u32[]{:S(2)}, u32[]{:S(2)}) collective-permute-start(f32[48,128]{1,0:T(8,128)S(1)} %get-tuple-element.49), channel_id=1, source_target_pairs={{0,16},{16,0},{32,48},{48,32},{64,80},{80,64},{96,112},{112,96},{1... | collective-permute-start | bytes 73736 | tf_op jit(solution)/shard_map/ppermute | solution.py:635
  60.1 13.7 %all-to-all-start.1 = ((f32[32,2,128]{2,1,0:T(2,128)}), f32[32,2,128]{2,1,0:T(2,128)S(1)}, u32[]{:S(2)}, u32[]{:S(2)}) async-start(f32[32,2,128]{2,1,0:T(2,128)} %bitcast.5), calls=%async_computation.1 | async-start | bytes 65536 | tf_op jit(solution)/shard_map/all_to_all | solution.py:641
  64.8 9.0 %collective-permute-start.10 = (f32[32,128]{1,0:T(8,128)S(1)}, f32[32,128]{1,0:T(8,128)S(1)}, u32[]{:S(2)}, u32[]{:S(2)}) collective-permute-start(f32[32,128]{1,0:T(8,128)S(1)} %get-tuple-element.53), channel_id=1, source_target_pairs={{0,496},{16,32},{32,16},{48,64},{64,48},{80,96},{96,80},{112,128},... | collective-permute-start | bytes 49160 | tf_op jit(solution)/shard_map/ppermute | solution.py:635
  68.4 6.3 %collective-permute-start.11 = (f32[32,128]{1,0:T(8,128)S(1)}, f32[32,128]{1,0:T(8,128)S(1)}, u32[]{:S(2)}, u32[]{:S(2)}) collective-permute-start(f32[32,128]{1,0:T(8,128)S(1)} %get-tuple-element.54), channel_id=1, source_target_pairs={{0,16},{16,0},{32,48},{48,32},{64,80},{80,64},{96,112},{112,96},{1... | collective-permute-start | bytes 49160 | tf_op jit(solution)/shard_map/ppermute | solution.py:635

commit v8 on v7

--- a/solution.py
+++ b/solution.py
@@ -11,7 +11,7 @@
 N_GZ = 16
 F32 = jnp.float32
 HIGHEST = lax.Precision.HIGHEST
-TREE_Z, TREE_X = 0, 0
+TREE_Z, TREE_X = 0, 7
 END_Z, END_X = 9, 20
 
 cheb_high = 2.0
@@ -171,8 +171,8 @@
 
 def sum_y(field):
     lane = lane_iota()
-    first = (lane % 8 == 0) & (lane > 0)
-    last = (lane % 8 == 7) & (lane < 127)
+    first = ((lane & 7) == 0) & (lane > 0)
+    last = ((lane & 7) == 7) & (lane < 127)
     return each(
         lambda value: value
         + jnp.where(last, pltpu.roll(value, 127, 1), jnp.where(first, pltpu.roll(value, 1, 1), 0.0)),
@@ -240,7 +240,7 @@
         sum_of_x, sum_of_rest = part_x, part_rest
         if i in (0, 7):
             side = left_ref if i == 0 else right_ref
-            side_x, side_rest = diagonal_parts(side, Facross_refE_METRIC, column, table_ref)
+            side_x, side_rest = diagonal_parts(side, FACE_METRIC, column, table_ref)
             sum_of_x, sum_of_rest = part_x + side_x, part_rest + side_rest
         out.append(KD[i] * sum_of_x + W[i] * sum_of_rest)
     return out
@@ -292,7 +292,7 @@
     begins = lax.rem(lax.axis_index("gz"), 4) < 2
     element = lax.broadcasted_iota(jnp.int32, (16, 128), 0)
     lane = lax.broadcasted_iota(jnp.int32, (16, 128), 1)
-    expand = jnp.where(element == lane // 8, 1.0, 0.0)
+    expand = jnp.where(element == (lane >> 3), 1.0, 0.0)
     for ref, start in ((near_ref, 128), (inner_ref, 72), (outer_ref, 72)):
         ref[start + 6 : start + 8, :] = jnp.zeros((2, 128), F32)
     for m in range(3):
@@ -312,29 +312,35 @@
         outer_ref[64 + i : 65 + i, :] = jnp.where(begins, down, up)
 
 
-Facross_refE_METRIC = 72
-Facross_refE_ROWS = 104
+FACE_METRIC = 72
+FACE_ROWS = 104
+
+
+def neighbours_z(even_ref, odd_ref, inner_ref, outer_ref):
+    place = lax.axis_index("gz")
+    return (
+        Either(lax.rem(place, 4) >= 2, inner_ref, outer_ref),
+        Either(lax.rem(place, 2) == 1, even_ref, odd_ref),
+        Either(lax.rem(place, 2) == 0, even_ref, odd_ref),
+        Either(lax.rem(place, 4) < 2, inner_ref, outer_ref),
+    )
+
+
+def wide_load(near_ref, far_below_ref, below_ref, above_ref, far_above_ref, i):
+    far = slice(8 * i, 8 * i + 8)
+    pair = [slice(8 * (2 * i + z), 8 * (2 * i + z) + 8) for z in range(2)]
+    return (
+        [far_below_ref[far, :]]
+        + [ref[rows, :] for ref in (below_ref, near_ref, above_ref) for rows in pair]
+        + [far_above_ref[far, :]]
+    )
 
 
 def gather(
-    near_ref, even_ref, odd_ref, inner_ref, outer_ref, earlier_ref,
-    load_ref, edge_ref, rows_ref, low_ref, high_ref,
+    near_ref, even_ref, odd_ref, inner_ref, outer_ref, earlier_ref, rows_ref, across_ref, within_ref
 ):
-    place = lax.axis_index("gz")
-    above_ref = Either(lax.rem(place, 2) == 0, even_ref, odd_ref)
-    below_ref = Either(lax.rem(place, 2) == 1, even_ref, odd_ref)
-    far_above_ref = Either(lax.rem(place, 4) < 2, inner_ref, outer_ref)
-    far_below_ref = Either(lax.rem(place, 4) >= 2, inner_ref, outer_ref)
-    for i in range(8):
-        load_ref[i, 0] = far_below_ref[8 * i : 8 * i + 8, :]
-        load_ref[i, 7] = far_above_ref[8 * i : 8 * i + 8, :]
-        for z in range(2):
-            start = 8 * (2 * i + z)
-            load_ref[i, 1 + z] = below_ref[start : start + 8, :]
-            load_ref[i, 3 + z] = near_ref[start : start + 8, :]
-            load_ref[i, 5 + z] = above_ref[start : start + 8, :]
-    edge_ref[0:8, :] = far_below_ref[64:72, :]
-    edge_ref[8:16, :] = far_above_ref[64:72, :]
+    messages = neighbours_z(even_ref, odd_ref, inner_ref, outer_ref)
+    far_below_ref, below_ref, above_ref, far_above_ref = messages
     sources = (
         (far_below_ref, 72), (below_ref, 128), (near_ref, 128), (above_ref, 128), (far_above_ref, 72),
     )
@@ -344,14 +350,15 @@
             rows_ref[row : row + 2, :] = source[start + 2 * m : start + 2 * m + 2, :]
     rows_ref[30:32, :] = jnp.zeros((2, 128), F32)
     rows = rows_ref[...]
-    out = Faces(low_ref, high_ref)
+    out = Faces(across_ref, within_ref)
+    lows, highs = wide_load(near_ref, *messages, 0), wide_load(near_ref, *messages, 7)
     for c in range(8):
-        out.put(8 * c, 8 * c + 8, load_ref[0, c], load_ref[7, c])
+        out.put(8 * c, 8 * c + 8, lows[c], highs[c])
     for row, ref in ((64, far_below_ref), (65, far_above_ref)):
         out.put(row, row + 1, ref[64:65, :], ref[71:72, :])
-    for ref in (low_ref, high_ref):
+    for ref in (across_ref, within_ref):
         ref[66:72, :] = jnp.zeros((6, 128), F32)
-        ref[Facross_refE_METRIC:Facross_refE_ROWS, :] = rows
+        ref[FACE_METRIC:FACE_ROWS, :] = rows
 
 
 def with_sums(face, first, second):
@@ -412,7 +419,7 @@
         stacked, table(table_ref, "modes"), (((1,), (1,)), ((), ())),
         precision=HIGHEST, preferred_element_type=F32,
     )
-    owner = lax.broadcasted_iota(jnp.int32, (8, 32), 1) // 8
+    owner = lax.broadcasted_iota(jnp.int32, (8, 32), 1) >> 3
     row = lax.broadcasted_iota(jnp.int32, (8, 32), 0)
     coarse_rhs = jnp.sum(jnp.where(owner == row, modes, 0.0), axis=0, keepdims=True)
     own = jnp.dot(
@@ -423,16 +430,16 @@
 
 
 def begin(
-    load_ref, edge_ref, rows_ref, across_ref, within_ref, table_ref,
+    near_ref, even_ref, odd_ref, inner_ref, outer_ref, rows_ref, across_ref, within_ref, table_ref,
     rhs_ref, inverse_ref, smooth_ref, applied_ref, across_out, within_out,
 ):
     left_ref, right_ref = sides(across_ref, within_ref)
 
+    messages = neighbours_z(even_ref, odd_ref, inner_ref, outer_ref)
+
     def edge(which):
-        start = 8 * which
-
         def row(i):
-            value = edge_ref[start + i : start + i + 1, :]
+            value = messages[3 * which][64 + i : 65 + i, :]
             if i == 0:
                 value = value + left_ref[64 + which : 65 + which, :]
             if i == 7:
@@ -441,7 +448,8 @@
 
         return row
 
-    load = sum_x(read(load_ref, 0, 8), faces(left_ref, 8), faces(right_ref, 8))
+    load = [wide_load(near_ref, *messages, i) for i in range(8)]
+    load = sum_x(load, faces(left_ref, 8), faces(right_ref, 8))
     rhs = each(wall, sum_y(sum_z(load, edge(0), edge(1))))
     columns = [
         diagonal_sum_x(rows_ref, left_ref, right_ref, column, table_ref) for column in range(-4, 6)
@@ -459,23 +467,23 @@
 
 def write_pairs(ref, first, second):
     row = lax.broadcasted_iota(jnp.int32, (8, 128), 0)
-    pairs = jnp.where(row % 2 == 0, spread(first), spread(second))
+    pairs = jnp.where((row & 1) == 0, spread(first), spread(second))
     for start in range(0, ref.shape[0], 8):
         ref[start : start + 8, :] = pairs
 
 
 def tree_sums(ref, here, skipped, head):
     row = lax.broadcasted_iota(jnp.int32, (8, 128), 0)
-    level = (row % 2) * 8 + lane_iota() // 16
+    level = (row & 1) * 8 + (lane_iota() >> 4)
     shift = jnp.maximum(level - skipped, 0)
     mine = lax.shift_right_logical(jnp.full((8, 128), here, jnp.int32), shift)
     total = jnp.zeros((8, 128), F32)
     for start in range(0, ref.shape[0], 8):
-        device = (head + start // 2 + row // 2) % (ref.shape[0] // 2)
+        device = (head + start // 2 + (row >> 1)) & (ref.shape[0] // 2 - 1)
         other = lax.shift_right_logical(device, shift)
         total = total + jnp.where(other == mine, ref[start : start + 8, :], 0.0)
-    first = jnp.sum(jnp.where(row % 2 == 0, total, 0.0), axis=0, keepdims=True)
-    second = jnp.sum(jnp.where(row % 2 == 1, total, 0.0), axis=0, keepdims=True)
+    first = jnp.sum(jnp.where((row & 1) == 0, total, 0.0), axis=0, keepdims=True)
+    second = jnp.sum(jnp.where((row & 1) == 1, total, 0.0), axis=0, keepdims=True)
     return first, second
 
 
@@ -533,7 +541,7 @@
         columns, factor_ref[...], (((1,), (1,)), ((), ())),
         precision=HIGHEST, preferred_element_type=F32,
     )
-    owner = lax.broadcasted_iota(jnp.int32, (8, 32), 1) // 8
+    owner = lax.broadcasted_iota(jnp.int32, (8, 32), 1) >> 3
     row = lax.broadcasted_iota(jnp.int32, (8, 32), 0)
     across = jnp.dot(
         jnp.where(owner == row, coarse, 0.0), table(table_ref, "modes"),
@@ -609,15 +617,18 @@
     return (8, count, 8, 128)
 
 
-def run(kernel, shapes, *operands, first=False, last=False):
+def run(kernel, shapes, *operands, first=False, last=False, after=None):
     spec = pl.BlockSpec(memory_space=pltpu.VMEM)
     outs = [
         jax.ShapeDtypeStruct(shape, F32) if last else pltpu.VMEM(shape, F32) for shape in shapes
     ]
     if not first:
         operands = [pltpu.with_memory_space_constraint(value, pltpu.VMEM) for value in operands]
+    specs = [spec] * len(operands)
+    if after is not None:
+        operands, specs = [*operands, after], [*specs, pl.BlockSpec(memory_space=pl.ANY)]
     return pl.pallas_call(
-        kernel, out_shape=outs, in_specs=[spec] * len(operands), out_specs=[spec] * len(outs)
+        kernel, out_shape=outs, in_specs=specs, out_specs=[spec] * len(outs)
     )(*operands)
 
 
@@ -656,14 +667,14 @@
     far_inner, far_outer = swap_z(inner, 2), swap_z(outer, 2, 2)
     (send,) = run(coarse_start, [(2 * N_GZ, 128)], near, factor, constants)
     tree = send_pairs(send, "gz", TREE_Z)
-    wide, edge, rows, low, high = run(
-        gather, [field_shape(8), (16, 128), (32, 128)] + [(Facross_refE_ROWS, 128)] * 2,
-        near, near_even, near_odd, far_inner, far_outer, send,
+    rows, low, high = run(
+        gather, [(32, 128)] + [(FACE_ROWS, 128)] * 2,
+        near, near_even, near_odd, far_inner, far_outer, after=send,
     )
     left, right = swap_x(low, high)
     rhs, inverse, smooth, applied, low, high = run(
         begin, [field_shape(6)] * 3 + [field_shape(8)] + [(64, 128)] * 2,
-        wide, edge, rows, left, right, constants,
+        near, near_even, near_odd, far_inner, far_outer, rows, left, right, constants,
     )
     left, right = swap_x(low, high)
     (send,) = run(lower_tree, [(2 * N_GX, 128)], tree)

time: 104 us -> 102 us (0.981)
  starting transfers between devices: 65.9 us -> 63.5 us
    ppermute x4, starting transfers between devices: 19.8 us -> 18.2 us  [swap_x(): lax.ppermute(within, 'gx', inside)]
where the time goes in v8:
time: 102 us; the launch traced here: 101 us
  starting transfers between devices  63.5 us (62%)
  blocking collectives  28.1 us (28%)
  Pallas kernels  6.07 us (6%)
  waiting for transfers between devices  1.65 us (2%)
    all_to_all x2, blocking collectives, send_chunks(): lax.all_to_all(chunks, axis, 0, 0, tiled=True, axis_index_groups=[group])  28.1 us
    ppermute x4, starting transfers between devices, swap_z(): return lax.ppermute(value, 'gz', pairs)  22 us
    ppermute x4, starting transfers between devices, swap_x(): lax.ppermute(within, 'gx', inside)  18.2 us
    ppermute x4, starting transfers between devices, swap_x(): lax.ppermute(across, 'gx', over)  12 us
    all_to_all x2, starting transfers between devices, send_chunks(): lax.all_to_all(chunks, axis, 0, 0, tiled=True, axis_index_groups=[group])  11.3 us
    pallas_call x10, Pallas kernels, run(): pl.pallas_call(kernel, out_shape=outs, in_specs=specs, out_specs=[spec] *...  6.07 us
  transfers between devices with their start and end apart: 14, of which 2 were waited for; matrix products, arithmetic and copies ran while one was open for 1% of the time, Pallas kernels for 3%

profile of v8, /device:TPU:1, one launch (start us, length us, event | category | flops | bytes accessed | tf_op | source)
XLA Modules:
  0.0 101.2 jit_solution(13436121243066456364)
XLA Ops:
  0.6 0.0 copy-start
  0.6 1.0 %shard_map.59 = (f32[136,128]{1,0:T(8,128)S(1)}, f32[80,128]{1,0:T(8,128)S(1)}, f32[80,128]{1,0:T(8,128)S(1)}) custom-call(f32[1,8,2,8,128]{4,3,2,1,0:T(8,128)} %load_ref.1, f32[3,1,2,16]{3,2,1,0:T(2,128)} %metric_ref.1), custom_call_target="tpu_custom_call" | custom-call | tf_op jit(solution)/shard_map/pallas_call | solution.py:630
  1.7 4.4 %collective-permute-start = (f32[136,128]{1,0:T(8,128)S(1)}, f32[136,128]{1,0:T(8,128)S(1)}, u32[]{:S(2)}, u32[]{:S(2)}) collective-permute-start(f32[136,128]{1,0:T(8,128)S(1)} %get-tuple-element.31.near_ref), channel_id=1, source_target_pairs={{0,1},{1,0},{2,3},{3,2},{4,5},{5,4},{6,7},{7,6},{8,9},{9,8},{10,11... | collective-permute-start | bytes 208904 | tf_op jit(solution)/shard_map/ppermute | solution.py:638
  6.1 10.2 %collective-permute-start.1 = (f32[136,128]{1,0:T(8,128)S(1)}, f32[136,128]{1,0:T(8,128)S(1)}, u32[]{:S(2)}, u32[]{:S(2)}) collective-permute-start(f32[136,128]{1,0:T(8,128)S(1)} %get-tuple-element.31.near_ref), channel_id=1, source_target_pairs={{0,15},{1,2},{2,1},{3,4},{4,3},{5,6},{6,5},{7,8},{8,7},{9,10},{10,... | collective-permute-start | bytes 208904 | tf_op jit(solution)/shard_map/ppermute | solution.py:638
  16.3 1.9 %collective-permute-start.2 = (f32[80,128]{1,0:T(8,128)S(1)}, f32[80,128]{1,0:T(8,128)S(1)}, u32[]{:S(2)}, u32[]{:S(2)}) collective-permute-start(f32[80,128]{1,0:T(8,128)S(1)} %get-tuple-element.32), channel_id=1, source_target_pairs={{0,2},{1,3},{2,0},{3,1},{4,6},{5,7},{6,4},{7,5},{8,10},{9,11},{10,... | collective-permute-start | bytes 122888 | tf_op jit(solution)/shard_map/ppermute | solution.py:638
  18.2 5.5 %collective-permute-start.3 = (f32[80,128]{1,0:T(8,128)S(1)}, f32[80,128]{1,0:T(8,128)S(1)}, u32[]{:S(2)}, u32[]{:S(2)}) collective-permute-start(f32[80,128]{1,0:T(8,128)S(1)} %get-tuple-element.33), channel_id=1, source_target_pairs={{0,14},{1,15},{2,4},{3,5},{4,2},{5,3},{6,8},{7,9},{8,6},{9,7},{10,... | collective-permute-start | bytes 122888 | tf_op jit(solution)/shard_map/ppermute | solution.py:638
  23.7 1.0 copy.7
  24.6 0.0 copy-done
  24.7 0.9 shard_map.60.earlier_ref
  25.6 0.0 collective-permute-done.2.inner_ref
  25.6 0.0 collective-permute-done.3.outer_ref
  25.6 0.0 collective-permute-done.even_ref
  25.6 0.0 collective-permute-done.1.odd_ref
  25.7 4.9 %collective-permute-start.4 = (f32[104,128]{1,0:T(8,128)S(1)}, f32[104,128]{1,0:T(8,128)S(1)}, u32[]{:S(2)}, u32[]{:S(2)}) collective-permute-start(f32[104,128]{1,0:T(8,128)S(1)} %get-tuple-element.35), channel_id=1, source_target_pairs={{0,496},{16,32},{32,16},{48,64},{64,48},{80,96},{96,80},{112,128},... | collective-permute-start | bytes 159752 | tf_op jit(solution)/shard_map/ppermute | solution.py:646
  30.6 4.2 %collective-permute-start.5 = (f32[104,128]{1,0:T(8,128)S(1)}, f32[104,128]{1,0:T(8,128)S(1)}, u32[]{:S(2)}, u32[]{:S(2)}) collective-permute-start(f32[104,128]{1,0:T(8,128)S(1)} %get-tuple-element.36), channel_id=1, source_target_pairs={{0,16},{16,0},{32,48},{48,32},{64,80},{80,64},{96,112},{112,96},{1... | collective-permute-start | bytes 159752 | tf_op jit(solution)/shard_map/ppermute | solution.py:646
  34.8 7.1 %all-to-all-start = ((f32[16,2,128]{2,1,0:T(2,128)}), f32[16,2,128]{2,1,0:T(2,128)S(1)}, u32[]{:S(2)}, u32[]{:S(2)}) async-start(f32[16,2,128]{2,1,0:T(2,128)} %bitcast.3), calls=%async_computation | async-start | bytes 32768 | tf_op jit(solution)/shard_map/all_to_all | solution.py:652
  41.9 0.0 collective-permute-done.4.across_ref
  41.9 0.0 collective-permute-done.5.within_ref
  41.9 0.8 shard_map.62
  42.8 2.4 %collective-permute-start.6 = (f32[64,128]{1,0:T(8,128)S(1)}, f32[64,128]{1,0:T(8,128)S(1)}, u32[]{:S(2)}, u32[]{:S(2)}) collective-permute-start(f32[64,128]{1,0:T(8,128)S(1)} %get-tuple-element.38), channel_id=1, source_target_pairs={{0,496},{16,32},{32,16},{48,64},{64,48},{80,96},{96,80},{112,128},... | collective-permute-start | bytes 98312 | tf_op jit(solution)/shard_map/ppermute | solution.py:646
  45.2 4.1 %collective-permute-start.7 = (f32[64,128]{1,0:T(8,128)S(1)}, f32[64,128]{1,0:T(8,128)S(1)}, u32[]{:S(2)}, u32[]{:S(2)}) collective-permute-start(f32[64,128]{1,0:T(8,128)S(1)} %get-tuple-element.39), channel_id=1, source_target_pairs={{0,16},{16,0},{32,48},{48,32},{64,80},{80,64},{96,112},{112,96},{1... | collective-permute-start | bytes 98312 | tf_op jit(solution)/shard_map/ppermute | solution.py:646
  49.3 0.0 collective-permute-done.6.refs_1_
  49.3 0.8 collective-permute-done.7.refs_2_
  50.1 0.6 shard_map.63
  50.7 1.9 %collective-permute-start.8 = (f32[48,128]{1,0:T(8,128)S(1)}, f32[48,128]{1,0:T(8,128)S(1)}, u32[]{:S(2)}, u32[]{:S(2)}) collective-permute-start(f32[48,128]{1,0:T(8,128)S(1)} %get-tuple-element.44), channel_id=1, source_target_pairs={{0,496},{16,32},{32,16},{48,64},{64,48},{80,96},{96,80},{112,128},... | collective-permute-start | bytes 73736 | tf_op jit(solution)/shard_map/ppermute | solution.py:646
  52.7 6.1 %collective-permute-start.9 = (f32[48,128]{1,0:T(8,128)S(1)}, f32[48,128]{1,0:T(8,128)S(1)}, u32[]{:S(2)}, u32[]{:S(2)}) collective-permute-start(f32[48,128]{1,0:T(8,128)S(1)} %get-tuple-element.45), channel_id=1, source_target_pairs={{0,16},{16,0},{32,48},{48,32},{64,80},{80,64},{96,112},{112,96},{1... | collective-permute-start | bytes 73736 | tf_op jit(solution)/shard_map/ppermute | solution.py:646
  58.8 0.0 all-to-all-done
  58.8 0.6 shard_map.65
  59.4 4.2 %all-to-all-start.1 = ((f32[32,2,128]{2,1,0:T(2,128)}), f32[32,2,128]{2,1,0:T(2,128)S(1)}, u32[]{:S(2)}, u32[]{:S(2)}) async-start(f32[32,2,128]{2,1,0:T(2,128)} %bitcast.5), calls=%async_computation.1 | async-start | bytes 65536 | tf_op jit(solution)/shard_map/all_to_all | solution.py:652
  63.6 0.0 collective-permute-done.8.refs_1_
  63.6 0.0 collective-permute-done.9.refs_2_
  63.6 0.5 shard_map.64
  64.1 2.7 %collective-permute-start.10 = (f32[32,128]{1,0:T(8,128)S(1)}, f32[32,128]{1,0:T(8,128)S(1)}, u32[]{:S(2)}, u32[]{:S(2)}) collective-permute-start(f32[32,128]{1,0:T(8,128)S(1)} %get-tuple-element.49), channel_id=1, source_target_pairs={{0,496},{16,32},{32,16},{48,64},{64,48},{80,96},{96,80},{112,128},... | collective-permute-start | bytes 49160 | tf_op jit(solution)/shard_map/ppermute | solution.py:646
  66.8 3.8 %collective-permute-start.11 = (f32[32,128]{1,0:T(8,128)S(1)}, f32[32,128]{1,0:T(8,128)S(1)}, u32[]{:S(2)}, u32[]{:S(2)}) collective-permute-start(f32[32,128]{1,0:T(8,128)S(1)} %get-tuple-element.50), channel_id=1, source_target_pairs={{0,16},{16,0},{32,48},{48,32},{64,80},{80,64},{96,112},{112,96},{1... | collective-permute-start | bytes 49160 | tf_op jit(solution)/shard_map/ppermute | solution.py:646
  70.7 0.0 all-to-all-done.1
  70.7 0.0 collective-permute-done.10.across_ref
  70.7 0.8 collective-permute-done.11.within_ref
  71.5 0.7 shard_map.66
  72.2 12.2 %all_to_all.20.received_ref = f32[32,16,128]{2,1,0:T(8,128)S(1)} all-to-all(f32[32,16,128]{2,1,0:T(8,128)S(1)} %get-tuple-element.54), channel_id=1, replica_groups={{320,336,352,368,384,400,416,432,448,464,480,496,0,16,32,48,64,80,96,11..., dimensions={0} | all-to-all | bytes 524288 | tf_op jit(solution)/shard_map/all_to_all | solution.py:652
  84.4 15.9 %all_to_all.21.received_ref = f32[16,8,128]{2,1,0:T(8,128)S(1)} all-to-all(f32[16,8,128]{2,1,0:T(8,128)S(1)} %get-tuple-element.56), channel_id=1, replica_groups={{9,10,11,12,13,14,15,0,1,2,3,4,5,6,7,8},{25,26,27,28,29,30,31,16,17,18,..., dimensions={0} | all-to-all | bytes 131072 | tf_op jit(solution)/shard_map/all_to_all | solution.py:652
  100.4 0.8 shard_map.68
  (3 shorter events, 0.1 us)
Async XLA Ops:
  0.6 24.0 %copy-start = (f32[232,128]{1,0:T(8,128)S(1)}, f32[232,128]{1,0:T(8,128)}, u32[]{:S(2)}) copy-start(f32[232,128]{1,0:T(8,128)} %constant.5.clone.table_ref.refs_8_) | copy-start | bytes 356356
  1.7 23.9 %collective-permute-start = (f32[136,128]{1,0:T(8,128)S(1)}, f32[136,128]{1,0:T(8,128)S(1)}, u32[]{:S(2)}, u32[]{:S(2)}) collective-permute-start(f32[136,128]{1,0:T(8,128)S(1)} %get-tuple-element.31.near_ref), channel_id=1, source_target_pairs={{0,1},{1,0},{2,3},{3,2},{4,5},{5,4},{6,7},{7,6},{8,9},{9,8},{10,11... | collective-permute-start | bytes 208904 | tf_op jit(solution)/shard_map/ppermute | solution.py:638
  6.1 19.5 %collective-permute-start.1 = (f32[136,128]{1,0:T(8,128)S(1)}, f32[136,128]{1,0:T(8,128)S(1)}, u32[]{:S(2)}, u32[]{:S(2)}) collective-permute-start(f32[136,128]{1,0:T(8,128)S(1)} %get-tuple-element.31.near_ref), channel_id=1, source_target_pairs={{0,15},{1,2},{2,1},{3,4},{4,3},{5,6},{6,5},{7,8},{8,7},{9,10},{10,... | collective-permute-start | bytes 208904 | tf_op jit(solution)/shard_map/ppermute | solution.py:638
  16.3 9.3 %collective-permute-start.2 = (f32[80,128]{1,0:T(8,128)S(1)}, f32[80,128]{1,0:T(8,128)S(1)}, u32[]{:S(2)}, u32[]{:S(2)}) collective-permute-start(f32[80,128]{1,0:T(8,128)S(1)} %get-tuple-element.32), channel_id=1, source_target_pairs={{0,2},{1,3},{2,0},{3,1},{4,6},{5,7},{6,4},{7,5},{8,10},{9,11},{10,... | collective-permute-start | bytes 122888 | tf_op jit(solution)/shard_map/ppermute | solution.py:638
  18.2 7.4 %collective-permute-start.3 = (f32[80,128]{1,0:T(8,128)S(1)}, f32[80,128]{1,0:T(8,128)S(1)}, u32[]{:S(2)}, u32[]{:S(2)}) collective-permute-start(f32[80,128]{1,0:T(8,128)S(1)} %get-tuple-element.33), channel_id=1, source_target_pairs={{0,14},{1,15},{2,4},{3,5},{4,2},{5,3},{6,8},{7,9},{8,6},{9,7},{10,... | collective-permute-start | bytes 122888 | tf_op jit(solution)/shard_map/ppermute | solution.py:638
  25.7 16.3 %collective-permute-start.4 = (f32[104,128]{1,0:T(8,128)S(1)}, f32[104,128]{1,0:T(8,128)S(1)}, u32[]{:S(2)}, u32[]{:S(2)}) collective-permute-start(f32[104,128]{1,0:T(8,128)S(1)} %get-tuple-element.35), channel_id=1, source_target_pairs={{0,496},{16,32},{32,16},{48,64},{64,48},{80,96},{96,80},{112,128},... | collective-permute-start | bytes 159752 | tf_op jit(solution)/shard_map/ppermute | solution.py:646
  30.6 11.3 %collective-permute-start.5 = (f32[104,128]{1,0:T(8,128)S(1)}, f32[104,128]{1,0:T(8,128)S(1)}, u32[]{:S(2)}, u32[]{:S(2)}) collective-permute-start(f32[104,128]{1,0:T(8,128)S(1)} %get-tuple-element.36), channel_id=1, source_target_pairs={{0,16},{16,0},{32,48},{48,32},{64,80},{80,64},{96,112},{112,96},{1... | collective-permute-start | bytes 159752 | tf_op jit(solution)/shard_map/ppermute | solution.py:646
  34.8 23.9 %all-to-all-start = ((f32[16,2,128]{2,1,0:T(2,128)}), f32[16,2,128]{2,1,0:T(2,128)S(1)}, u32[]{:S(2)}, u32[]{:S(2)}) async-start(f32[16,2,128]{2,1,0:T(2,128)} %bitcast.3), calls=%async_computation | async-start | bytes 32768 | tf_op jit(solution)/shard_map/all_to_all | solution.py:652
  42.8 6.5 %collective-permute-start.6 = (f32[64,128]{1,0:T(8,128)S(1)}, f32[64,128]{1,0:T(8,128)S(1)}, u32[]{:S(2)}, u32[]{:S(2)}) collective-permute-start(f32[64,128]{1,0:T(8,128)S(1)} %get-tuple-element.38), channel_id=1, source_target_pairs={{0,496},{16,32},{32,16},{48,64},{64,48},{80,96},{96,80},{112,128},... | collective-permute-start | bytes 98312 | tf_op jit(solution)/shard_map/ppermute | solution.py:646
  45.2 4.9 %collective-permute-start.7 = (f32[64,128]{1,0:T(8,128)S(1)}, f32[64,128]{1,0:T(8,128)S(1)}, u32[]{:S(2)}, u32[]{:S(2)}) collective-permute-start(f32[64,128]{1,0:T(8,128)S(1)} %get-tuple-element.39), channel_id=1, source_target_pairs={{0,16},{16,0},{32,48},{48,32},{64,80},{80,64},{96,112},{112,96},{1... | collective-permute-start | bytes 98312 | tf_op jit(solution)/shard_map/ppermute | solution.py:646
  50.7 12.9 %collective-permute-start.8 = (f32[48,128]{1,0:T(8,128)S(1)}, f32[48,128]{1,0:T(8,128)S(1)}, u32[]{:S(2)}, u32[]{:S(2)}) collective-permute-start(f32[48,128]{1,0:T(8,128)S(1)} %get-tuple-element.44), channel_id=1, source_target_pairs={{0,496},{16,32},{32,16},{48,64},{64,48},{80,96},{96,80},{112,128},... | collective-permute-start | bytes 73736 | tf_op jit(solution)/shard_map/ppermute | solution.py:646
  52.7 10.9 %collective-permute-start.9 = (f32[48,128]{1,0:T(8,128)S(1)}, f32[48,128]{1,0:T(8,128)S(1)}, u32[]{:S(2)}, u32[]{:S(2)}) collective-permute-start(f32[48,128]{1,0:T(8,128)S(1)} %get-tuple-element.45), channel_id=1, source_target_pairs={{0,16},{16,0},{32,48},{48,32},{64,80},{80,64},{96,112},{112,96},{1... | collective-permute-start | bytes 73736 | tf_op jit(solution)/shard_map/ppermute | solution.py:646
  59.4 11.3 %all-to-all-start.1 = ((f32[32,2,128]{2,1,0:T(2,128)}), f32[32,2,128]{2,1,0:T(2,128)S(1)}, u32[]{:S(2)}, u32[]{:S(2)}) async-start(f32[32,2,128]{2,1,0:T(2,128)} %bitcast.5), calls=%async_computation.1 | async-start | bytes 65536 | tf_op jit(solution)/shard_map/all_to_all | solution.py:652
  64.1 6.6 %collective-permute-start.10 = (f32[32,128]{1,0:T(8,128)S(1)}, f32[32,128]{1,0:T(8,128)S(1)}, u32[]{:S(2)}, u32[]{:S(2)}) collective-permute-start(f32[32,128]{1,0:T(8,128)S(1)} %get-tuple-element.49), channel_id=1, source_target_pairs={{0,496},{16,32},{32,16},{48,64},{64,48},{80,96},{96,80},{112,128},... | collective-permute-start | bytes 49160 | tf_op jit(solution)/shard_map/ppermute | solution.py:646
  66.8 4.7 %collective-permute-start.11 = (f32[32,128]{1,0:T(8,128)S(1)}, f32[32,128]{1,0:T(8,128)S(1)}, u32[]{:S(2)}, u32[]{:S(2)}) collective-permute-start(f32[32,128]{1,0:T(8,128)S(1)} %get-tuple-element.50), channel_id=1, source_target_pairs={{0,16},{16,0},{32,48},{48,32},{64,80},{80,64},{96,112},{112,96},{1... | collective-permute-start | bytes 49160 | tf_op jit(solution)/shard_map/ppermute | solution.py:646

commit v9 on v8

--- a/solution.py
+++ b/solution.py
@@ -295,12 +295,10 @@
     expand = jnp.where(element == (lane >> 3), 1.0, 0.0)
     for ref, start in ((near_ref, 128), (inner_ref, 72), (outer_ref, 72)):
         ref[start + 6 : start + 8, :] = jnp.zeros((2, 128), F32)
-    for m in range(3):
-        expanded = jnp.dot(
-            metric_ref[m, 0], expand, precision=HIGHEST, preferred_element_type=F32
-        )
-        for ref, start in ((near_ref, 128), (inner_ref, 72), (outer_ref, 72)):
-            ref[start + 2 * m : start + 2 * m + 2, :] = expanded
+    stacked = jnp.concatenate([metric_ref[m, 0] for m in range(3)], axis=0)
+    expanded = jnp.dot(stacked, expand, precision=HIGHEST, preferred_element_type=F32)
+    for ref, start in ((near_ref, 128), (inner_ref, 72), (outer_ref, 72)):
+        ref[start : start + 6, :] = expanded
     for i in range(8):
         for z in range(2):
             near_ref[8 * (2 * i + z) : 8 * (2 * i + z) + 8, :] = load_ref[0, i, z]
@@ -560,16 +558,20 @@
     return out
 
 
+def coarse_stage(tree_ref, factor_ref, table_ref, coarse_ref, spare_ref):
+    write(coarse_ref, coarse_field(tree_ref, factor_ref, table_ref))
+    spare_ref[...] = jnp.zeros((8, 128), F32)
+
+
 def last_sweep(
     applied_ref, across_ref, within_ref, rhs_ref, inverse_ref, smooth_ref, update_ref, rows_ref,
-    tree_ref, factor_ref, near_ref, table_ref,
+    coarse_ref, near_ref, table_ref,
     precond_ref, out_ref, send_ref,
 ):
     smooth, update = relax(
         2, 2, applied_ref, across_ref, within_ref, rhs_ref, inverse_ref, smooth_ref, update_ref
     )
-    coarse = coarse_field(tree_ref, factor_ref, table_ref)
-    precond = each(lambda s, c: s + c, smooth, coarse)
+    precond = each(lambda s, c: s + c, smooth, read(coarse_ref))
     write(precond_ref, precond)
     applied = element_apply(precond, 0, rows_ref, table_ref)
     write(out_ref, applied)
@@ -690,9 +692,10 @@
             applied, left, right, rhs, inverse, smooth, update, rows, constants,
         )
         left, right = swap_x(low, high)
+    coarse, _ = run(coarse_stage, [field_shape(2), (8, 128)], tree, factor, constants)
     precond, applied, send = run(
         last_sweep, [field_shape(2)] * 2 + [(N_GX, 16, 128)],
-        applied, left, right, rhs, inverse, smooth, update, rows, tree, factor, near, constants,
+        applied, left, right, rhs, inverse, smooth, update, rows, coarse, near, constants,
     )
     received = send_chunks(send, "gx", END_X)
     summed, send = run(middle, [field_shape(2), (N_GZ, 8, 128)], applied, received)

time: 102 us -> 102 us (level)
    pallas_call x10 -> x11, Pallas kernels: 6.07 us -> 6.42 us  [run(): pl.pallas_call(kernel, out_shape=outs, in_specs=specs, out_specs=[spec] *...]
  transfers between devices with their start and end apart: 14 -> 14, of which waited for: 2 -> 2; matrix products, arithmetic and copies ran while one was open for 1% -> 1% of each run, Pallas kernels for 3% -> 4%
where the time goes in v9:
time: 102 us; the launch traced here: 101 us
  starting transfers between devices  63.5 us (62%)
  blocking collectives  28.1 us (28%)
  Pallas kernels  6.42 us (6%)
  waiting for transfers between devices  1.05 us (1%)
    all_to_all x2, blocking collectives, send_chunks(): lax.all_to_all(chunks, axis, 0, 0, tiled=True, axis_index_groups=[group])  28.1 us
    ppermute x4, starting transfers between devices, swap_z(): return lax.ppermute(value, 'gz', pairs)  22 us
    ppermute x4, starting transfers between devices, swap_x(): lax.ppermute(within, 'gx', inside)  18.2 us
    ppermute x4, starting transfers between devices, swap_x(): lax.ppermute(across, 'gx', over)  12 us
    all_to_all x2, starting transfers between devices, send_chunks(): lax.all_to_all(chunks, axis, 0, 0, tiled=True, axis_index_groups=[group])  11.3 us
    pallas_call x11, Pallas kernels, run(): pl.pallas_call(kernel, out_shape=outs, in_specs=specs, out_specs=[spec] *...  6.42 us
  transfers between devices with their start and end apart: 14, of which 2 were waited for; matrix products, arithmetic and copies ran while one was open for 1% of the time, Pallas kernels for 4%

profile of v9, /device:TPU:1, one launch (start us, length us, event | category | flops | bytes accessed | tf_op | source)
XLA Modules:
  0.0 100.9 jit_solution(16371443522282893556)
XLA Ops:
  0.6 0.0 copy-start
  0.6 1.0 %shard_map.59 = (f32[136,128]{1,0:T(8,128)S(1)}, f32[80,128]{1,0:T(8,128)S(1)}, f32[80,128]{1,0:T(8,128)S(1)}) custom-call(f32[1,8,2,8,128]{4,3,2,1,0:T(8,128)} %load_ref.1, f32[3,1,2,16]{3,2,1,0:T(2,128)} %metric_ref.1), custom_call_target="tpu_custom_call" | custom-call | tf_op jit(solution)/shard_map/pallas_call | solution.py:632
  1.7 4.4 %collective-permute-start = (f32[136,128]{1,0:T(8,128)S(1)}, f32[136,128]{1,0:T(8,128)S(1)}, u32[]{:S(2)}, u32[]{:S(2)}) collective-permute-start(f32[136,128]{1,0:T(8,128)S(1)} %get-tuple-element.32.near_ref), channel_id=1, source_target_pairs={{0,1},{1,0},{2,3},{3,2},{4,5},{5,4},{6,7},{7,6},{8,9},{9,8},{10,11... | collective-permute-start | bytes 208904 | tf_op jit(solution)/shard_map/ppermute | solution.py:640
  6.0 10.2 %collective-permute-start.1 = (f32[136,128]{1,0:T(8,128)S(1)}, f32[136,128]{1,0:T(8,128)S(1)}, u32[]{:S(2)}, u32[]{:S(2)}) collective-permute-start(f32[136,128]{1,0:T(8,128)S(1)} %get-tuple-element.32.near_ref), channel_id=1, source_target_pairs={{0,15},{1,2},{2,1},{3,4},{4,3},{5,6},{6,5},{7,8},{8,7},{9,10},{10,... | collective-permute-start | bytes 208904 | tf_op jit(solution)/shard_map/ppermute | solution.py:640
  16.3 1.9 %collective-permute-start.2 = (f32[80,128]{1,0:T(8,128)S(1)}, f32[80,128]{1,0:T(8,128)S(1)}, u32[]{:S(2)}, u32[]{:S(2)}) collective-permute-start(f32[80,128]{1,0:T(8,128)S(1)} %get-tuple-element.33), channel_id=1, source_target_pairs={{0,2},{1,3},{2,0},{3,1},{4,6},{5,7},{6,4},{7,5},{8,10},{9,11},{10,... | collective-permute-start | bytes 122888 | tf_op jit(solution)/shard_map/ppermute | solution.py:640
  18.2 5.5 %collective-permute-start.3 = (f32[80,128]{1,0:T(8,128)S(1)}, f32[80,128]{1,0:T(8,128)S(1)}, u32[]{:S(2)}, u32[]{:S(2)}) collective-permute-start(f32[80,128]{1,0:T(8,128)S(1)} %get-tuple-element.34), channel_id=1, source_target_pairs={{0,14},{1,15},{2,4},{3,5},{4,2},{5,3},{6,8},{7,9},{8,6},{9,7},{10,... | collective-permute-start | bytes 122888 | tf_op jit(solution)/shard_map/ppermute | solution.py:640
  23.6 1.0 copy.7
  24.6 0.0 copy-done
  24.6 0.9 shard_map.60.earlier_ref
  25.6 0.0 collective-permute-done.2.inner_ref
  25.6 0.0 collective-permute-done.3.outer_ref
  25.6 0.0 collective-permute-done.even_ref
  25.6 0.0 collective-permute-done.1.odd_ref
  25.6 4.9 %collective-permute-start.4 = (f32[104,128]{1,0:T(8,128)S(1)}, f32[104,128]{1,0:T(8,128)S(1)}, u32[]{:S(2)}, u32[]{:S(2)}) collective-permute-start(f32[104,128]{1,0:T(8,128)S(1)} %get-tuple-element.36), channel_id=1, source_target_pairs={{0,496},{16,32},{32,16},{48,64},{64,48},{80,96},{96,80},{112,128},... | collective-permute-start | bytes 159752 | tf_op jit(solution)/shard_map/ppermute | solution.py:648
  30.6 4.2 %collective-permute-start.5 = (f32[104,128]{1,0:T(8,128)S(1)}, f32[104,128]{1,0:T(8,128)S(1)}, u32[]{:S(2)}, u32[]{:S(2)}) collective-permute-start(f32[104,128]{1,0:T(8,128)S(1)} %get-tuple-element.37), channel_id=1, source_target_pairs={{0,16},{16,0},{32,48},{48,32},{64,80},{80,64},{96,112},{112,96},{1... | collective-permute-start | bytes 159752 | tf_op jit(solution)/shard_map/ppermute | solution.py:648
  34.8 7.1 %all-to-all-start = ((f32[16,2,128]{2,1,0:T(2,128)}), f32[16,2,128]{2,1,0:T(2,128)S(1)}, u32[]{:S(2)}, u32[]{:S(2)}) async-start(f32[16,2,128]{2,1,0:T(2,128)} %bitcast.3), calls=%async_computation | async-start | bytes 32768 | tf_op jit(solution)/shard_map/all_to_all | solution.py:654
  41.9 0.0 collective-permute-done.4.across_ref
  41.9 0.0 collective-permute-done.5.within_ref
  41.9 0.8 shard_map.62
  42.8 2.4 %collective-permute-start.6 = (f32[64,128]{1,0:T(8,128)S(1)}, f32[64,128]{1,0:T(8,128)S(1)}, u32[]{:S(2)}, u32[]{:S(2)}) collective-permute-start(f32[64,128]{1,0:T(8,128)S(1)} %get-tuple-element.39), channel_id=1, source_target_pairs={{0,496},{16,32},{32,16},{48,64},{64,48},{80,96},{96,80},{112,128},... | collective-permute-start | bytes 98312 | tf_op jit(solution)/shard_map/ppermute | solution.py:648
  45.2 4.1 %collective-permute-start.7 = (f32[64,128]{1,0:T(8,128)S(1)}, f32[64,128]{1,0:T(8,128)S(1)}, u32[]{:S(2)}, u32[]{:S(2)}) collective-permute-start(f32[64,128]{1,0:T(8,128)S(1)} %get-tuple-element.40), channel_id=1, source_target_pairs={{0,16},{16,0},{32,48},{48,32},{64,80},{80,64},{96,112},{112,96},{1... | collective-permute-start | bytes 98312 | tf_op jit(solution)/shard_map/ppermute | solution.py:648
  49.3 0.0 collective-permute-done.6.refs_1_
  49.3 0.8 collective-permute-done.7.refs_2_
  50.1 0.6 shard_map.63
  50.7 1.9 %collective-permute-start.8 = (f32[48,128]{1,0:T(8,128)S(1)}, f32[48,128]{1,0:T(8,128)S(1)}, u32[]{:S(2)}, u32[]{:S(2)}) collective-permute-start(f32[48,128]{1,0:T(8,128)S(1)} %get-tuple-element.45), channel_id=1, source_target_pairs={{0,496},{16,32},{32,16},{48,64},{64,48},{80,96},{96,80},{112,128},... | collective-permute-start | bytes 73736 | tf_op jit(solution)/shard_map/ppermute | solution.py:648
  52.6 6.1 %collective-permute-start.9 = (f32[48,128]{1,0:T(8,128)S(1)}, f32[48,128]{1,0:T(8,128)S(1)}, u32[]{:S(2)}, u32[]{:S(2)}) collective-permute-start(f32[48,128]{1,0:T(8,128)S(1)} %get-tuple-element.46), channel_id=1, source_target_pairs={{0,16},{16,0},{32,48},{48,32},{64,80},{80,64},{96,112},{112,96},{1... | collective-permute-start | bytes 73736 | tf_op jit(solution)/shard_map/ppermute | solution.py:648
  58.7 0.0 all-to-all-done
  58.7 0.6 shard_map.65
  59.4 4.2 %all-to-all-start.1 = ((f32[32,2,128]{2,1,0:T(2,128)}), f32[32,2,128]{2,1,0:T(2,128)S(1)}, u32[]{:S(2)}, u32[]{:S(2)}) async-start(f32[32,2,128]{2,1,0:T(2,128)} %bitcast.5), calls=%async_computation.1 | async-start | bytes 65536 | tf_op jit(solution)/shard_map/all_to_all | solution.py:654
  63.6 0.0 collective-permute-done.8.refs_1_
  63.6 0.0 collective-permute-done.9.refs_2_
  63.6 0.5 shard_map.64
  64.1 2.7 %collective-permute-start.10 = (f32[32,128]{1,0:T(8,128)S(1)}, f32[32,128]{1,0:T(8,128)S(1)}, u32[]{:S(2)}, u32[]{:S(2)}) collective-permute-start(f32[32,128]{1,0:T(8,128)S(1)} %get-tuple-element.50), channel_id=1, source_target_pairs={{0,496},{16,32},{32,16},{48,64},{64,48},{80,96},{96,80},{112,128},... | collective-permute-start | bytes 49160 | tf_op jit(solution)/shard_map/ppermute | solution.py:648
  66.8 3.8 %collective-permute-start.11 = (f32[32,128]{1,0:T(8,128)S(1)}, f32[32,128]{1,0:T(8,128)S(1)}, u32[]{:S(2)}, u32[]{:S(2)}) collective-permute-start(f32[32,128]{1,0:T(8,128)S(1)} %get-tuple-element.51), channel_id=1, source_target_pairs={{0,16},{16,0},{32,48},{48,32},{64,80},{80,64},{96,112},{112,96},{1... | collective-permute-start | bytes 49160 | tf_op jit(solution)/shard_map/ppermute | solution.py:648
  70.7 0.0 all-to-all-done.1
  70.7 0.6 shard_map.66
  71.3 0.0 collective-permute-done.10.across_ref
  71.3 0.2 collective-permute-done.11.within_ref
  71.5 0.5 shard_map.67
  71.9 12.2 %all_to_all.20.received_ref = f32[32,16,128]{2,1,0:T(8,128)S(1)} all-to-all(f32[32,16,128]{2,1,0:T(8,128)S(1)} %get-tuple-element.56), channel_id=1, replica_groups={{320,336,352,368,384,400,416,432,448,464,480,496,0,16,32,48,64,80,96,11..., dimensions={0} | all-to-all | bytes 524288 | tf_op jit(solution)/shard_map/all_to_all | solution.py:654
  84.2 15.9 %all_to_all.21.received_ref = f32[16,8,128]{2,1,0:T(8,128)S(1)} all-to-all(f32[16,8,128]{2,1,0:T(8,128)S(1)} %get-tuple-element.58), channel_id=1, replica_groups={{9,10,11,12,13,14,15,0,1,2,3,4,5,6,7,8},{25,26,27,28,29,30,31,16,17,18,..., dimensions={0} | all-to-all | bytes 131072 | tf_op jit(solution)/shard_map/all_to_all | solution.py:654
  100.1 0.8 shard_map.69
  (3 shorter events, 0.1 us)
Async XLA Ops:
  0.6 24.0 %copy-start = (f32[232,128]{1,0:T(8,128)S(1)}, f32[232,128]{1,0:T(8,128)}, u32[]{:S(2)}) copy-start(f32[232,128]{1,0:T(8,128)} %constant.5.clone.table_ref.refs_8_) | copy-start | bytes 356356
  1.7 23.9 %collective-permute-start = (f32[136,128]{1,0:T(8,128)S(1)}, f32[136,128]{1,0:T(8,128)S(1)}, u32[]{:S(2)}, u32[]{:S(2)}) collective-permute-start(f32[136,128]{1,0:T(8,128)S(1)} %get-tuple-element.32.near_ref), channel_id=1, source_target_pairs={{0,1},{1,0},{2,3},{3,2},{4,5},{5,4},{6,7},{7,6},{8,9},{9,8},{10,11... | collective-permute-start | bytes 208904 | tf_op jit(solution)/shard_map/ppermute | solution.py:640
  6.0 19.5 %collective-permute-start.1 = (f32[136,128]{1,0:T(8,128)S(1)}, f32[136,128]{1,0:T(8,128)S(1)}, u32[]{:S(2)}, u32[]{:S(2)}) collective-permute-start(f32[136,128]{1,0:T(8,128)S(1)} %get-tuple-element.32.near_ref), channel_id=1, source_target_pairs={{0,15},{1,2},{2,1},{3,4},{4,3},{5,6},{6,5},{7,8},{8,7},{9,10},{10,... | collective-permute-start | bytes 208904 | tf_op jit(solution)/shard_map/ppermute | solution.py:640
  16.3 9.3 %collective-permute-start.2 = (f32[80,128]{1,0:T(8,128)S(1)}, f32[80,128]{1,0:T(8,128)S(1)}, u32[]{:S(2)}, u32[]{:S(2)}) collective-permute-start(f32[80,128]{1,0:T(8,128)S(1)} %get-tuple-element.33), channel_id=1, source_target_pairs={{0,2},{1,3},{2,0},{3,1},{4,6},{5,7},{6,4},{7,5},{8,10},{9,11},{10,... | collective-permute-start | bytes 122888 | tf_op jit(solution)/shard_map/ppermute | solution.py:640
  18.2 7.4 %collective-permute-start.3 = (f32[80,128]{1,0:T(8,128)S(1)}, f32[80,128]{1,0:T(8,128)S(1)}, u32[]{:S(2)}, u32[]{:S(2)}) collective-permute-start(f32[80,128]{1,0:T(8,128)S(1)} %get-tuple-element.34), channel_id=1, source_target_pairs={{0,14},{1,15},{2,4},{3,5},{4,2},{5,3},{6,8},{7,9},{8,6},{9,7},{10,... | collective-permute-start | bytes 122888 | tf_op jit(solution)/shard_map/ppermute | solution.py:640
  25.6 16.3 %collective-permute-start.4 = (f32[104,128]{1,0:T(8,128)S(1)}, f32[104,128]{1,0:T(8,128)S(1)}, u32[]{:S(2)}, u32[]{:S(2)}) collective-permute-start(f32[104,128]{1,0:T(8,128)S(1)} %get-tuple-element.36), channel_id=1, source_target_pairs={{0,496},{16,32},{32,16},{48,64},{64,48},{80,96},{96,80},{112,128},... | collective-permute-start | bytes 159752 | tf_op jit(solution)/shard_map/ppermute | solution.py:648
  30.6 11.3 %collective-permute-start.5 = (f32[104,128]{1,0:T(8,128)S(1)}, f32[104,128]{1,0:T(8,128)S(1)}, u32[]{:S(2)}, u32[]{:S(2)}) collective-permute-start(f32[104,128]{1,0:T(8,128)S(1)} %get-tuple-element.37), channel_id=1, source_target_pairs={{0,16},{16,0},{32,48},{48,32},{64,80},{80,64},{96,112},{112,96},{1... | collective-permute-start | bytes 159752 | tf_op jit(solution)/shard_map/ppermute | solution.py:648
  34.8 23.9 %all-to-all-start = ((f32[16,2,128]{2,1,0:T(2,128)}), f32[16,2,128]{2,1,0:T(2,128)S(1)}, u32[]{:S(2)}, u32[]{:S(2)}) async-start(f32[16,2,128]{2,1,0:T(2,128)} %bitcast.3), calls=%async_computation | async-start | bytes 32768 | tf_op jit(solution)/shard_map/all_to_all | solution.py:654
  42.8 6.5 %collective-permute-start.6 = (f32[64,128]{1,0:T(8,128)S(1)}, f32[64,128]{1,0:T(8,128)S(1)}, u32[]{:S(2)}, u32[]{:S(2)}) collective-permute-start(f32[64,128]{1,0:T(8,128)S(1)} %get-tuple-element.39), channel_id=1, source_target_pairs={{0,496},{16,32},{32,16},{48,64},{64,48},{80,96},{96,80},{112,128},... | collective-permute-start | bytes 98312 | tf_op jit(solution)/shard_map/ppermute | solution.py:648
  45.2 4.9 %collective-permute-start.7 = (f32[64,128]{1,0:T(8,128)S(1)}, f32[64,128]{1,0:T(8,128)S(1)}, u32[]{:S(2)}, u32[]{:S(2)}) collective-permute-start(f32[64,128]{1,0:T(8,128)S(1)} %get-tuple-element.40), channel_id=1, source_target_pairs={{0,16},{16,0},{32,48},{48,32},{64,80},{80,64},{96,112},{112,96},{1... | collective-permute-start | bytes 98312 | tf_op jit(solution)/shard_map/ppermute | solution.py:648
  50.7 12.9 %collective-permute-start.8 = (f32[48,128]{1,0:T(8,128)S(1)}, f32[48,128]{1,0:T(8,128)S(1)}, u32[]{:S(2)}, u32[]{:S(2)}) collective-permute-start(f32[48,128]{1,0:T(8,128)S(1)} %get-tuple-element.45), channel_id=1, source_target_pairs={{0,496},{16,32},{32,16},{48,64},{64,48},{80,96},{96,80},{112,128},... | collective-permute-start | bytes 73736 | tf_op jit(solution)/shard_map/ppermute | solution.py:648
  52.6 10.9 %collective-permute-start.9 = (f32[48,128]{1,0:T(8,128)S(1)}, f32[48,128]{1,0:T(8,128)S(1)}, u32[]{:S(2)}, u32[]{:S(2)}) collective-permute-start(f32[48,128]{1,0:T(8,128)S(1)} %get-tuple-element.46), channel_id=1, source_target_pairs={{0,16},{16,0},{32,48},{48,32},{64,80},{80,64},{96,112},{112,96},{1... | collective-permute-start | bytes 73736 | tf_op jit(solution)/shard_map/ppermute | solution.py:648
  59.4 11.3 %all-to-all-start.1 = ((f32[32,2,128]{2,1,0:T(2,128)}), f32[32,2,128]{2,1,0:T(2,128)S(1)}, u32[]{:S(2)}, u32[]{:S(2)}) async-start(f32[32,2,128]{2,1,0:T(2,128)} %bitcast.5), calls=%async_computation.1 | async-start | bytes 65536 | tf_op jit(solution)/shard_map/all_to_all | solution.py:654
  64.1 7.2 %collective-permute-start.10 = (f32[32,128]{1,0:T(8,128)S(1)}, f32[32,128]{1,0:T(8,128)S(1)}, u32[]{:S(2)}, u32[]{:S(2)}) collective-permute-start(f32[32,128]{1,0:T(8,128)S(1)} %get-tuple-element.50), channel_id=1, source_target_pairs={{0,496},{16,32},{32,16},{48,64},{64,48},{80,96},{96,80},{112,128},... | collective-permute-start | bytes 49160 | tf_op jit(solution)/shard_map/ppermute | solution.py:648
  66.8 4.7 %collective-permute-start.11 = (f32[32,128]{1,0:T(8,128)S(1)}, f32[32,128]{1,0:T(8,128)S(1)}, u32[]{:S(2)}, u32[]{:S(2)}) collective-permute-start(f32[32,128]{1,0:T(8,128)S(1)} %get-tuple-element.51), channel_id=1, source_target_pairs={{0,16},{16,0},{32,48},{48,32},{64,80},{80,64},{96,112},{112,96},{1... | collective-permute-start | bytes 49160 | tf_op jit(solution)/shard_map/ppermute | solution.py:648

commit v10 on v9

--- a/solution.py
+++ b/solution.py
@@ -197,30 +197,31 @@
     return ref[row : row + 1, :]
 
 
-def element_apply(field, first, metric_ref, table_ref):
+def element_apply(field, first, metric_ref, table_ref, nodes=range(8)):
     count = len(field[0])
+    rows = 8 * len(nodes)
     stiff = table(table_ref, "stiff")
     out = [[None] * count for i in range(8)]
-    columns = [jnp.concatenate([field[i][c] for i in range(8)], axis=0) for c in range(count)]
+    columns = [jnp.concatenate([field[i][c] for i in nodes], axis=0) for c in range(count)]
     along_y = jnp.dot(
         jnp.concatenate(columns, axis=0), stiff, precision=HIGHEST, preferred_element_type=F32
     )
     for c in range(count):
         stacked = columns[c]
-        along_l = along_y[64 * c : 64 * c + 64, :]
+        along_l = along_y[rows * c : rows * c + rows, :]
         along_j = jnp.dot(
-            stiff[0:64, 0:64], stacked, precision=HIGHEST, preferred_element_type=F32
+            stiff[0:rows, 0:rows], stacked, precision=HIGHEST, preferred_element_type=F32
         )
-        rows = [spread(metric_row(metric_ref, 0, m, first + c)) for m in range(3)]
-        scale_x = rows[0] * table(table_ref, "ww")
-        scale_z = rows[1] * table(table_ref, "wl")
-        scale_y = rows[2] * table(table_ref, "wj")
-        for p in range(8):
+        factors = [spread(metric_row(metric_ref, 0, m, first + c)) for m in range(3)]
+        scale_x = factors[0] * table(table_ref, "ww")
+        scale_z = factors[1] * table(table_ref, "wl")
+        scale_y = factors[2] * table(table_ref, "wj")
+        for place, p in enumerate(nodes):
             along_i = K[0][p] * field[0][c]
             for i in range(1, 8):
                 along_i = along_i + K[i][p] * field[i][c]
             out[p][c] = scale_x * along_i + W[p] * (
-                scale_z * along_j[8 * p : 8 * p + 8, :] + scale_y * along_l[8 * p : 8 * p + 8, :]
+                scale_z * along_j[8 * place : 8 * place + 8, :] + scale_y * along_l[8 * place : 8 * place + 8, :]
             )
     return out
 
@@ -429,7 +430,7 @@
 
 def begin(
     near_ref, even_ref, odd_ref, inner_ref, outer_ref, rows_ref, across_ref, within_ref, table_ref,
-    rhs_ref, inverse_ref, smooth_ref, applied_ref, across_out, within_out,
+    rhs_ref, inverse_ref, smooth_ref, wide_ref, across_out, within_out,
 ):
     left_ref, right_ref = sides(across_ref, within_ref)
 
@@ -458,8 +459,8 @@
     write(rhs_ref, [row[1:7] for row in rhs])
     write(inverse_ref, [row[1:7] for row in inverse])
     write(smooth_ref, [row[1:7] for row in smooth])
-    applied = element_apply(smooth, -3, rows_ref, table_ref)
-    write(applied_ref, applied)
+    write(wide_ref, smooth)
+    applied = element_apply(smooth, -3, rows_ref, table_ref, (0, 7))
     write_x_faces(applied, across_out, within_out)
 
 
@@ -530,6 +531,11 @@
     applied = element_apply(smooth, 1 - count // 2, rows_ref, table_ref)
     write(out_ref, applied)
     write_x_faces(applied, low_ref, high_ref)
+
+
+def apply_wide(wide_ref, rows_ref, table_ref, applied_ref, spare_ref):
+    write(applied_ref, element_apply(read(wide_ref, 0, 8), -3, rows_ref, table_ref))
+    spare_ref[...] = jnp.zeros((8, 128), F32)
 
 
 def coarse_field(received_ref, factor_ref, table_ref):
@@ -674,11 +680,12 @@
         near, near_even, near_odd, far_inner, far_outer, after=send,
     )
     left, right = swap_x(low, high)
-    rhs, inverse, smooth, applied, low, high = run(
+    rhs, inverse, smooth, wide, low, high = run(
         begin, [field_shape(6)] * 3 + [field_shape(8)] + [(64, 128)] * 2,
         near, near_even, near_odd, far_inner, far_outer, rows, left, right, constants,
     )
     left, right = swap_x(low, high)
+    applied, _ = run(apply_wide, [field_shape(8), (8, 128)], wide, rows, constants)
     (send,) = run(lower_tree, [(2 * N_GX, 128)], tree)
     tree = send_pairs(send, "gx", TREE_X)
     update = smooth

time: 102 us -> 101 us (level)
    pallas_call x11 -> x12, Pallas kernels: 6.42 us -> 7.29 us  [run(): pl.pallas_call(kernel, out_shape=outs, in_specs=specs, out_specs=[spec] *...]
  transfers between devices with their start and end apart: 14 -> 14, of which waited for: 2 -> 1; matrix products, arithmetic and copies ran while one was open for 1% -> 1% of each run, Pallas kernels for 4% -> 5%
where the time goes in v10:
time: 101 us
  starting transfers between devices  63.1 us (62%)
  blocking collectives  28.1 us (28%)
  Pallas kernels  7.29 us (7%)
    all_to_all x2, blocking collectives, send_chunks(): lax.all_to_all(chunks, axis, 0, 0, tiled=True, axis_index_groups=[group])  28.1 us
    ppermute x4, starting transfers between devices, swap_z(): return lax.ppermute(value, 'gz', pairs)  22 us
    ppermute x4, starting transfers between devices, swap_x(): lax.ppermute(within, 'gx', inside)  17.9 us
    ppermute x4, starting transfers between devices, swap_x(): lax.ppermute(across, 'gx', over)  12 us
    all_to_all x2, starting transfers between devices, send_chunks(): lax.all_to_all(chunks, axis, 0, 0, tiled=True, axis_index_groups=[group])  11.3 us
    pallas_call x12, Pallas kernels, run(): pl.pallas_call(kernel, out_shape=outs, in_specs=specs, out_specs=[spec] *...  7.29 us
  transfers between devices with their start and end apart: 14, of which 1 were waited for; matrix products, arithmetic and copies ran while one was open for 1% of the time, Pallas kernels for 5%

profile of v10, /device:TPU:1, one launch (start us, length us, event | category | flops | bytes accessed | tf_op | source)
XLA Modules:
  0.0 100.6 jit_solution(12367749488677136722)
XLA Ops:
  0.6 0.0 copy-start
  0.6 1.0 %shard_map.59 = (f32[136,128]{1,0:T(8,128)S(1)}, f32[80,128]{1,0:T(8,128)S(1)}, f32[80,128]{1,0:T(8,128)S(1)}) custom-call(f32[1,8,2,8,128]{4,3,2,1,0:T(8,128)} %load_ref.1, f32[3,1,2,16]{3,2,1,0:T(2,128)} %metric_ref.1), custom_call_target="tpu_custom_call" | custom-call | tf_op jit(solution)/shard_map/pallas_call | solution.py:638
  1.7 4.4 %collective-permute-start = (f32[136,128]{1,0:T(8,128)S(1)}, f32[136,128]{1,0:T(8,128)S(1)}, u32[]{:S(2)}, u32[]{:S(2)}) collective-permute-start(f32[136,128]{1,0:T(8,128)S(1)} %get-tuple-element.33.near_ref), channel_id=1, source_target_pairs={{0,1},{1,0},{2,3},{3,2},{4,5},{5,4},{6,7},{7,6},{8,9},{9,8},{10,11... | collective-permute-start | bytes 208904 | tf_op jit(solution)/shard_map/ppermute | solution.py:646
  6.0 10.2 %collective-permute-start.1 = (f32[136,128]{1,0:T(8,128)S(1)}, f32[136,128]{1,0:T(8,128)S(1)}, u32[]{:S(2)}, u32[]{:S(2)}) collective-permute-start(f32[136,128]{1,0:T(8,128)S(1)} %get-tuple-element.33.near_ref), channel_id=1, source_target_pairs={{0,15},{1,2},{2,1},{3,4},{4,3},{5,6},{6,5},{7,8},{8,7},{9,10},{10,... | collective-permute-start | bytes 208904 | tf_op jit(solution)/shard_map/ppermute | solution.py:646
  16.3 1.9 %collective-permute-start.2 = (f32[80,128]{1,0:T(8,128)S(1)}, f32[80,128]{1,0:T(8,128)S(1)}, u32[]{:S(2)}, u32[]{:S(2)}) collective-permute-start(f32[80,128]{1,0:T(8,128)S(1)} %get-tuple-element.34), channel_id=1, source_target_pairs={{0,2},{1,3},{2,0},{3,1},{4,6},{5,7},{6,4},{7,5},{8,10},{9,11},{10,... | collective-permute-start | bytes 122888 | tf_op jit(solution)/shard_map/ppermute | solution.py:646
  18.2 5.5 %collective-permute-start.3 = (f32[80,128]{1,0:T(8,128)S(1)}, f32[80,128]{1,0:T(8,128)S(1)}, u32[]{:S(2)}, u32[]{:S(2)}) collective-permute-start(f32[80,128]{1,0:T(8,128)S(1)} %get-tuple-element.35), channel_id=1, source_target_pairs={{0,14},{1,15},{2,4},{3,5},{4,2},{5,3},{6,8},{7,9},{8,6},{9,7},{10,... | collective-permute-start | bytes 122888 | tf_op jit(solution)/shard_map/ppermute | solution.py:646
  23.6 1.0 copy.7
  24.6 0.0 copy-done
  24.6 0.9 shard_map.60.earlier_ref
  25.6 0.0 collective-permute-done.2.inner_ref
  25.6 0.0 collective-permute-done.3.outer_ref
  25.6 0.0 collective-permute-done.even_ref
  25.6 0.0 collective-permute-done.1.odd_ref
  25.6 4.9 %collective-permute-start.4 = (f32[104,128]{1,0:T(8,128)S(1)}, f32[104,128]{1,0:T(8,128)S(1)}, u32[]{:S(2)}, u32[]{:S(2)}) collective-permute-start(f32[104,128]{1,0:T(8,128)S(1)} %get-tuple-element.37), channel_id=1, source_target_pairs={{0,496},{16,32},{32,16},{48,64},{64,48},{80,96},{96,80},{112,128},... | collective-permute-start | bytes 159752 | tf_op jit(solution)/shard_map/ppermute | solution.py:654
  30.6 4.2 %collective-permute-start.5 = (f32[104,128]{1,0:T(8,128)S(1)}, f32[104,128]{1,0:T(8,128)S(1)}, u32[]{:S(2)}, u32[]{:S(2)}) collective-permute-start(f32[104,128]{1,0:T(8,128)S(1)} %get-tuple-element.38), channel_id=1, source_target_pairs={{0,16},{16,0},{32,48},{48,32},{64,80},{80,64},{96,112},{112,96},{1... | collective-permute-start | bytes 159752 | tf_op jit(solution)/shard_map/ppermute | solution.py:654
  34.8 7.1 %all-to-all-start = ((f32[16,2,128]{2,1,0:T(2,128)}), f32[16,2,128]{2,1,0:T(2,128)S(1)}, u32[]{:S(2)}, u32[]{:S(2)}) async-start(f32[16,2,128]{2,1,0:T(2,128)} %bitcast.3), calls=%async_computation | async-start | bytes 32768 | tf_op jit(solution)/shard_map/all_to_all | solution.py:660
  41.9 0.0 collective-permute-done.4.across_ref
  41.9 0.0 collective-permute-done.5.within_ref
  41.9 0.5 shard_map.62
  42.4 2.4 %collective-permute-start.6 = (f32[64,128]{1,0:T(8,128)S(1)}, f32[64,128]{1,0:T(8,128)S(1)}, u32[]{:S(2)}, u32[]{:S(2)}) collective-permute-start(f32[64,128]{1,0:T(8,128)S(1)} %get-tuple-element.41), channel_id=1, source_target_pairs={{0,496},{16,32},{32,16},{48,64},{64,48},{80,96},{96,80},{112,128},... | collective-permute-start | bytes 98312 | tf_op jit(solution)/shard_map/ppermute | solution.py:654
  44.8 4.1 %collective-permute-start.7 = (f32[64,128]{1,0:T(8,128)S(1)}, f32[64,128]{1,0:T(8,128)S(1)}, u32[]{:S(2)}, u32[]{:S(2)}) collective-permute-start(f32[64,128]{1,0:T(8,128)S(1)} %get-tuple-element.42), channel_id=1, source_target_pairs={{0,16},{16,0},{32,48},{48,32},{64,80},{80,64},{96,112},{112,96},{1... | collective-permute-start | bytes 98312 | tf_op jit(solution)/shard_map/ppermute | solution.py:654
  48.9 1.2 %shard_map.63 = (f32[8,8,8,128]{3,2,1,0:T(8,128)S(1)}, f32[8,128]{1,0:T(8,128)}) custom-call(f32[8,8,8,128]{3,2,1,0:T(8,128)S(1)} %get-tuple-element.39.wide_ref, f32[32,128]{1,0:T(8,128)S(1)} %get-tuple-element.36.rows_ref.refs_7_, f32[232,128]{1,0:T(8,128)S(1)} %copy-done), custom_call_target="tpu_custom_call" | custom-call | tf_op jit(solution)/shard_map/pallas_call | solution.py:638
  50.1 0.0 collective-permute-done.6.refs_1_
  50.1 0.0 collective-permute-done.7.refs_2_
  50.1 0.6 shard_map.64
  50.7 1.9 %collective-permute-start.8 = (f32[48,128]{1,0:T(8,128)S(1)}, f32[48,128]{1,0:T(8,128)S(1)}, u32[]{:S(2)}, u32[]{:S(2)}) collective-permute-start(f32[48,128]{1,0:T(8,128)S(1)} %get-tuple-element.47), channel_id=1, source_target_pairs={{0,496},{16,32},{32,16},{48,64},{64,48},{80,96},{96,80},{112,128},... | collective-permute-start | bytes 73736 | tf_op jit(solution)/shard_map/ppermute | solution.py:654
  52.7 5.7 %collective-permute-start.9 = (f32[48,128]{1,0:T(8,128)S(1)}, f32[48,128]{1,0:T(8,128)S(1)}, u32[]{:S(2)}, u32[]{:S(2)}) collective-permute-start(f32[48,128]{1,0:T(8,128)S(1)} %get-tuple-element.48), channel_id=1, source_target_pairs={{0,16},{16,0},{32,48},{48,32},{64,80},{80,64},{96,112},{112,96},{1... | collective-permute-start | bytes 73736 | tf_op jit(solution)/shard_map/ppermute | solution.py:654
  58.4 0.0 all-to-all-done
  58.4 0.6 shard_map.66
  59.0 4.2 %all-to-all-start.1 = ((f32[32,2,128]{2,1,0:T(2,128)}), f32[32,2,128]{2,1,0:T(2,128)S(1)}, u32[]{:S(2)}, u32[]{:S(2)}) async-start(f32[32,2,128]{2,1,0:T(2,128)} %bitcast.5), calls=%async_computation.1 | async-start | bytes 65536 | tf_op jit(solution)/shard_map/all_to_all | solution.py:660
  63.2 0.0 collective-permute-done.8.refs_1_
  63.2 0.0 collective-permute-done.9.refs_2_
  63.2 0.5 shard_map.65
  63.7 2.7 %collective-permute-start.10 = (f32[32,128]{1,0:T(8,128)S(1)}, f32[32,128]{1,0:T(8,128)S(1)}, u32[]{:S(2)}, u32[]{:S(2)}) collective-permute-start(f32[32,128]{1,0:T(8,128)S(1)} %get-tuple-element.52), channel_id=1, source_target_pairs={{0,496},{16,32},{32,16},{48,64},{64,48},{80,96},{96,80},{112,128},... | collective-permute-start | bytes 49160 | tf_op jit(solution)/shard_map/ppermute | solution.py:654
  66.5 3.8 %collective-permute-start.11 = (f32[32,128]{1,0:T(8,128)S(1)}, f32[32,128]{1,0:T(8,128)S(1)}, u32[]{:S(2)}, u32[]{:S(2)}) collective-permute-start(f32[32,128]{1,0:T(8,128)S(1)} %get-tuple-element.53), channel_id=1, source_target_pairs={{0,16},{16,0},{32,48},{48,32},{64,80},{80,64},{96,112},{112,96},{1... | collective-permute-start | bytes 49160 | tf_op jit(solution)/shard_map/ppermute | solution.py:654
  70.3 0.0 all-to-all-done.1
  70.3 0.6 shard_map.67
  71.0 0.0 collective-permute-done.10.across_ref
  71.0 0.2 collective-permute-done.11.within_ref
  71.1 0.4 shard_map.68
  71.6 12.2 %all_to_all.20.received_ref = f32[32,16,128]{2,1,0:T(8,128)S(1)} all-to-all(f32[32,16,128]{2,1,0:T(8,128)S(1)} %get-tuple-element.58), channel_id=1, replica_groups={{320,336,352,368,384,400,416,432,448,464,480,496,0,16,32,48,64,80,96,11..., dimensions={0} | all-to-all | bytes 524288 | tf_op jit(solution)/shard_map/all_to_all | solution.py:660
  83.8 15.9 %all_to_all.21.received_ref = f32[16,8,128]{2,1,0:T(8,128)S(1)} all-to-all(f32[16,8,128]{2,1,0:T(8,128)S(1)} %get-tuple-element.60), channel_id=1, replica_groups={{9,10,11,12,13,14,15,0,1,2,3,4,5,6,7,8},{25,26,27,28,29,30,31,16,17,18,..., dimensions={0} | all-to-all | bytes 131072 | tf_op jit(solution)/shard_map/all_to_all | solution.py:660
  99.8 0.8 shard_map.70
  (3 shorter events, 0.1 us)
Async XLA Ops:
  0.6 24.0 %copy-start = (f32[232,128]{1,0:T(8,128)S(1)}, f32[232,128]{1,0:T(8,128)}, u32[]{:S(2)}) copy-start(f32[232,128]{1,0:T(8,128)} %constant.5.clone.table_ref.refs_8_) | copy-start | bytes 356356
  1.7 23.9 %collective-permute-start = (f32[136,128]{1,0:T(8,128)S(1)}, f32[136,128]{1,0:T(8,128)S(1)}, u32[]{:S(2)}, u32[]{:S(2)}) collective-permute-start(f32[136,128]{1,0:T(8,128)S(1)} %get-tuple-element.33.near_ref), channel_id=1, source_target_pairs={{0,1},{1,0},{2,3},{3,2},{4,5},{5,4},{6,7},{7,6},{8,9},{9,8},{10,11... | collective-permute-start | bytes 208904 | tf_op jit(solution)/shard_map/ppermute | solution.py:646
  6.0 19.5 %collective-permute-start.1 = (f32[136,128]{1,0:T(8,128)S(1)}, f32[136,128]{1,0:T(8,128)S(1)}, u32[]{:S(2)}, u32[]{:S(2)}) collective-permute-start(f32[136,128]{1,0:T(8,128)S(1)} %get-tuple-element.33.near_ref), channel_id=1, source_target_pairs={{0,15},{1,2},{2,1},{3,4},{4,3},{5,6},{6,5},{7,8},{8,7},{9,10},{10,... | collective-permute-start | bytes 208904 | tf_op jit(solution)/shard_map/ppermute | solution.py:646
  16.3 9.3 %collective-permute-start.2 = (f32[80,128]{1,0:T(8,128)S(1)}, f32[80,128]{1,0:T(8,128)S(1)}, u32[]{:S(2)}, u32[]{:S(2)}) collective-permute-start(f32[80,128]{1,0:T(8,128)S(1)} %get-tuple-element.34), channel_id=1, source_target_pairs={{0,2},{1,3},{2,0},{3,1},{4,6},{5,7},{6,4},{7,5},{8,10},{9,11},{10,... | collective-permute-start | bytes 122888 | tf_op jit(solution)/shard_map/ppermute | solution.py:646
  18.2 7.4 %collective-permute-start.3 = (f32[80,128]{1,0:T(8,128)S(1)}, f32[80,128]{1,0:T(8,128)S(1)}, u32[]{:S(2)}, u32[]{:S(2)}) collective-permute-start(f32[80,128]{1,0:T(8,128)S(1)} %get-tuple-element.35), channel_id=1, source_target_pairs={{0,14},{1,15},{2,4},{3,5},{4,2},{5,3},{6,8},{7,9},{8,6},{9,7},{10,... | collective-permute-start | bytes 122888 | tf_op jit(solution)/shard_map/ppermute | solution.py:646
  25.6 16.3 %collective-permute-start.4 = (f32[104,128]{1,0:T(8,128)S(1)}, f32[104,128]{1,0:T(8,128)S(1)}, u32[]{:S(2)}, u32[]{:S(2)}) collective-permute-start(f32[104,128]{1,0:T(8,128)S(1)} %get-tuple-element.37), channel_id=1, source_target_pairs={{0,496},{16,32},{32,16},{48,64},{64,48},{80,96},{96,80},{112,128},... | collective-permute-start | bytes 159752 | tf_op jit(solution)/shard_map/ppermute | solution.py:654
  30.6 11.3 %collective-permute-start.5 = (f32[104,128]{1,0:T(8,128)S(1)}, f32[104,128]{1,0:T(8,128)S(1)}, u32[]{:S(2)}, u32[]{:S(2)}) collective-permute-start(f32[104,128]{1,0:T(8,128)S(1)} %get-tuple-element.38), channel_id=1, source_target_pairs={{0,16},{16,0},{32,48},{48,32},{64,80},{80,64},{96,112},{112,96},{1... | collective-permute-start | bytes 159752 | tf_op jit(solution)/shard_map/ppermute | solution.py:654
  34.8 23.6 %all-to-all-start = ((f32[16,2,128]{2,1,0:T(2,128)}), f32[16,2,128]{2,1,0:T(2,128)S(1)}, u32[]{:S(2)}, u32[]{:S(2)}) async-start(f32[16,2,128]{2,1,0:T(2,128)} %bitcast.3), calls=%async_computation | async-start | bytes 32768 | tf_op jit(solution)/shard_map/all_to_all | solution.py:660
  42.4 7.7 %collective-permute-start.6 = (f32[64,128]{1,0:T(8,128)S(1)}, f32[64,128]{1,0:T(8,128)S(1)}, u32[]{:S(2)}, u32[]{:S(2)}) collective-permute-start(f32[64,128]{1,0:T(8,128)S(1)} %get-tuple-element.41), channel_id=1, source_target_pairs={{0,496},{16,32},{32,16},{48,64},{64,48},{80,96},{96,80},{112,128},... | collective-permute-start | bytes 98312 | tf_op jit(solution)/shard_map/ppermute | solution.py:654
  44.8 5.3 %collective-permute-start.7 = (f32[64,128]{1,0:T(8,128)S(1)}, f32[64,128]{1,0:T(8,128)S(1)}, u32[]{:S(2)}, u32[]{:S(2)}) collective-permute-start(f32[64,128]{1,0:T(8,128)S(1)} %get-tuple-element.42), channel_id=1, source_target_pairs={{0,16},{16,0},{32,48},{48,32},{64,80},{80,64},{96,112},{112,96},{1... | collective-permute-start | bytes 98312 | tf_op jit(solution)/shard_map/ppermute | solution.py:654
  50.7 12.5 %collective-permute-start.8 = (f32[48,128]{1,0:T(8,128)S(1)}, f32[48,128]{1,0:T(8,128)S(1)}, u32[]{:S(2)}, u32[]{:S(2)}) collective-permute-start(f32[48,128]{1,0:T(8,128)S(1)} %get-tuple-element.47), channel_id=1, source_target_pairs={{0,496},{16,32},{32,16},{48,64},{64,48},{80,96},{96,80},{112,128},... | collective-permute-start | bytes 73736 | tf_op jit(solution)/shard_map/ppermute | solution.py:654
  52.7 10.6 %collective-permute-start.9 = (f32[48,128]{1,0:T(8,128)S(1)}, f32[48,128]{1,0:T(8,128)S(1)}, u32[]{:S(2)}, u32[]{:S(2)}) collective-permute-start(f32[48,128]{1,0:T(8,128)S(1)} %get-tuple-element.48), channel_id=1, source_target_pairs={{0,16},{16,0},{32,48},{48,32},{64,80},{80,64},{96,112},{112,96},{1... | collective-permute-start | bytes 73736 | tf_op jit(solution)/shard_map/ppermute | solution.py:654
  59.0 11.3 %all-to-all-start.1 = ((f32[32,2,128]{2,1,0:T(2,128)}), f32[32,2,128]{2,1,0:T(2,128)S(1)}, u32[]{:S(2)}, u32[]{:S(2)}) async-start(f32[32,2,128]{2,1,0:T(2,128)} %bitcast.5), calls=%async_computation.1 | async-start | bytes 65536 | tf_op jit(solution)/shard_map/all_to_all | solution.py:660
  63.7 7.2 %collective-permute-start.10 = (f32[32,128]{1,0:T(8,128)S(1)}, f32[32,128]{1,0:T(8,128)S(1)}, u32[]{:S(2)}, u32[]{:S(2)}) collective-permute-start(f32[32,128]{1,0:T(8,128)S(1)} %get-tuple-element.52), channel_id=1, source_target_pairs={{0,496},{16,32},{32,16},{48,64},{64,48},{80,96},{96,80},{112,128},... | collective-permute-start | bytes 49160 | tf_op jit(solution)/shard_map/ppermute | solution.py:654
  66.5 4.7 %collective-permute-start.11 = (f32[32,128]{1,0:T(8,128)S(1)}, f32[32,128]{1,0:T(8,128)S(1)}, u32[]{:S(2)}, u32[]{:S(2)}) collective-permute-start(f32[32,128]{1,0:T(8,128)S(1)} %get-tuple-element.53), channel_id=1, source_target_pairs={{0,16},{16,0},{32,48},{48,32},{64,80},{80,64},{96,112},{112,96},{1... | collective-permute-start | bytes 49160 | tf_op jit(solution)/shard_map/ppermute | solution.py:654
